TPU v7x, 32 devices: a whole 2x2x4 slice. The times are simulated.
32 devices in a mesh: row: 4 (over z), col: 8 (over y, x, core).
Axes of the slice: x: 2, y: 2, z: 4, core: 2. Of those that a mesh axis runs over, the one named last changes fastest.
Arguments:
- matrix: float32 [16384, 16384], P('row', 'col'), may hold values from -48 to 48, as said below
- pivots: int32 [2, 64], replicated, may hold values from 128 to 16383, as said below
Outputs:
- factored: float32 [16384, 16384], P('row', 'col')
Inputs may be any that keep to these rules, and one draw needn't show every extreme that they name: `pivots`: the 128 entries are distinct global row numbers. `matrix`: the entry of row pivots[c, k] in global column c * 64 + k dominates the other entries of its global column, so that multipliers stay well below one.
All inputs are finite; a program needn't handle non-finite values.
Results may differ from a plain program's by a relative error of at most 0.0002.
Values sent between devices are 32-bit elements; how exact they have to be, the bound alone decides.
No kernel may reach another device: no remote copies, remote signals or barrier semaphores. Data moves between devices by JAX's collectives and lax.ppermute only.
A program may use at most 128 MiB of HBM per device.

v0:
```python
import jax
import jax.numpy as jnp
from jax import lax
from jax.sharding import PartitionSpec as P

NB = 64


HIGHEST_PRECISION = lax.Precision.HIGHEST


def eliminate(panel_t):
    panel_width, row_count = panel_t.shape
    row_ids = jnp.arange(row_count, dtype=jnp.int32)
    col_ids = jnp.arange(panel_width, dtype=jnp.int32)

    def eliminate_step(column, current):
        pivot_line = lax.dynamic_index_in_dim(current, column, 1, keepdims=False)
        pivot_value = lax.dynamic_index_in_dim(pivot_line, column, 0, keepdims=False)
        weight = 1.0 / pivot_value
        column_line = lax.dynamic_index_in_dim(current, column, 0, keepdims=False)
        below_rows = row_ids > column
        multiplier = jnp.where(below_rows, column_line * weight, 0.0)
        later_part = jnp.where(col_ids > column, pivot_line, 0.0)
        current = current - later_part[:, None] * multiplier[None, :]
        return jnp.where(
            (col_ids == column)[:, None] & below_rows[None, :], multiplier[None, :], current
        )

    return lax.fori_loop(0, panel_width, eliminate_step, panel_t)


def solve_rows(top_t, right_side):
    unit_part = jnp.tril(top_t.T, -1) + jnp.eye(top_t.shape[0], dtype=top_t.dtype)
    return lax.linalg.triangular_solve(
        unit_part, right_side, left_side=True, lower=True, unit_diagonal=True
    )


def fetch_rows(local_matrix, global_rows, my_row, grid_rows):
    block_ids = global_rows // NB
    owned = block_ids % grid_rows == my_row
    local_index = block_ids // grid_rows * NB + global_rows % NB
    row_values = jnp.where(owned[:, None], local_matrix[jnp.where(owned, local_index, 0)], 0.0)
    return (row_values, jnp.where(owned, local_index, local_matrix.shape[0]))


def place_rows(local_matrix, local_index, row_values):
    return local_matrix.at[local_index].set(row_values, mode="drop")


def apply_panel(
    local_matrix,
    panel,
    lower_t,
    top_t,
    upper_rows,
    row_blocks,
    col_blocks,
    my_row,
    my_col,
    grid_rows,
    grid_cols,
):
    below_rows = row_blocks > panel
    right_cols = col_blocks > panel
    product = lax.dot_general(
        lower_t,
        upper_rows,
        (((0,), (0,)), ((), ())),
        precision=HIGHEST_PRECISION,
        preferred_element_type=jnp.float32,
    )
    result = jnp.where(
        below_rows[:, None] & right_cols[None, :], local_matrix - product, local_matrix
    )
    col_start = panel // grid_cols * NB
    row_start = panel // grid_rows * NB
    owns_col = my_col == panel % grid_cols
    owns_row = my_row == panel % grid_rows
    col_part = jnp.where(
        below_rows[:, None] & owns_col, lower_t.T, result[:, col_start : col_start + NB]
    )
    result = result.at[:, col_start : col_start + NB].set(col_part)
    row_part = jnp.where(
        right_cols[None, :] & owns_row, upper_rows, result[row_start : row_start + NB]
    )
    result = result.at[row_start : row_start + NB].set(row_part)
    corner = jnp.where(
        owns_row & owns_col, top_t.T, result[row_start : row_start + NB, col_start : col_start + NB]
    )
    return result.at[row_start : row_start + NB, col_start : col_start + NB].set(corner)


def shards(matrix, pivots):
    rows_dev, cols_dev = matrix.shape
    grid_rows = lax.axis_size("row")
    grid_cols = lax.axis_size("col")
    my_row = lax.axis_index("row")
    my_col = lax.axis_index("col")
    row_blocks = jnp.arange(rows_dev, dtype=jnp.int32) // NB * grid_rows + my_row
    col_blocks = jnp.arange(cols_dev, dtype=jnp.int32) // NB * grid_cols + my_col
    local_matrix = matrix
    top_global = jnp.arange(2 * NB, dtype=jnp.int32)
    pivot_values, pivot_index = fetch_rows(local_matrix, pivots.reshape(-1), my_row, grid_rows)
    top_values, top_index = fetch_rows(local_matrix, top_global, my_row, grid_rows)
    new_top, new_pivot = lax.psum((pivot_values, top_values), "row")
    local_matrix = place_rows(place_rows(local_matrix, top_index, new_top), pivot_index, new_pivot)
    pieces = []
    top_pieces = []
    for panel in range(2):
        col_start = panel // grid_cols * NB
        owns_col = my_col == panel % grid_cols
        pieces.append(jnp.where(owns_col, local_matrix[:, col_start : col_start + NB].T, 0.0))
        top_pieces.append(jnp.where(owns_col, new_top[:, col_start : col_start + NB].T, 0.0))
    panel_both, top_both = lax.psum(
        (jnp.concatenate(pieces, axis=0), jnp.concatenate(top_pieces, axis=0)), "col"
    )
    first_panel = eliminate(jnp.concatenate([top_both[:NB], panel_both[:NB]], axis=1))
    top_first = first_panel[:, :NB]
    middle_first = first_panel[:, NB : 2 * NB]
    lower_first = first_panel[:, 2 * NB :]
    upper_middle = solve_rows(top_first, top_both[NB:, :NB].T)
    second_input = jnp.concatenate([top_both[NB:, NB:], panel_both[NB:]], axis=1)
    second_input = second_input - jnp.dot(
        upper_middle.T,
        first_panel[:, NB:],
        precision=HIGHEST_PRECISION,
        preferred_element_type=jnp.float32,
    )
    second_panel = eliminate(second_input)
    top_second = second_panel[:, :NB]
    lower_second = second_panel[:, NB:]
    upper_first = solve_rows(top_first, new_top[:NB])
    rest_rows = new_top[NB:] - jnp.dot(
        middle_first.T, upper_first, precision=HIGHEST_PRECISION, preferred_element_type=jnp.float32
    )
    upper_second = solve_rows(top_second, rest_rows)
    local_matrix = apply_panel(
        local_matrix,
        0,
        lower_first,
        top_first,
        upper_first,
        row_blocks,
        col_blocks,
        my_row,
        my_col,
        grid_rows,
        grid_cols,
    )
    local_matrix = apply_panel(
        local_matrix,
        1,
        lower_second,
        top_second,
        upper_second,
        row_blocks,
        col_blocks,
        my_row,
        my_col,
        grid_rows,
        grid_cols,
    )
    return local_matrix


def solution(mesh):
    placed = (P("row", "col"), P())
    return jax.shard_map(
        shards, mesh=mesh, in_specs=placed, out_specs=P("row", "col"), check_vma=False
    )
```

profile of v0, /device:TPU:0, one launch (start us, length us, event | category | flops | bytes accessed | tf_op | source)
XLA Modules:
  0.0 906.1 jit_solution(7099615620316264399)
XLA Ops:
  6.5 23.2 %copy.45 = f32[4096,2048]{1,0:T(8,128)} copy(f32[4096,2048]{1,0:T(8,128)} %param.20) | data formatting | bytes 67108864
  29.9 12.0 %gather_fusion.1 = f32[128,2048]{1,0:T(8,128)S(1)} fusion(f32[4096,2048]{1,0:T(8,128)} %copy.45, s32[1024]{0:T(1024)S(1)} %pad_clamp_fusion), kind=kCustom, calls=%fused_computation.1 | custom fusion | bytes 2097664 | tf_op jit(solution)/shard_map/gather | solution.py:44
  42.3 12.0 %gather_fusion = f32[128,2048]{1,0:T(8,128)S(1)} fusion(f32[4096,2048]{1,0:T(8,128)} %copy.45, s32[1024]{0:T(1024)S(1)} %pad_clamp_fusion.1), kind=kCustom, calls=%fused_computation | custom fusion | bytes 2097664 | tf_op jit(solution)/shard_map/gather | solution.py:44
  56.9 89.8 %all-reduce.7.cloned.1.call-done = (f32[128,2048]{0,1:T(8,128)}, f32[128,2048]{0,1:T(8,128)}) async-done(((f32[128,2048]{0,1:T(8,128)}, f32[128,2048]{0,1:T(8,128)}), (f32[128,2048]{0,1:T(8,128)}, f32[128,2048]{0,1:T(8,128)})) %all-reduce.7.cloned.1.call-update) | async-done | bytes 2097168 | tf_op jit(solution)/shard_map/psum | solution.py:107
  148.7 23.4 %scatter_fusion = f32[4096,2048]{1,0:T(8,128)} fusion(f32[4096,2048]{1,0:T(8,128)} %copy.45, s32[128]{0:T(128)S(1)} %fusion.50, f32[128,2048]{1,0:T(8,128)S(1)} %copy.7), kind=kCustom, calls=%fused_computation.2 | custom fusion | bytes 3146240 | tf_op jit(solution)/shard_map/scatter | solution.py:49
  172.1 23.4 %scatter_fusion.1 = f32[4096,2048]{1,0:T(8,128)} fusion(f32[4096,2048]{1,0:T(8,128)} %scatter_fusion, s32[128]{0:T(128)S(1)} %get-tuple-element.388, f32[128,2048]{1,0:T(8,128)S(1)} %copy.9), kind=kCustom, calls=%fused_computation.3 | custom fusion | bytes 3146240 | tf_op jit(solution)/shard_map/scatter | solution.py:49
  201.7 60.3 %all-reduce.5.cloned.1.call-done = (f32[128,4096]{1,0:T(8,128)}, f32[128,128]{1,0:T(8,128)}) async-done(((f32[128,4096]{1,0:T(8,128)}, f32[128,128]{1,0:T(8,128)}), (f32[128,4096]{1,0:T(8,128)}, f32[128,128]{1,0:T(8,128)})) %all-reduce.5.cloned.1.call-update) | async-done | bytes 2162704 | tf_op jit(solution)/shard_map/psum | solution.py:116
  263.6 2.7 fusion.55
  266.3 197.7 %while.42 = (s32[]{:T(128)}, f32[64,4224]{1,0:T(8,128)S(1)}, s32[]{:T(128)}, f32[1,1]{1,0:T(1,128)}, s32[]{:T(128)}, /*index=5*/s32[]{:T(128)}, s32[]{:T(128)}) while((s32[]{:T(128)}, f32[64,4224]{1,0:T(8,128)S(1)}, s32[]{:T(128)}, f32[1,1]{1,0:T(1,128)}, s32[]{:T(128)}, /*index=5*/s32[]{:T(128)}, s32[]{:T(128)}) %tuple.122), condition=%wide.region_7.8_spmd.clone.clone, body=%wide.region_6.7_spmd.clone.clone.sunk | while | flops 1094213 | bytes 4390805 | solution.py:30
  465.3 4.9 custom-call.8
  470.5 3.4 fusion.15
  475.2 293.7 %while.43 = (s32[]{:T(128)}, f32[64,4160]{1,0:T(8,128)S(1)}, s32[]{:T(128)}, f32[1,1]{1,0:T(1,128)}, s32[]{:T(128)}, /*index=5*/s32[]{:T(128)}, s32[]{:T(128)}) while((s32[]{:T(128)}, f32[64,4160]{1,0:T(8,128)S(1)}, s32[]{:T(128)}, f32[1,1]{1,0:T(1,128)}, s32[]{:T(128)}, /*index=5*/s32[]{:T(128)}, s32[]{:T(128)}) %tuple.125), condition=%wide.region_10.12_spmd.clone.clone, body=%wide.region_9.11_spmd.clone.clone.sunk | while | flops 1077637 | bytes 4324565 | solution.py:30
  476.7 1.9 copy.19
  481.3 1.9 copy.19
  485.9 1.9 copy.19
  490.5 1.9 copy.19
  495.1 1.9 copy.19
  499.7 1.9 copy.19
  504.3 1.9 copy.19
  508.9 1.9 copy.19
  513.5 1.9 copy.19
  518.1 1.9 copy.19
  522.7 1.9 copy.19
  527.2 1.9 copy.19
  531.8 1.9 copy.19
  536.4 1.9 copy.19
  541.0 1.9 copy.19
  545.6 1.9 copy.19
  550.2 1.9 copy.19
  554.8 1.9 copy.19
  559.4 1.9 copy.19
  564.0 1.9 copy.19
  568.6 1.9 copy.19
  573.1 1.9 copy.19
  577.7 1.9 copy.19
  771.8 4.9 custom-call.9
  776.7 4.4 convolution_subtract_fusion.1
  781.1 36.1 %subtract_select_fusion.3 = f32[4096,2048]{1,0:T(8,128)} fusion(f32[4096,2048]{1,0:T(8,128)} %scatter_fusion.1, pred[2048]{0:T(1024)(128)(4,1)S(1)} %get-tuple-element.405, pred[4096]{0:T(1024)(128)(4,1)S(1)} %get-tuple-element.397, f32[64,2048]{1,0:T(8,128)S(1)} %copy-done.3, f32[64,4224]{0,1:T(8,128)S(1)} %copy-done.2), kind=kOutput, calls=%fused_computation.23 | convolution fusion | flops 6467616768 | bytes 69736448 | tf_op jit(solution)/shard_map/dot_general | solution.py:67
  817.3 5.4 select_select_fusion.1
  822.6 11.3 %scatter.36 = f32[4096,2048]{1,0:T(8,128)} dynamic-update-slice(f32[4096,2048]{1,0:T(8,128)} %subtract_select_fusion.3, f32[4096,64]{1,0:T(8,128)} %select_select_fusion.1, s32[]{:T(128)} %constant.527.clone.1, s32[]{:T(128)} %constant.527.clone.1) | dynamic-update-slice | bytes 2097156 | tf_op jit(solution)/shard_map/scatter | solution.py:84
  833.9 2.7 fusion.23
  836.5 1.9 constant_dynamic-update-slice_fusion.1
  839.2 2.8 scatter.48
  842.0 35.9 %subtract_select_fusion.2 = f32[4096,2048]{1,0:T(8,128)} fusion(f32[4096,2048]{1,0:T(8,128)} %scatter.48, pred[2048]{0:T(1024)(128)(4,1)S(1)} %fusion.42, pred[4096]{0:T(1024)(128)(4,1)S(1)} %get-tuple-element.398, f32[64,2048]{1,0:T(8,128)S(1)} %fusion.23, f32[64,4160]{0,1:T(8,128)S(1)} %copy-done), kind=kOutput, calls=%fused_computation.22 | convolution fusion | flops 6467616768 | bytes 69736448 | tf_op jit(solution)/shard_map/dot_general | solution.py:67
  878.0 5.3 select_select_fusion
  883.3 11.2 %scatter.49 = f32[4096,2048]{1,0:T(8,128)} dynamic-update-slice(f32[4096,2048]{1,0:T(8,128)} %subtract_select_fusion.2, f32[4096,64]{1,0:T(8,128)} %select_select_fusion, s32[]{:T(128)} %constant.527.clone.1, s32[]{:T(128)} %constant.527.clone.1) | dynamic-update-slice | bytes 2097156 | tf_op jit(solution)/shard_map/scatter | solution.py:84
  894.5 1.9 constant_dynamic-update-slice_fusion
  896.4 2.8 scatter.51
  (933 shorter events, 370.6 us)
Async XLA Ops:
  6.5 23.2 %copy-start.8 = (s32[2,64]{1,0:T(2,128)S(1)}, s32[2,64]{1,0:T(2,128)}, u32[]{:S(2)}) copy-start(s32[2,64]{1,0:T(2,128)} %param.21) | copy-start | bytes 1540
  6.5 140.2 %all-reduce.7.cloned.1.call-start = ((), (), s32[]{:S(2)}) async-start(), calls=%async_computation.1 | async-start | bytes 4194304 | tf_op jit(solution)/shard_map/psum | solution.py:107
  56.8 205.2 %all-reduce.5.cloned.1.call-start = ((), (), s32[]{:S(2)}) async-start(), calls=%async_computation | async-start | bytes 4325376 | tf_op jit(solution)/shard_map/psum | solution.py:116
  146.7 1.7 copy-start.6
  464.1 6.2 copy-start.7
  465.2 8.6 copy-start.1
  470.3 3.6 copy-start.5
  770.8 10.3 %copy-start.2 = (f32[64,4224]{0,1:T(8,128)S(1)}, f32[64,4224]{0,1:T(8,128)}, u32[]{:S(2)}) copy-start(f32[64,4224]{0,1:T(8,128)} %copy-done.1) | copy-start | bytes 3244036
  776.7 4.5 copy-start.3
  822.6 13.9 %copy-start.4 = (f32[64,2048]{1,0:T(8,128)S(1)}, f32[64,2048]{1,0:T(8,128)}, u32[]{:S(2)}) copy-start(f32[64,2048]{1,0:T(8,128)} %fusion.15) | copy-start | bytes 1572868
  833.9 8.1 copy-start
Sparse Core Ops, SparseCore 0:
  56.9 89.7 all-reduce.6
  201.0 60.9 all-reduce.4
where the time goes:
time: 911 us; the launch traced here: 906 us
  local copies, waits for them, and re-layouts  410 us (45%)
  other arithmetic  151 us (17%)
  waiting for transfers between devices  150 us (16%)
  loops' own time  96.8 us (11%)
  matrix products  84.1 us (9%)
  between operations  13.7 us (2%)
    while x128, local copies, waits for them, and re-layouts  195 us
    another operation x2, loops' own time, eliminate(): return lax.fori_loop(0, panel_width, eliminate_step, panel_t)  96.8 us
    psum x1, waiting for transfers between devices, shards(): new_top, new_pivot = lax.psum((pivot_values, top_values), 'row')  89.8 us
    dynamic_slice x128, local copies, waits for them, and re-layouts, eliminate_step(): lax.dynamic_index_in_dim(pivot_line, column, 0, keepdims=False)  81.3 us
    dot_general x2, matrix products, apply_panel(): lax.dot_general(lower_t, upper_rows, (((0,), (0,)), ((), ())), precision=...  72.1 us
    select_n x128, other arithmetic, eliminate_step(): jnp.where((col_ids == column)[:, None] & below_rows[None, :], multiplier[...  63.1 us
    psum x1, waiting for transfers between devices, shards(): lax.psum((jnp.concatenate(pieces, axis=0), jnp.concatenate(top_pieces, ax...  60.3 us
    scatter x2, local copies, waits for them, and re-layouts, place_rows(): return local_matrix.at[local_index].set(row_values, mode='drop')  46.8 us
  transfers between devices with their start and end apart: 2, of which 2 were waited for; matrix products, arithmetic and copies ran while one was open for 0% of the time, Pallas kernels for 0%

commit v1 on v0

v1 whole, which is shorter than its diff:
```python
import functools

import jax
import jax.numpy as jnp
from jax import lax
from jax.experimental import pallas as pl
from jax.experimental.pallas import tpu as pltpu
from jax.sharding import PartitionSpec as P

NB = 64
NP = 2 * NB
LANES = 128
SUB = 8
HIGHEST_PRECISION = lax.Precision.HIGHEST
MIB = 1024 * 1024


def capacities(grid_rows):
    cap = min(NP, -(-3 * NP // (2 * grid_rows * SUB)) * SUB)
    cap_top = min(NB, -(-2 * NB // (grid_rows * SUB)) * SUB)
    return cap, cap_top


def owner_of(row, grid_rows):
    return lax.rem(lax.div(row, NB), grid_rows)


def local_of(row, grid_rows):
    return lax.div(row, NB * grid_rows) * NB + lax.rem(row, NB)


def split(x):
    high = x.astype(jnp.bfloat16)
    return high, (x - high.astype(jnp.float32)).astype(jnp.bfloat16)


def mm(a, b):
    return jnp.dot(a, b, preferred_element_type=jnp.float32)


def gather_kernel(grid_rows, where_ref, piv_ref, m_ref, rows_ref, corner_ref, _, line_ref, sem):
    my_row = where_ref[0]
    cap = rows_ref.shape[0]
    line_ref[...] = jnp.zeros_like(line_ref)

    def line_copy(row, t):
        return pltpu.make_async_copy(
            m_ref.at[pl.ds(row, 1), pl.ds(0, LANES)], line_ref.at[pl.ds(t, 1), :], sem.at[0]
        )

    def row_copy(row, slot):
        return pltpu.make_async_copy(
            m_ref.at[pl.ds(row, 1), :], rows_ref.at[pl.ds(slot, 1), :], sem.at[1]
        )

    def start(t, count):
        row = piv_ref[t]
        mine = owner_of(row, grid_rows) == my_row

        @pl.when(mine)
        def _():
            line_copy(local_of(row, grid_rows), t).start()

        @pl.when(mine & (count < cap))
        def _():
            row_copy(local_of(row, grid_rows), count).start()

        return count + mine.astype(jnp.int32)

    count = lax.fori_loop(0, NP, start, jnp.int32(0))

    def wait_line(_, carry):
        line_copy(0, 0).wait()
        return carry

    def wait_row(_, carry):
        row_copy(0, 0).wait()
        return carry

    lax.fori_loop(0, count, wait_line, 0)
    lane = lax.broadcasted_iota(jnp.int32, (NB, LANES), 1)
    corner_ref[...] = jnp.where(lane < NB, line_ref[:NB], pltpu.roll(line_ref[NB:], NB, 1))
    lax.fori_loop(0, jnp.minimum(count, cap), wait_row, 0)


def gather_rows(matrix, pivots, where, cap, grid_rows):
    cols = matrix.shape[1]
    smem = pl.BlockSpec(memory_space=pltpu.SMEM)
    vmem = pl.BlockSpec(memory_space=pltpu.VMEM)
    anywhere = pl.BlockSpec(memory_space=pl.ANY)
    return pl.pallas_call(
        functools.partial(gather_kernel, grid_rows),
        out_shape=(
            jax.ShapeDtypeStruct((cap, cols), jnp.float32),
            jax.ShapeDtypeStruct((NB, LANES), jnp.float32),
            jax.ShapeDtypeStruct((NP, cols), jnp.float32),
        ),
        in_specs=[smem, smem, anywhere],
        out_specs=(vmem, vmem, anywhere),
        scratch_shapes=[pltpu.VMEM((NP, LANES), jnp.float32), pltpu.SemaphoreType.DMA((2,))],
        compiler_params=pltpu.CompilerParams(vmem_limit_bytes=16 * MIB),
        name="gather_rows",
    )(where, pivots, matrix)


def pack_kernel(top_ref, bottom_ref, out_ref):
    lane = lax.broadcasted_iota(jnp.int32, out_ref.shape, 1)
    out_ref[...] = jnp.where(lane < NB, top_ref[...], pltpu.roll(bottom_ref[...], NB, 1))


def pack_panel(matrix, steps):
    half = matrix.shape[0] // 2
    size = half // steps
    return pl.pallas_call(
        pack_kernel,
        out_shape=jax.ShapeDtypeStruct((half, LANES), jnp.float32),
        grid=(steps,),
        in_specs=[
            pl.BlockSpec((size, LANES), lambda i: (i, 0)),
            pl.BlockSpec((size, LANES), lambda i: (i + steps, 0)),
        ],
        out_specs=pl.BlockSpec((size, LANES), lambda i: (i, 0)),
        compiler_params=pltpu.CompilerParams(vmem_limit_bytes=16 * MIB),
        name="pack_panel",
    )(matrix, matrix)


GROUP = 4


def eliminate_in_place(work, lane, sub):
    count = len(work)
    work = list(work)
    shape = work[0].shape
    for first in range(0, NP, GROUP):
        block, inner = divmod(first, SUB)
        below = list(range(block, count))
        cols = [
            {i: jnp.broadcast_to(work[i][:, first + j : first + j + 1], shape) for i in below}
            for j in range(GROUP)
        ]
        rows = [
            jnp.broadcast_to(work[block][inner + j : inner + j + 1, :], shape)
            for j in range(GROUP)
        ]
        spots = [
            [jnp.broadcast_to(cols[j][block][inner + i : inner + i + 1, :], shape) for j in range(GROUP)]
            for i in range(GROUP)
        ]
        scaled = []
        for j in range(GROUP):
            weight = 1.0 / spots[j][j]
            at_j = lane == first + j
            line = jnp.where(at_j, 1.0, rows[j]) * weight
            factor = {l: spots[j][l] * weight for l in range(j + 1, GROUP)}
            for i in range(j + 1, GROUP):
                rows[i] = jnp.where(at_j, 0.0, rows[i]) - spots[i][j] * line
                for l in range(j + 1, GROUP):
                    spots[i][l] = spots[i][l] - spots[i][j] * factor[l]
            for l in range(j + 1, GROUP):
                for i in below:
                    cols[l][i] = cols[l][i] - cols[j][i] * factor[l]
            later = (lane > first + j) & (lane < first + GROUP)
            scaled.append(jnp.where(later, 0.0, line))
        in_group = (lane >= first) & (lane < first + GROUP)
        for i in below:
            updated = jnp.where(in_group, 0.0, work[i])
            for j in range(GROUP):
                updated = updated - cols[j][i] * scaled[j]
            if i == block:
                updated = jnp.where(sub < inner, work[i], updated)
                for j in range(GROUP):
                    updated = jnp.where(sub == inner + j, rows[j], updated)
            work[i] = updated
    return work


def corner_kernel(where_ref, mine_ref, other_ref, lu_ref, linv_ref, weights_ref):
    my_col = where_ref[1]
    odd = lax.rem(my_col, 2) == 1
    even_part = jnp.where(odd, other_ref[...], mine_ref[...])
    odd_part = jnp.where(odd, mine_ref[...], other_ref[...])
    left = lax.broadcasted_iota(jnp.int32, (NB, LANES), 1) < NB
    a = jnp.concatenate(
        [
            jnp.where(left, even_part, pltpu.roll(odd_part, NB, 1)),
            jnp.where(left, pltpu.roll(even_part, NB, 1), odd_part),
        ],
        axis=0,
    )
    a_t = a.T
    lane = lax.broadcasted_iota(jnp.int32, (SUB, LANES), 1)
    sub = lax.broadcasted_iota(jnp.int32, (SUB, LANES), 0)
    blocks = range(0, NP, SUB)
    first = eliminate_in_place([a[i : i + SUB] for i in blocks], lane, sub)
    second = eliminate_in_place([a_t[i : i + SUB] for i in blocks], lane, sub)
    w1 = jnp.concatenate(first, axis=0)
    w2 = jnp.concatenate(second, axis=0)
    row = lax.broadcasted_iota(jnp.int32, (NP, NP), 0)
    col = lax.broadcasted_iota(jnp.int32, (NP, NP), 1)
    inverse_d = 1.0 / jnp.sum(jnp.where(row == col, w1, 0.0), axis=0, keepdims=True)
    linv_ref[...] = jnp.where(row > col, w1, jnp.where(row == col, 1.0, 0.0))
    w2_t = w2.T
    lu = jnp.where(row <= col, w1, w2_t * inverse_d)
    lu_ref[...] = jnp.where(my_col == 1, pltpu.roll(lu, NB, 1), lu)
    uinv = jnp.where(row < col, w2_t, jnp.where(row == col, 1.0, 0.0)) * inverse_d
    mine = jnp.where(odd, uinv[NB:], uinv[:NB])
    other = jnp.where(odd, uinv[:NB], uinv[NB:])
    zero = jnp.zeros_like(mine)
    weights_ref[0] = jnp.concatenate([mine, zero, other, zero], axis=0)
    weights_ref[1] = jnp.concatenate([zero, mine, zero, other], axis=0)


def assemble(grid_rows, my_row, piv_ref, piece_refs, out_ref, count_ref):
    for r in range(grid_rows):
        count_ref[r] = 0

    def place(t, carry):
        owner = owner_of(piv_ref[t], grid_rows)
        slot = count_ref[owner]
        count_ref[owner] = slot + 1
        back = lax.rem(my_row - owner + grid_rows, grid_rows)
        for s in range(grid_rows):

            @pl.when(back == s)
            def _(s=s):
                out_ref[pl.ds(t, 1), :] = piece_refs[s][pl.ds(slot, 1), :]

        return carry

    lax.fori_loop(0, NP, place, 0)


def factor_corner(mine, other, where):
    smem = pl.BlockSpec(memory_space=pltpu.SMEM)
    vmem = pl.BlockSpec(memory_space=pltpu.VMEM)
    square = jax.ShapeDtypeStruct((NP, NP), jnp.float32)
    return pl.pallas_call(
        corner_kernel,
        out_shape=(square, square, jax.ShapeDtypeStruct((2, 2 * NP, NP), jnp.float32)),
        in_specs=[smem, vmem, vmem],
        out_specs=(vmem, vmem, vmem),
        compiler_params=pltpu.CompilerParams(vmem_limit_bytes=24 * MIB),
        name="factor_corner",
    )(where, mine, other)


def upper_kernel(grid_rows, where_ref, piv_ref, *refs):
    piece_refs = refs[:grid_rows]
    all_ref, linv_ref, lu_ref, high_ref, low_ref, top_ref, a_ref, count_ref, sem = refs[grid_rows:]
    my_row = where_ref[0]
    my_col = where_ref[1]

    @pl.when(where_ref[2] == 0)
    def _():
        assemble(grid_rows, my_row, piv_ref, piece_refs, a_ref, count_ref)

    @pl.when(where_ref[2] != 0)
    def _():
        copy = pltpu.make_async_copy(all_ref, a_ref, sem)
        copy.start()
        copy.wait()

    cols = a_ref.shape[1]
    width = min(cols, 512)
    linv_high, linv_low = split(linv_ref[...])
    linv_both = jnp.concatenate([linv_high, linv_low], axis=1)
    for start in range(0, cols, width):
        span = slice(start, start + width)
        a_high, a_low = split(a_ref[:, span])
        a_ref[:, span] = mm(linv_both, jnp.concatenate([a_high, a_high], axis=0)) + mm(
            linv_high, a_low
        )

    @pl.when(my_row == 0)
    def _():
        top_ref[...] = a_ref[:NB]

    @pl.when(my_row != 0)
    def _():
        top_ref[...] = a_ref[NB:]

    @pl.when(my_col < 2)
    def _():
        lane = lax.broadcasted_iota(jnp.int32, (NP, LANES), 1)
        row = lax.broadcasted_iota(jnp.int32, (NP, LANES), 0)
        lu_part = jnp.where(my_row == 0, lu_ref[:NB], lu_ref[NB:])
        top_ref[:, :LANES] = jnp.where(lane[:NB] < NB, lu_part, top_ref[:, :LANES])
        unit = jnp.where(row == lane + my_col * NB, -1.0, 0.0)
        a_ref[:, :LANES] = jnp.where(lane < NB, unit, a_ref[:, :LANES])

    high, low = split(a_ref[...])
    high_ref[...] = high
    low_ref[...] = low


def upper_rows_of(pieces, everything, linv, lu, pivots, where, grid_rows):
    cols = pieces[0].shape[1]
    smem = pl.BlockSpec(memory_space=pltpu.SMEM)
    vmem = pl.BlockSpec(memory_space=pltpu.VMEM)
    return pl.pallas_call(
        functools.partial(upper_kernel, grid_rows),
        out_shape=(
            jax.ShapeDtypeStruct((NP, cols), jnp.bfloat16),
            jax.ShapeDtypeStruct((NP, cols), jnp.bfloat16),
            jax.ShapeDtypeStruct((NB, cols), jnp.float32),
        ),
        in_specs=[smem, smem] + [vmem] * grid_rows + [pl.BlockSpec(memory_space=pl.ANY), vmem, vmem],
        out_specs=(vmem, vmem, vmem),
        scratch_shapes=[
            pltpu.VMEM((NP, cols), jnp.float32),
            pltpu.SMEM((grid_rows,), jnp.int32),
            pltpu.SemaphoreType.DMA(()),
        ],
        compiler_params=pltpu.CompilerParams(vmem_limit_bytes=32 * MIB),
        name="upper_rows",
    )(where, pivots, *pieces, everything, linv, lu)


def updated_rows(a_ref, panel, weights, high_ref, low_ref, out_ref, is_panel):
    rows, cols = out_ref.shape
    p_high, p_low = split(panel)
    w_high, w_low = split(weights)
    lower = mm(p_high, w_high) + (mm(p_high, w_low) + mm(p_low, w_high))
    l_high, l_low = split(lower)
    both = jnp.concatenate([l_high, l_low], axis=1)
    width = min(cols, 512)
    lane = lax.broadcasted_iota(jnp.int32, (rows, LANES), 1)
    for start in range(0, cols, width):
        span = slice(start, start + width)
        high = high_ref[:, span]
        product = mm(both, jnp.concatenate([high, high], axis=0)) + mm(l_high, low_ref[:, span])
        a = a_ref[:, span]
        if start == 0:
            first = jnp.where((lane < NB) & is_panel, 0.0, a[:, :LANES])
            if width > LANES:
                a = jnp.concatenate([first, a[:, LANES:]], axis=1)
            else:
                a = first
        out_ref[:, span] = a - product


def moved_kernel(grid_rows, cap_top, where_ref, piv_ref, m_ref, own_ref, other_ref, weights_ref, high_ref, low_ref, out_ref, packed_ref, count_ref):
    my_row = where_ref[0]
    panel = jnp.concatenate([own_ref[...], other_ref[...]], axis=1)
    updated_rows(m_ref, panel, weights_ref[0], high_ref, low_ref, out_ref, where_ref[1] < 2)
    for r in range(grid_rows):
        count_ref[r] = 0

    @pl.when(my_row < 2)
    def _():
        def place(k, carry):
            owner = owner_of(piv_ref[my_row * NB + k], grid_rows)
            slot = count_ref[owner]
            count_ref[owner] = slot + 1
            ahead = lax.rem(owner - my_row + grid_rows, grid_rows)

            @pl.when((ahead > 0) & (slot < cap_top))
            def _():
                packed_ref[ahead - 1, pl.ds(slot, 1), :] = out_ref[pl.ds(k, 1), :]

            return carry

        lax.fori_loop(0, NB, place, 0)


def moved_rows(matrix, own, other, weights, high, low, pivots, where, cap_top, grid_rows):
    cols = matrix.shape[1]
    smem = pl.BlockSpec(memory_space=pltpu.SMEM)
    vmem = pl.BlockSpec(memory_space=pltpu.VMEM)
    head = lambda width: pl.BlockSpec((NB, width), lambda i: (0, 0))
    return pl.pallas_call(
        functools.partial(moved_kernel, grid_rows, cap_top),
        out_shape=(
            jax.ShapeDtypeStruct((NB, cols), jnp.float32),
            jax.ShapeDtypeStruct((grid_rows - 1, cap_top, cols), jnp.float32),
        ),
        grid=(1,),
        in_specs=[smem, smem, head(cols), head(LANES), head(LANES), vmem, vmem, vmem],
        out_specs=(
            pl.BlockSpec((NB, cols), lambda i: (0, 0)),
            pl.BlockSpec((grid_rows - 1, cap_top, cols), lambda i: (0, 0, 0)),
        ),
        scratch_shapes=[pltpu.SMEM((grid_rows,), jnp.int32)],
        compiler_params=pltpu.CompilerParams(vmem_limit_bytes=32 * MIB),
        name="moved_rows",
    )(where, pivots, matrix, own, other, weights, high, low)


def trailing_kernel(blocks, where_ref, m_ref, own1, own2, other1, other2, weights_ref, high_ref, low_ref, out_ref, panel_ref):
    step = pl.program_id(0)
    rows = m_ref.shape[0]
    quarter = blocks // 4
    inside = lax.rem(step, quarter)
    part = lax.div(step, quarter)
    here = pl.ds(pl.multiple_of(inside * rows, rows), rows)

    @pl.when(lax.rem(part, 2) == 0)
    def _():
        panel_ref[:, :LANES] = own1[here, :]
        panel_ref[:, LANES:] = other1[here, :]

    @pl.when(lax.rem(part, 2) == 1)
    def _():
        panel_ref[:, :LANES] = own2[here, :]
        panel_ref[:, LANES:] = other2[here, :]

    weights = weights_ref[lax.div(part, 2)]
    updated_rows(m_ref, panel_ref[...], weights, high_ref, low_ref, out_ref, where_ref[1] < 2)


def trailing(matrix, own, other, weights, high, low, where):
    rows, cols = matrix.shape
    size = min(256, rows // 4)
    blocks = rows // size
    smem = pl.BlockSpec(memory_space=pltpu.SMEM)
    vmem = pl.BlockSpec(memory_space=pltpu.VMEM)
    return pl.pallas_call(
        functools.partial(trailing_kernel, blocks),
        out_shape=jax.ShapeDtypeStruct((rows, cols), jnp.float32),
        grid=(blocks,),
        in_specs=[smem, pl.BlockSpec((size, cols), lambda i: (i, 0))] + [vmem] * 7,
        out_specs=pl.BlockSpec((size, cols), lambda i: (i, 0)),
        scratch_shapes=[pltpu.VMEM((size, 2 * LANES), jnp.float32)],
        compiler_params=pltpu.CompilerParams(vmem_limit_bytes=40 * MIB),
        cost_estimate=pl.CostEstimate(
            flops=6 * rows * cols * NP, bytes_accessed=8 * rows * cols, transcendentals=0
        ),
        name="trailing",
    )(where, matrix, own[0], own[1], other[0], other[1], weights, high, low)


def place_kernel(grid_rows, where_ref, piv_ref, *refs):
    moved_refs = refs[:grid_rows]
    all_ref, top_ref, _, out_ref, sem, count_ref = refs[grid_rows:]
    my_row = where_ref[0]
    packed = where_ref[2] == 0

    @pl.when(my_row < 2)
    def _():
        pltpu.make_async_copy(top_ref, out_ref.at[pl.ds(0, NB), :], sem).start()

    count_ref[0] = 0
    count_ref[1] = 0

    def put(t, total):
        row = piv_ref[t]
        mine = owner_of(row, grid_rows) == my_row
        source = lax.div(t, NB)
        back = lax.rem(my_row - source + grid_rows, grid_rows)
        slot = count_ref[source]
        count_ref[source] = slot + mine.astype(jnp.int32)
        to = pl.ds(local_of(row, grid_rows), 1)

        @pl.when(mine & ~packed)
        def _():
            pltpu.make_async_copy(all_ref.at[pl.ds(t, 1), :], out_ref.at[to, :], sem).start()

        @pl.when(mine & packed & (back == 0))
        def _():
            pltpu.make_async_copy(
                moved_refs[0].at[pl.ds(lax.rem(t, NB), 1), :], out_ref.at[to, :], sem
            ).start()

        for s in range(1, grid_rows):

            @pl.when(mine & packed & (back == s))
            def _(s=s):
                pltpu.make_async_copy(
                    moved_refs[s].at[pl.ds(slot, 1), :], out_ref.at[to, :], sem
                ).start()

        return total + mine.astype(jnp.int32)

    total = lax.fori_loop(0, NP, put, jnp.int32(0))

    def wait(_, carry):
        pltpu.make_async_copy(
            moved_refs[0].at[pl.ds(0, 1), :], out_ref.at[pl.ds(0, 1), :], sem
        ).wait()
        return carry

    lax.fori_loop(0, total, wait, 0)

    @pl.when(my_row < 2)
    def _():
        pltpu.make_async_copy(top_ref, out_ref.at[pl.ds(0, NB), :], sem).wait()


def place_moved(moved, everything, top, result, pivots, where, grid_rows):
    smem = pl.BlockSpec(memory_space=pltpu.SMEM)
    anywhere = pl.BlockSpec(memory_space=pl.ANY)
    return pl.pallas_call(
        functools.partial(place_kernel, grid_rows),
        out_shape=jax.ShapeDtypeStruct(result.shape, result.dtype),
        in_specs=[smem, smem] + [anywhere] * (grid_rows + 3),
        out_specs=anywhere,
        input_output_aliases={grid_rows + 4: 0},
        scratch_shapes=[pltpu.SemaphoreType.DMA(()), pltpu.SMEM((2,), jnp.int32)],
        compiler_params=pltpu.CompilerParams(vmem_limit_bytes=16 * MIB),
        name="place_moved",
    )(where, pivots, *moved, everything, top, result)


def spread_chips(value, order, my_chip, chips):
    reached = [0]
    for bit in order:
        pairs = [(2 * c + k, 2 * (c | bit) + k) for c in reached for k in range(2)]
        arrived = lax.ppermute(value, "col", pairs)
        value = jnp.where((my_chip & bit) != 0, arrived, value)
        reached = reached + [c | bit for c in reached]
    return value


def shards(matrix, pivots):
    grid_rows = lax.axis_size("row")
    grid_cols = lax.axis_size("col")
    chips = grid_cols // 2
    assert grid_rows > 1 and chips * 2 == grid_cols and not chips & (chips - 1)
    my_row = lax.axis_index("row")
    my_col = lax.axis_index("col")
    my_chip = my_col // 2
    cap, cap_top = capacities(grid_rows)
    flat = pivots.reshape(-1)
    owner = owner_of(flat, grid_rows)
    owned = jnp.sum(
        owner.reshape(2, NB)[:, :, None] == jnp.arange(grid_rows, dtype=jnp.int32), axis=1
    )
    over = (jnp.max(jnp.sum(owned, axis=0)) > cap) | (jnp.max(owned) > cap_top)
    over = over.astype(jnp.int32)
    where = jnp.stack([my_row, my_col, over]).astype(jnp.int32)
    swap = [(c, c ^ 1) for c in range(grid_cols)]
    shifts = [[(r, (r + s) % grid_rows) for r in range(grid_rows)] for s in range(1, grid_rows)]
    bits = [1 << b for b in range(chips.bit_length() - 1)]

    rows, corner, unwritten = gather_rows(matrix, flat, where, cap, grid_rows)
    corner = corner + sum(lax.ppermute(corner, "row", shift) for shift in shifts)
    corner = jnp.where(my_chip == 0, corner, 0.0) + sum(
        lax.ppermute(corner, "col", [(0, 2 * chip), (1, 2 * chip + 1)]) for chip in range(1, chips)
    )
    corner_other = lax.ppermute(corner, "col", swap)

    packed = pack_panel(matrix, 2)
    quarter = packed.shape[0] // 2
    own = (
        spread_chips(packed[:quarter], bits, my_chip, chips),
        spread_chips(packed[quarter:], bits[::-1], my_chip, chips),
    )
    other = tuple(lax.ppermute(x, "col", swap) for x in own)

    pieces = [rows] + [lax.ppermute(rows, "row", shift) for shift in shifts]

    def sum_rows(state):
        local = jnp.where(owner == my_row, local_of(flat, grid_rows), 0)
        picked = jnp.where((owner == my_row)[:, None], matrix[local], 0.0)
        return jnp.int32(0), lax.psum(picked, "row")

    everything = lax.while_loop(lambda state: state[0] > 0, sum_rows, (over, unwritten))[1]

    lu, linv, weights = factor_corner(corner, corner_other, where)
    high, low, top = upper_rows_of(pieces, everything, linv, lu, flat, where, grid_rows)
    kept, leaving = moved_rows(
        matrix, own[0], other[0], weights, high, low, flat, where, cap_top, grid_rows
    )
    moved = [kept]
    for s in range(1, grid_rows):
        pairs = [(c, (c + s) % grid_rows) for c in range(2)]
        moved.append(lax.ppermute(leaving[s - 1], "row", pairs))

    def sum_moved(state):
        halves = [jnp.where(my_row == c, kept, 0.0) for c in range(2)]
        return jnp.int32(0), lax.psum(jnp.concatenate(halves, axis=0), "row")

    everything = lax.while_loop(lambda state: state[0] > 0, sum_moved, (over, everything))[1]
    result = trailing(matrix, own, other, weights, high, low, where)
    return place_moved(moved, everything, top, result, flat, where, grid_rows)


def solution(mesh):
    placed = (P("row", "col"), P())
    return jax.shard_map(
        shards, mesh=mesh, in_specs=placed, out_specs=P("row", "col"), check_vma=False
    )
```

time: 911 us -> 140 us (0.15)
  local copies, waits for them, and re-layouts: 410 us -> 2.8 us
  other arithmetic: 151 us -> 1.95 us
  waiting for transfers between devices: 150 us -> 12 us
  loops' own time: 96.8 us -> 0.01 us
  matrix products: 84.1 us -> 0 us
  Pallas kernels: 0 us -> 68.1 us
  starting transfers between devices: 0.04 us -> 39.7 us
    while x130 -> x0, local copies, waits for them, and re-layouts: 198 us -> none
    psum x2 -> x0, waiting for transfers between devices: 150 us -> none  [the longest x1 89.8 us: shards(): new_top, new_pivot = lax.psum((pivot_values, top_values), 'row')]
    another operation x2, loops' own time: 96.8 us -> 0.01 us  [the longest x1 0.01 us: shards(): lax.while_loop(lambda state: state[0] > 0, sum_rows, (over, unwritten))[1]]
    dynamic_slice x128 -> x0, local copies, waits for them, and re-layouts: 81.3 us -> none  [eliminate_step(): lax.dynamic_index_in_dim(pivot_line, column, 0, keepdims=False)]
    dot_general x4 -> x0, matrix products: 77.8 us -> none  [the longest x2 72.1 us: apply_panel(): lax.dot_general(lower_t, upper_rows, (((0,), (0,)), ((), ())), precision=...]
    select_n x265 -> x3, other arithmetic: 76.7 us -> 0.37 us  [spread_chips(): value = jnp.where(my_chip & bit != 0, arrived, value)]
    scatter x6 -> x0, local copies, waits for them, and re-layouts: 74.8 us -> none  [the longest x2 46.8 us: place_rows(): return local_matrix.at[local_index].set(row_values, mode='drop')]
    pallas_call x0 -> x7, Pallas kernels: none -> 68.1 us  [the longest x1 33.1 us: trailing(): pl.pallas_call(functools.partial(trailing_kernel, blocks), out_shape=jax....]
  transfers between devices with their start and end apart: 2 -> 19, of which waited for: 2 -> 3; matrix products, arithmetic and copies ran while one was open for 0% -> 2% of each run, Pallas kernels for 0% -> 43%
where the time goes in v1:
time: 140 us; the launch traced here: 139 us
  Pallas kernels  68.1 us (49%)
  starting transfers between devices  39.7 us (28%)
  between operations  14.9 us (11%)
  waiting for transfers between devices  12 us (9%)
  local copies, waits for them, and re-layouts  2.8 us (2%)
  other arithmetic  1.95 us (1%)
    pallas_call x1, Pallas kernels, trailing(): pl.pallas_call(functools.partial(trailing_kernel, blocks), out_shape=jax....  33.1 us
    ppermute x4, starting transfers between devices, spread_chips(): arrived = lax.ppermute(value, 'col', pairs)  14.8 us
    pallas_call x1, Pallas kernels, factor_corner(): pl.pallas_call(corner_kernel, out_shape=(square, square, jax.ShapeDtypeSt...  12.6 us
    ppermute x3, starting transfers between devices, shards(): moved.append(lax.ppermute(leaving[s - 1], 'row', pairs))  7.88 us
    ppermute x3, starting transfers between devices, shards(): pieces = [rows] + [lax.ppermute(rows, 'row', shift) for shift in shifts]  7.82 us
    ppermute x3, waiting for transfers between devices, shards(): pieces = [rows] + [lax.ppermute(rows, 'row', shift) for shift in shifts]  7.8 us
    pallas_call x1, Pallas kernels, upper_rows_of(): pl.pallas_call(functools.partial(upper_kernel, grid_rows), out_shape=(jax...  6.86 us
    pallas_call x1, Pallas kernels, place_moved(): pl.pallas_call(functools.partial(place_kernel, grid_rows), out_shape=jax....  6.28 us
  transfers between devices with their start and end apart: 19, of which 3 were waited for; matrix products, arithmetic and copies ran while one was open for 2% of the time, Pallas kernels for 43%

profile of v1, /device:TPU:0, one launch (start us, length us, event | category | flops | bytes accessed | tf_op | source)
XLA Modules:
  0.0 139.3 jit_solution(8755016874434949177)
XLA Ops:
  6.5 1.8 %pack_panel.1 = f32[2048,128]{1,0:T(8,128)S(1)} custom-call(f32[4096,2048]{1,0:T(8,128)} %m_ref.5, f32[4096,2048]{1,0:T(8,128)} %m_ref.5), custom_call_target="tpu_custom_call" | custom-call | tf_op jit(solution)/shard_map/pack_panel/pallas_call | solution.py:114
  8.3 0.1 fusion.6
  8.4 4.9 %collective-permute-start.16 = (f32[1024,128]{1,0:T(8,128)S(1)}, f32[1024,128]{1,0:T(8,128)S(1)}, u32[]{:S(2)}, u32[]{:S(2)}) collective-permute-start(f32[1024,128]{1,0:T(8,128)S(1)} %get-tuple-element.107), channel_id=1, source_target_pairs={{0,4},{1,5},{8,12},{9,13},{16,20},{17,21},{24,28},{25,29}} | collective-permute-start | bytes 1572872 | tf_op jit(solution)/shard_map/ppermute | solution.py:509
  13.3 2.1 %collective-permute-start = (f32[1024,128]{1,0:T(8,128)S(1)}, f32[1024,128]{1,0:T(8,128)}, u32[]{:S(2)}, u32[]{:S(2)}) collective-permute-start(f32[1024,128]{1,0:T(8,128)S(1)} %get-tuple-element.108), channel_id=1, source_target_pairs={{0,2},{1,3},{8,10},{9,11},{16,18},{17,19},{24,26},{25,27}} | collective-permute-start | bytes 1572872 | tf_op jit(solution)/shard_map/ppermute | solution.py:509
  15.4 0.1 reshape.84.piv_ref
  15.5 0.2 convert_reduce_fusion
  15.7 0.6 reduce_max.18
  16.3 0.7 reduce_max.19
  18.2 0.1 pad_add_fusion.where_ref
  18.3 3.4 %gather_rows.1 = (f32[48,2048]{1,0:T(8,128)S(1)}, f32[64,128]{1,0:T(8,128)S(1)}, f32[128,2048]{1,0:T(8,128)}) custom-call(s32[3]{0:T(128)S(1)} %pad_add_fusion.where_ref, s32[128]{0:T(128)S(1)} %reshape.84.piv_ref, f32[4096,2048]{1,0:T(8,128)} %m_ref.5), custom_call_target="tpu_custom_call" | custom-call | tf_op jit(solution)/shard_map/gather_rows/pallas_call | solution.py:91
  21.8 3.6 %collective-permute-start.5 = (f32[64,128]{1,0:T(8,128)S(1)}, f32[64,128]{1,0:T(8,128)S(1)}, u32[]{:S(2)}, u32[]{:S(2)}) collective-permute-start(f32[64,128]{1,0:T(8,128)S(1)} %get-tuple-element.66), channel_id=1, source_target_pairs={{0,24},{8,0},{16,8},{24,16},{1,25},{9,1},{17,9},{25,17},{2,26},{10... | collective-permute-start | bytes 98312 | tf_op jit(solution)/shard_map/ppermute | solution.py:537
  25.3 0.0 collective-permute-start.4
  25.3 1.0 collective-permute-start.3
  26.4 0.2 broadcast_select_fusion.5
  26.6 5.7 %collective-permute-start.17 = (f32[1024,128]{1,0:T(8,128)S(1)}, f32[1024,128]{1,0:T(8,128)}, u32[]{:S(2)}, u32[]{:S(2)}) collective-permute-start(f32[1024,128]{1,0:T(8,128)S(1)} %get-tuple-element.105), channel_id=1, source_target_pairs={{0,2},{1,3},{4,6},{5,7},{8,10},{9,11},{12,14},{13,15},{16,18},{17,... | collective-permute-start | bytes 1572872 | tf_op jit(solution)/shard_map/ppermute | solution.py:509
  32.3 0.0 collective-permute-done.5
  32.3 0.0 collective-permute-done.4
  32.3 1.3 collective-permute-start.8
  33.6 1.3 collective-permute-start.7
  34.9 1.3 collective-permute-start.6
  36.2 3.7 %collective-permute-start.12 = (f32[48,2048]{1,0:T(8,128)S(1)}, f32[48,2048]{1,0:T(8,128)S(1)}, u32[]{:S(2)}, u32[]{:S(2)}) collective-permute-start(f32[48,2048]{1,0:T(8,128)S(1)} %get-tuple-element.68.refs_0_), channel_id=1, source_target_pairs={{0,24},{8,0},{16,8},{24,16},{1,25},{9,1},{17,9},{25,17},{2,26},{10... | collective-permute-start | bytes 1179656 | tf_op jit(solution)/shard_map/ppermute | solution.py:551
  39.9 3.0 %collective-permute-done.8 = f32[64,128]{1,0:T(8,128)S(1)} collective-permute-done((f32[64,128]{1,0:T(8,128)S(1)}, f32[64,128]{1,0:T(8,128)S(1)}, u32[]{:S(2)}, u32[]{:S(2)}) %collective-permute-start.8) | collective-permute-done | bytes 32800 | tf_op jit(solution)/shard_map/ppermute | solution.py:539
  42.8 2.6 %collective-permute-start.11 = (f32[48,2048]{1,0:T(8,128)S(1)}, f32[48,2048]{1,0:T(8,128)}, u32[]{:S(2)}, u32[]{:S(2)}) collective-permute-start(f32[48,2048]{1,0:T(8,128)S(1)} %get-tuple-element.68.refs_0_), channel_id=1, source_target_pairs={{0,16},{8,24},{16,0},{24,8},{1,17},{9,25},{17,1},{25,9},{2,18},{10... | collective-permute-start | bytes 1179656 | tf_op jit(solution)/shard_map/ppermute | solution.py:551
  45.4 2.1 %collective-permute-start.1 = (f32[1024,128]{1,0:T(8,128)S(1)}, f32[1024,128]{1,0:T(8,128)}, u32[]{:S(2)}, u32[]{:S(2)}) collective-permute-start(f32[1024,128]{1,0:T(8,128)S(1)} %get-tuple-element.106), channel_id=1, source_target_pairs={{0,4},{1,5},{2,6},{3,7},{8,12},{9,13},{10,14},{11,15},{16,20},{17,... | collective-permute-start | bytes 1572872 | tf_op jit(solution)/shard_map/ppermute | solution.py:509
  47.5 0.1 collective-permute-start.9
  47.6 1.2 collective-permute-done.9.other_ref
  48.8 1.6 %collective-permute-start.10 = (f32[48,2048]{1,0:T(8,128)S(1)}, f32[48,2048]{1,0:T(8,128)}, u32[]{:S(2)}, u32[]{:S(2)}) collective-permute-start(f32[48,2048]{1,0:T(8,128)S(1)} %get-tuple-element.68.refs_0_), channel_id=1, source_target_pairs={{0,8},{8,16},{16,24},{24,0},{1,9},{9,17},{17,25},{25,1},{2,10},{10... | collective-permute-start | bytes 1179656 | tf_op jit(solution)/shard_map/ppermute | solution.py:551
  50.4 12.6 %factor_corner.1 = (f32[128,128]{1,0:T(8,128)S(1)}, f32[128,128]{1,0:T(8,128)S(1)}, f32[2,256,128]{2,1,0:T(8,128)S(1)}) custom-call(s32[3]{0:T(128)S(1)} %pad_add_fusion.where_ref, f32[64,128]{1,0:T(8,128)S(1)} %add_add_fusion.mine_ref, f32[64,128]{1,0:T(8,128)S(1)} %collective-permute-done.9.other_ref), custom_call_target="tpu_custom_call" | custom-call | tf_op jit(solution)/shard_map/factor_corner/pallas_call | solution.py:238
  63.0 0.1 broadcast_select_fusion.3.own2
  63.1 0.1 collective-permute-start.18
  63.2 0.0 collective-permute-done.1
  63.2 0.1 broadcast_select_fusion.6.own_ref.own1
  63.3 0.5 collective-permute-start.2
  63.8 0.7 copy-done
  64.6 7.8 %collective-permute-done.11.refs_2_ = f32[48,2048]{1,0:T(8,128)} collective-permute-done((f32[48,2048]{1,0:T(8,128)S(1)}, f32[48,2048]{1,0:T(8,128)}, u32[]{:S(2)}, u32[]{:S(2)}) %collective-permute-start.11) | collective-permute-done | bytes 393248 | tf_op jit(solution)/shard_map/ppermute | solution.py:551
  72.4 0.0 collective-permute-done.10.refs_1_
  72.4 1.0 copy-done.1
  73.4 6.9 %upper_rows.1 = (bf16[128,2048]{1,0:T(8,128)(2,1)S(1)}, bf16[128,2048]{1,0:T(8,128)(2,1)S(1)}, f32[64,2048]{1,0:T(8,128)S(1)}) custom-call(s32[3]{0:T(128)S(1)} %pad_add_fusion.where_ref, s32[128]{0:T(128)S(1)} %get-tuple-element.185, f32[48,2048]{1,0:T(8,128)S(1)} %get-tuple-element.68.refs_0_, f32[48,2048]{1,0:T(8,128)} %collective-permute-done.10.refs_1_, ...), custom_call_target="tpu_custom_call" | custom-call | tf_op jit(solution)/shard_map/upper_rows/pallas_call | solution.py:301
  80.2 4.0 %moved_rows.1 = (f32[64,2048]{1,0:T(8,128)}, f32[3,32,2048]{2,1,0:T(8,128)S(1)}) custom-call(s32[3]{0:T(128)S(1)} %pad_add_fusion.where_ref, s32[128]{0:T(128)S(1)} %get-tuple-element.185, f32[4096,2048]{1,0:T(8,128)} %get-tuple-element.169, f32[1024,128]{1,0:T(8,128)S(1)} %broadcast_select_fusion.6.own_ref.own1, ...), custom_call_target="tpu_custom_call" | custom-call | tf_op jit(solution)/shard_map/moved_rows/pallas_call | solution.py:372
  84.3 0.9 slice_bitcast_fusion
  85.2 1.9 %collective-permute-start.15 = (f32[32,2048]{1,0:T(8,128)}, f32[32,2048]{1,0:T(8,128)S(1)}, u32[]{:S(2)}, u32[]{:S(2)}) collective-permute-start(f32[32,2048]{1,0:T(8,128)} %get-tuple-element.109), channel_id=1, source_target_pairs={{0,24},{8,0},{1,25},{9,1},{2,26},{10,2},{3,27},{11,3},{4,28},{12,4... | collective-permute-start | bytes 786440 | tf_op jit(solution)/shard_map/ppermute | solution.py:568
  87.1 2.6 %collective-permute-start.14 = (f32[32,2048]{1,0:T(8,128)}, f32[32,2048]{1,0:T(8,128)S(1)}, u32[]{:S(2)}, u32[]{:S(2)}) collective-permute-start(f32[32,2048]{1,0:T(8,128)} %get-tuple-element.110), channel_id=1, source_target_pairs={{0,16},{8,24},{1,17},{9,25},{2,18},{10,26},{3,19},{11,27},{4,20},{... | collective-permute-start | bytes 786440 | tf_op jit(solution)/shard_map/ppermute | solution.py:568
  89.7 3.4 %collective-permute-start.13 = (f32[32,2048]{1,0:T(8,128)}, f32[32,2048]{1,0:T(8,128)}, u32[]{:S(2)}, u32[]{:S(2)}) collective-permute-start(f32[32,2048]{1,0:T(8,128)} %get-tuple-element.111), channel_id=1, source_target_pairs={{0,8},{8,16},{1,9},{9,17},{2,10},{10,18},{3,11},{11,19},{4,12},{12... | collective-permute-start | bytes 786440 | tf_op jit(solution)/shard_map/ppermute | solution.py:568
  93.1 0.0 collective-permute-done.18.other2
  93.1 33.1 %trailing.1.refs_6_ = f32[4096,2048]{1,0:T(8,128)} custom-call(s32[3]{0:T(128)S(1)} %pad_add_fusion.where_ref, f32[4096,2048]{1,0:T(8,128)} %get-tuple-element.169, f32[1024,128]{1,0:T(8,128)S(1)} %broadcast_select_fusion.6.own_ref.own1, f32[1024,128]{1,0:T(8,128)S(1)} %broadcast_select_fusion.3.own2, ...), custom_call_target="tpu_custom_call" | custom-call | flops 6442450944 | bytes 67108864 | tf_op jit(solution)/shard_map/trailing/pallas_call | solution.py:418
  126.2 0.0 collective-permute-done.15.refs_3_
  126.2 0.0 collective-permute-done.14.refs_2_
  126.2 6.3 %place_moved.1 = f32[4096,2048]{1,0:T(8,128)} custom-call(s32[3]{0:T(128)S(1)} %pad_add_fusion.where_ref, s32[128]{0:T(128)S(1)} %get-tuple-element.185, f32[64,2048]{1,0:T(8,128)} %get-tuple-element.174, f32[32,2048]{1,0:T(8,128)} %collective-permute-done.13.refs_1_, ...), custom_call_target="tpu_custom_call", output_to_operand_aliasing={{}: (8, {})} | custom-call | tf_op jit(solution)/shard_map/place_moved/pallas_call | solution.py:493
  (19 shorter events, 0.1 us)
Async XLA Ops:
  6.5 8.9 %copy-start.2 = (s32[2,64]{1,0:T(2,128)S(1)}, s32[2,64]{1,0:T(2,128)}, u32[]{:S(2)}) copy-start(s32[2,64]{1,0:T(2,128)} %param.7) | copy-start | bytes 1540
  8.4 18.0 %collective-permute-start.16 = (f32[1024,128]{1,0:T(8,128)S(1)}, f32[1024,128]{1,0:T(8,128)S(1)}, u32[]{:S(2)}, u32[]{:S(2)}) collective-permute-start(f32[1024,128]{1,0:T(8,128)S(1)} %get-tuple-element.107), channel_id=1, source_target_pairs={{0,4},{1,5},{8,12},{9,13},{16,20},{17,21},{24,28},{25,29}} | collective-permute-start | bytes 1572872 | tf_op jit(solution)/shard_map/ppermute | solution.py:509
  13.3 13.1 %collective-permute-start = (f32[1024,128]{1,0:T(8,128)S(1)}, f32[1024,128]{1,0:T(8,128)}, u32[]{:S(2)}, u32[]{:S(2)}) collective-permute-start(f32[1024,128]{1,0:T(8,128)S(1)} %get-tuple-element.108), channel_id=1, source_target_pairs={{0,2},{1,3},{8,10},{9,11},{16,18},{17,19},{24,26},{25,27}} | collective-permute-start | bytes 1572872 | tf_op jit(solution)/shard_map/ppermute | solution.py:509
  21.8 10.5 %collective-permute-start.5 = (f32[64,128]{1,0:T(8,128)S(1)}, f32[64,128]{1,0:T(8,128)S(1)}, u32[]{:S(2)}, u32[]{:S(2)}) collective-permute-start(f32[64,128]{1,0:T(8,128)S(1)} %get-tuple-element.66), channel_id=1, source_target_pairs={{0,24},{8,0},{16,8},{24,16},{1,25},{9,1},{17,9},{25,17},{2,26},{10... | collective-permute-start | bytes 98312 | tf_op jit(solution)/shard_map/ppermute | solution.py:537
  25.3 6.9 %collective-permute-start.4 = (f32[64,128]{1,0:T(8,128)S(1)}, f32[64,128]{1,0:T(8,128)S(1)}, u32[]{:S(2)}, u32[]{:S(2)}) collective-permute-start(f32[64,128]{1,0:T(8,128)S(1)} %get-tuple-element.66), channel_id=1, source_target_pairs={{0,16},{8,24},{16,0},{24,8},{1,17},{9,25},{17,1},{25,9},{2,18},{10... | collective-permute-start | bytes 98312 | tf_op jit(solution)/shard_map/ppermute | solution.py:537
  25.3 6.9 %collective-permute-start.3 = (f32[64,128]{1,0:T(8,128)S(1)}, f32[64,128]{1,0:T(8,128)S(1)}, u32[]{:S(2)}, u32[]{:S(2)}) collective-permute-start(f32[64,128]{1,0:T(8,128)S(1)} %get-tuple-element.66), channel_id=1, source_target_pairs={{0,8},{8,16},{16,24},{24,0},{1,9},{9,17},{17,25},{25,1},{2,10},{10... | collective-permute-start | bytes 98312 | tf_op jit(solution)/shard_map/ppermute | solution.py:537
  26.6 36.4 %collective-permute-start.17 = (f32[1024,128]{1,0:T(8,128)S(1)}, f32[1024,128]{1,0:T(8,128)}, u32[]{:S(2)}, u32[]{:S(2)}) collective-permute-start(f32[1024,128]{1,0:T(8,128)S(1)} %get-tuple-element.105), channel_id=1, source_target_pairs={{0,2},{1,3},{4,6},{5,7},{8,10},{9,11},{12,14},{13,15},{16,18},{17,... | collective-permute-start | bytes 1572872 | tf_op jit(solution)/shard_map/ppermute | solution.py:509
  32.3 10.5 %collective-permute-start.8 = (f32[64,128]{1,0:T(8,128)S(1)}, f32[64,128]{1,0:T(8,128)S(1)}, u32[]{:S(2)}, u32[]{:S(2)}) collective-permute-start(f32[64,128]{1,0:T(8,128)S(1)} %add_add_fusion.1), channel_id=1, source_target_pairs={{0,6},{1,7},{8,14},{9,15},{16,22},{17,23},{24,30},{25,31}} | collective-permute-start | bytes 98312 | tf_op jit(solution)/shard_map/ppermute | solution.py:539
  33.6 11.8 %collective-permute-start.7 = (f32[64,128]{1,0:T(8,128)S(1)}, f32[64,128]{1,0:T(8,128)S(1)}, u32[]{:S(2)}, u32[]{:S(2)}) collective-permute-start(f32[64,128]{1,0:T(8,128)S(1)} %add_add_fusion.1), channel_id=1, source_target_pairs={{0,4},{1,5},{8,12},{9,13},{16,20},{17,21},{24,28},{25,29}} | collective-permute-start | bytes 98312 | tf_op jit(solution)/shard_map/ppermute | solution.py:539
  34.9 12.6 %collective-permute-start.6 = (f32[64,128]{1,0:T(8,128)S(1)}, f32[64,128]{1,0:T(8,128)S(1)}, u32[]{:S(2)}, u32[]{:S(2)}) collective-permute-start(f32[64,128]{1,0:T(8,128)S(1)} %add_add_fusion.1), channel_id=1, source_target_pairs={{0,2},{1,3},{8,10},{9,11},{16,18},{17,19},{24,26},{25,27}} | collective-permute-start | bytes 98312 | tf_op jit(solution)/shard_map/ppermute | solution.py:539
  36.2 27.6 %collective-permute-start.12 = (f32[48,2048]{1,0:T(8,128)S(1)}, f32[48,2048]{1,0:T(8,128)S(1)}, u32[]{:S(2)}, u32[]{:S(2)}) collective-permute-start(f32[48,2048]{1,0:T(8,128)S(1)} %get-tuple-element.68.refs_0_), channel_id=1, source_target_pairs={{0,24},{8,0},{16,8},{24,16},{1,25},{9,1},{17,9},{25,17},{2,26},{10... | collective-permute-start | bytes 1179656 | tf_op jit(solution)/shard_map/ppermute | solution.py:551
  42.8 29.5 %collective-permute-start.11 = (f32[48,2048]{1,0:T(8,128)S(1)}, f32[48,2048]{1,0:T(8,128)}, u32[]{:S(2)}, u32[]{:S(2)}) collective-permute-start(f32[48,2048]{1,0:T(8,128)S(1)} %get-tuple-element.68.refs_0_), channel_id=1, source_target_pairs={{0,16},{8,24},{16,0},{24,8},{1,17},{9,25},{17,1},{25,9},{2,18},{10... | collective-permute-start | bytes 1179656 | tf_op jit(solution)/shard_map/ppermute | solution.py:551
  45.4 17.7 %collective-permute-start.1 = (f32[1024,128]{1,0:T(8,128)S(1)}, f32[1024,128]{1,0:T(8,128)}, u32[]{:S(2)}, u32[]{:S(2)}) collective-permute-start(f32[1024,128]{1,0:T(8,128)S(1)} %get-tuple-element.106), channel_id=1, source_target_pairs={{0,4},{1,5},{2,6},{3,7},{8,12},{9,13},{10,14},{11,15},{16,20},{17,... | collective-permute-start | bytes 1572872 | tf_op jit(solution)/shard_map/ppermute | solution.py:509
  47.5 1.3 collective-permute-start.9
  48.8 23.5 %collective-permute-start.10 = (f32[48,2048]{1,0:T(8,128)S(1)}, f32[48,2048]{1,0:T(8,128)}, u32[]{:S(2)}, u32[]{:S(2)}) collective-permute-start(f32[48,2048]{1,0:T(8,128)S(1)} %get-tuple-element.68.refs_0_), channel_id=1, source_target_pairs={{0,8},{8,16},{16,24},{24,0},{1,9},{9,17},{17,25},{25,1},{2,10},{10... | collective-permute-start | bytes 1179656 | tf_op jit(solution)/shard_map/ppermute | solution.py:551
  63.1 30.0 %collective-permute-start.18 = (f32[1024,128]{1,0:T(8,128)S(1)}, f32[1024,128]{1,0:T(8,128)S(1)}, u32[]{:S(2)}, u32[]{:S(2)}) collective-permute-start(f32[1024,128]{1,0:T(8,128)S(1)} %broadcast_select_fusion.3.own2), channel_id=1, source_target_pairs={{0,1},{1,0},{2,3},{3,2},{4,5},{5,4},{6,7},{7,6},{8,9},{9,8},{10,11... | collective-permute-start | bytes 1572872 | tf_op jit(solution)/shard_map/ppermute | solution.py:549
  63.3 17.0 %collective-permute-start.2 = (f32[1024,128]{1,0:T(8,128)S(1)}, f32[1024,128]{1,0:T(8,128)S(1)}, u32[]{:S(2)}, u32[]{:S(2)}) collective-permute-start(f32[1024,128]{1,0:T(8,128)S(1)} %broadcast_select_fusion.6.own_ref.own1), channel_id=1, source_target_pairs={{0,1},{1,0},{2,3},{3,2},{4,5},{5,4},{6,7},{7,6},{8,9},{9,8},{10,11... | collective-permute-start | bytes 1572872 | tf_op jit(solution)/shard_map/ppermute | solution.py:549
  63.8 0.7 copy-start
  72.4 1.0 copy-start.1
  85.2 41.0 %collective-permute-start.15 = (f32[32,2048]{1,0:T(8,128)}, f32[32,2048]{1,0:T(8,128)S(1)}, u32[]{:S(2)}, u32[]{:S(2)}) collective-permute-start(f32[32,2048]{1,0:T(8,128)} %get-tuple-element.109), channel_id=1, source_target_pairs={{0,24},{8,0},{1,25},{9,1},{2,26},{10,2},{3,27},{11,3},{4,28},{12,4... | collective-permute-start | bytes 786440 | tf_op jit(solution)/shard_map/ppermute | solution.py:568
  87.1 39.1 %collective-permute-start.14 = (f32[32,2048]{1,0:T(8,128)}, f32[32,2048]{1,0:T(8,128)S(1)}, u32[]{:S(2)}, u32[]{:S(2)}) collective-permute-start(f32[32,2048]{1,0:T(8,128)} %get-tuple-element.110), channel_id=1, source_target_pairs={{0,16},{8,24},{1,17},{9,25},{2,18},{10,26},{3,19},{11,27},{4,20},{... | collective-permute-start | bytes 786440 | tf_op jit(solution)/shard_map/ppermute | solution.py:568
  89.7 36.5 %collective-permute-start.13 = (f32[32,2048]{1,0:T(8,128)}, f32[32,2048]{1,0:T(8,128)}, u32[]{:S(2)}, u32[]{:S(2)}) collective-permute-start(f32[32,2048]{1,0:T(8,128)} %get-tuple-element.111), channel_id=1, source_target_pairs={{0,8},{8,16},{1,9},{9,17},{2,10},{10,18},{3,11},{11,19},{4,12},{12... | collective-permute-start | bytes 786440 | tf_op jit(solution)/shard_map/ppermute | solution.py:568

commit v2 on v1

v2 whole, which is shorter than its diff:
```python
import functools

import jax
import jax.numpy as jnp
from jax import lax
from jax.experimental import pallas as pl
from jax.experimental.pallas import tpu as pltpu
from jax.sharding import PartitionSpec as P

NB = 64
NP = 2 * NB
LANES = 128
SUB = 8
HIGHEST_PRECISION = lax.Precision.HIGHEST
MIB = 1024 * 1024


def capacities(grid_rows):
    cap = min(NP, -(-3 * NP // (2 * grid_rows * SUB)) * SUB)
    cap_top = min(NB, -(-2 * NB // (grid_rows * SUB)) * SUB)
    return cap, cap_top


def owner_of(row, grid_rows):
    return lax.rem(lax.div(row, NB), grid_rows)


def local_of(row, grid_rows):
    return lax.div(row, NB * grid_rows) * NB + lax.rem(row, NB)


def split(x):
    high = x.astype(jnp.bfloat16)
    return high, (x - high.astype(jnp.float32)).astype(jnp.bfloat16)


def mm(a, b):
    return jnp.dot(a, b, preferred_element_type=jnp.float32)


def gather_kernel(grid_rows, piv_ref, m_ref, rows_ref, corner_ref, owned_ref, _, line_ref, sem):
    my_row = lax.axis_index("row")
    my_col = lax.axis_index("col")
    cap = rows_ref.shape[0]
    line_ref[...] = jnp.zeros_like(line_ref)
    rows_ref[...] = jnp.zeros_like(rows_ref)

    def line_copy(row, t):
        return pltpu.make_async_copy(
            m_ref.at[pl.ds(row, 1), pl.ds(0, LANES)], line_ref.at[pl.ds(t, 1), :], sem.at[0]
        )

    def row_copy(row, slot):
        return pltpu.make_async_copy(
            m_ref.at[pl.ds(row, 1), :], rows_ref.at[pl.ds(slot, 1), :], sem.at[1]
        )

    def start(t, count):
        row = piv_ref[t]
        mine = owner_of(row, grid_rows) == my_row

        @pl.when(mine)
        def _():
            owned_ref[count] = t
            line_copy(local_of(row, grid_rows), t).start()

        @pl.when(mine & (count < cap))
        def _():
            row_copy(local_of(row, grid_rows), count).start()

        return count + mine.astype(jnp.int32)

    first = lax.fori_loop(0, NB, start, jnp.int32(0))
    count = lax.fori_loop(NB, NP, start, first)
    owned_ref[NP] = first
    owned_ref[NP + 1] = count

    def wait_line(_, carry):
        line_copy(0, 0).wait()
        return carry

    def wait_row(_, carry):
        row_copy(0, 0).wait()
        return carry

    lax.fori_loop(0, count, wait_line, 0)
    lines = line_ref[...]
    left = lax.broadcasted_iota(jnp.int32, lines.shape, 1) < NB
    corner_ref[...] = jnp.where(
        left, jnp.where(my_col == 0, lines, 0.0), jnp.where(my_col == 1, pltpu.roll(lines, NB, 1), 0.0)
    )
    lax.fori_loop(0, jnp.minimum(count, cap), wait_row, 0)


def gather_rows(matrix, pivots, cap, grid_rows):
    cols = matrix.shape[1]
    smem = pl.BlockSpec(memory_space=pltpu.SMEM)
    vmem = pl.BlockSpec(memory_space=pltpu.VMEM)
    anywhere = pl.BlockSpec(memory_space=pl.ANY)
    return pl.pallas_call(
        functools.partial(gather_kernel, grid_rows),
        out_shape=(
            jax.ShapeDtypeStruct((cap, cols), jnp.float32),
            jax.ShapeDtypeStruct((NP, LANES), jnp.float32),
            jax.ShapeDtypeStruct((NP + 2,), jnp.int32),
            jax.ShapeDtypeStruct((NP, cols), jnp.float32),
        ),
        in_specs=[smem, anywhere],
        out_specs=(vmem, vmem, smem, anywhere),
        scratch_shapes=[pltpu.VMEM((NP, LANES), jnp.float32), pltpu.SemaphoreType.DMA((2,))],
        compiler_params=pltpu.CompilerParams(vmem_limit_bytes=16 * MIB),
        name="gather_rows",
    )(pivots, matrix)


def pack_kernel(top_ref, bottom_ref, _, out_ref):
    lane = lax.broadcasted_iota(jnp.int32, out_ref.shape, 1)
    out_ref[...] = jnp.where(lane < NB, top_ref[...], pltpu.roll(bottom_ref[...], NB, 1))


def pack_panel(matrix, after, steps):
    half = matrix.shape[0] // 2
    size = half // steps
    return pl.pallas_call(
        pack_kernel,
        out_shape=jax.ShapeDtypeStruct((half, LANES), jnp.float32),
        grid=(steps,),
        in_specs=[
            pl.BlockSpec((size, LANES), lambda i: (i, 0)),
            pl.BlockSpec((size, LANES), lambda i: (i + steps, 0)),
            pl.BlockSpec(memory_space=pl.ANY),
        ],
        out_specs=pl.BlockSpec((size, LANES), lambda i: (i, 0)),
        compiler_params=pltpu.CompilerParams(vmem_limit_bytes=16 * MIB),
        name="pack_panel",
    )(matrix, matrix, after)


GROUP = 4


def eliminate_in_place(work, lane, sub):
    count = len(work)
    work = list(work)
    shape = work[0].shape
    for first in range(0, NP, GROUP):
        block, inner = divmod(first, SUB)
        below = list(range(block, count))
        cols = [
            {i: jnp.broadcast_to(work[i][:, first + j : first + j + 1], shape) for i in below}
            for j in range(GROUP)
        ]
        rows = [
            jnp.broadcast_to(work[block][inner + j : inner + j + 1, :], shape)
            for j in range(GROUP)
        ]
        spots = [
            [jnp.broadcast_to(cols[j][block][inner + i : inner + i + 1, :], shape) for j in range(GROUP)]
            for i in range(GROUP)
        ]
        scaled = []
        for j in range(GROUP):
            weight = 1.0 / spots[j][j]
            at_j = lane == first + j
            line = jnp.where(at_j, 1.0, rows[j]) * weight
            factor = {l: spots[j][l] * weight for l in range(j + 1, GROUP)}
            for i in range(j + 1, GROUP):
                rows[i] = jnp.where(at_j, 0.0, rows[i]) - spots[i][j] * line
                for l in range(j + 1, GROUP):
                    spots[i][l] = spots[i][l] - spots[i][j] * factor[l]
            for l in range(j + 1, GROUP):
                for i in below:
                    cols[l][i] = cols[l][i] - cols[j][i] * factor[l]
            later = (lane > first + j) & (lane < first + GROUP)
            scaled.append(jnp.where(later, 0.0, line))
        in_group = (lane >= first) & (lane < first + GROUP)
        for i in below:
            updated = jnp.where(in_group, 0.0, work[i])
            for j in range(GROUP):
                updated = updated - cols[j][i] * scaled[j]
            if i == block:
                updated = jnp.where(sub < inner, work[i], updated)
                for j in range(GROUP):
                    updated = jnp.where(sub == inner + j, rows[j], updated)
            work[i] = updated
    return work


def corner_kernel(corner_ref, order_ref, lu_ref, linv_ref, weights_ref):
    my_col = lax.axis_index("col")
    odd = lax.rem(my_col, 2) == 1
    a = corner_ref[...]
    a_t = a.T
    lane = lax.broadcasted_iota(jnp.int32, (SUB, LANES), 1)
    sub = lax.broadcasted_iota(jnp.int32, (SUB, LANES), 0)
    blocks = range(0, NP, SUB)
    first = eliminate_in_place([a[i : i + SUB] for i in blocks], lane, sub)
    second = eliminate_in_place([a_t[i : i + SUB] for i in blocks], lane, sub)
    w1 = jnp.concatenate(first, axis=0)
    w2 = jnp.concatenate(second, axis=0)
    row = lax.broadcasted_iota(jnp.int32, (NP, NP), 0)
    col = lax.broadcasted_iota(jnp.int32, (NP, NP), 1)
    inverse_d = 1.0 / jnp.sum(jnp.where(row == col, w1, 0.0), axis=0, keepdims=True)
    order = order_ref[...]
    linv = split(jnp.where(row > col, w1, jnp.where(row == col, 1.0, 0.0)))
    linv_ref[...] = jnp.concatenate([mm(x, order).astype(jnp.bfloat16) for x in linv], axis=1)
    w2_t = w2.T
    lu = jnp.where(row <= col, w1, w2_t * inverse_d)
    lu_ref[...] = jnp.where(my_col == 1, pltpu.roll(lu, NB, 1), lu)
    uinv = jnp.where(row < col, w2_t, jnp.where(row == col, 1.0, 0.0)) * inverse_d
    mine = jnp.where(odd, uinv[NB:], uinv[:NB])
    other = jnp.where(odd, uinv[:NB], uinv[NB:])
    zero = jnp.zeros_like(mine)
    weights_ref[0] = jnp.concatenate([mine, zero, other, zero], axis=0)
    weights_ref[1] = jnp.concatenate([zero, mine, zero, other], axis=0)


def factor_corner(corner, order):
    vmem = pl.BlockSpec(memory_space=pltpu.VMEM)
    return pl.pallas_call(
        corner_kernel,
        out_shape=(
            jax.ShapeDtypeStruct((NP, NP), jnp.float32),
            jax.ShapeDtypeStruct((NP, 2 * order.shape[1]), jnp.bfloat16),
            jax.ShapeDtypeStruct((2, 2 * NP, NP), jnp.float32),
        ),
        in_specs=[vmem, vmem],
        out_specs=(vmem, vmem, vmem),
        compiler_params=pltpu.CompilerParams(vmem_limit_bytes=24 * MIB),
        name="factor_corner",
    )(corner, order)


def upper_kernel(over_ref, rows_ref, all_ref, linv_ref, lu_ref, upper_ref, top_ref, a_ref, sem):
    my_row = lax.axis_index("row")
    my_col = lax.axis_index("col")
    count, cols = rows_ref.shape
    width = min(cols, 512)

    def solve(source_ref, depth):
        high_part = linv_ref[:, :depth]
        both = jnp.concatenate([high_part, linv_ref[:, count : count + depth]], axis=1)
        for start in range(0, cols, width):
            span = slice(start, start + width)
            high, low = split(source_ref[:, span])
            a_ref[:, span] = mm(both, jnp.concatenate([high, high], axis=0)) + mm(high_part, low)

    @pl.when(over_ref[0] == 0)
    def _():
        solve(rows_ref, count)

    @pl.when(over_ref[0] != 0)
    def _():
        copy = pltpu.make_async_copy(all_ref, a_ref, sem)
        copy.start()
        copy.wait()
        solve(a_ref, NP)

    @pl.when(my_row == 0)
    def _():
        top_ref[...] = a_ref[:NB]

    @pl.when(my_row != 0)
    def _():
        top_ref[...] = a_ref[NB:]

    @pl.when(my_col < 2)
    def _():
        lane = lax.broadcasted_iota(jnp.int32, (NP, LANES), 1)
        row = lax.broadcasted_iota(jnp.int32, (NP, LANES), 0)
        lu_part = jnp.where(my_row == 0, lu_ref[:NB], lu_ref[NB:])
        top_ref[:, :LANES] = jnp.where(lane[:NB] < NB, lu_part, top_ref[:, :LANES])
        unit = jnp.where(row == lane + my_col * NB, -1.0, 0.0)
        a_ref[:, :LANES] = jnp.where(lane < NB, unit, a_ref[:, :LANES])

    high, low = split(a_ref[...])
    upper_ref[:NP] = high
    upper_ref[NP : 2 * NP] = high
    upper_ref[2 * NP :] = low


def upper_rows_of(rows, everything, linv, lu, over):
    cols = rows.shape[1]
    smem = pl.BlockSpec(memory_space=pltpu.SMEM)
    vmem = pl.BlockSpec(memory_space=pltpu.VMEM)
    return pl.pallas_call(
        upper_kernel,
        out_shape=(
            jax.ShapeDtypeStruct((3 * NP, cols), jnp.bfloat16),
            jax.ShapeDtypeStruct((NB, cols), jnp.float32),
        ),
        in_specs=[smem, vmem, pl.BlockSpec(memory_space=pl.ANY), vmem, vmem],
        out_specs=(vmem, vmem),
        scratch_shapes=[pltpu.VMEM((NP, cols), jnp.float32), pltpu.SemaphoreType.DMA(())],
        compiler_params=pltpu.CompilerParams(vmem_limit_bytes=32 * MIB),
        name="upper_rows",
    )(over, rows, everything, linv, lu)


def lower_of(own, other, weights):
    p_high, p_low = split(jnp.concatenate([own, other], axis=1))
    w_high, w_low = split(weights)
    lower = mm(p_high, w_high) + (mm(p_high, w_low) + mm(p_low, w_high))
    high, low = split(lower)
    return jnp.concatenate([high, low, high], axis=1)


def update_rows(a_ref, lower, upper_ref, out_ref, is_panel):
    rows, cols = out_ref.shape
    width = min(cols, 256)
    lane = lax.broadcasted_iota(jnp.int32, (rows, width), 1)
    for start in range(0, cols, width):
        span = slice(start, start + width)
        a = a_ref[:, span]
        if start == 0:
            a = jnp.where((lane < NB) & is_panel, 0.0, a)
        out_ref[:, span] = a - mm(lower, upper_ref[:, span])


def moved_kernel(grid_rows, cap_top, piv_ref, m_ref, own_ref, other_ref, weights_ref, upper_ref, out_ref, *refs):
    packed_refs = refs[: grid_rows - 1]
    count_ref = refs[grid_rows - 1]
    my_row = lax.axis_index("row")
    lower = lower_of(own_ref[...], other_ref[...], weights_ref[0])
    update_rows(m_ref, lower, upper_ref, out_ref, lax.axis_index("col") < 2)
    for r in range(grid_rows):
        count_ref[r] = 0

    @pl.when(my_row < 2)
    def _():
        def place(k, carry):
            owner = owner_of(piv_ref[my_row * NB + k], grid_rows)
            slot = count_ref[owner]
            count_ref[owner] = slot + 1
            ahead = lax.rem(owner - my_row + grid_rows, grid_rows)
            for s in range(1, grid_rows):

                @pl.when((ahead == s) & (slot < cap_top))
                def _(s=s):
                    packed_refs[s - 1][pl.ds(slot, 1), :] = out_ref[pl.ds(k, 1), :]

            return carry

        lax.fori_loop(0, NB, place, 0)


def moved_rows(matrix, own, other, weights, upper, pivots, cap_top, grid_rows):
    cols = matrix.shape[1]
    smem = pl.BlockSpec(memory_space=pltpu.SMEM)
    vmem = pl.BlockSpec(memory_space=pltpu.VMEM)
    head = lambda width: pl.BlockSpec((NB, width), lambda i: (0, 0))
    return pl.pallas_call(
        functools.partial(moved_kernel, grid_rows, cap_top),
        out_shape=(jax.ShapeDtypeStruct((NB, cols), jnp.float32),)
        + (jax.ShapeDtypeStruct((cap_top, cols), jnp.float32),) * (grid_rows - 1),
        grid=(1,),
        in_specs=[smem, head(cols), head(LANES), head(LANES), vmem, vmem],
        out_specs=(head(cols),)
        + (pl.BlockSpec((cap_top, cols), lambda i: (0, 0)),) * (grid_rows - 1),
        scratch_shapes=[pltpu.SMEM((grid_rows,), jnp.int32)],
        compiler_params=pltpu.CompilerParams(vmem_limit_bytes=32 * MIB),
        name="moved_rows",
    )(pivots, matrix, own, other, weights, upper)


def trailing_kernel(m_ref, own_ref, other_ref, weights_ref, upper_ref, out_ref, lower_ref):
    step = pl.program_id(0)
    rows = m_ref.shape[0]
    half = own_ref.shape[0] // rows

    def prepare(block):
        here = pl.ds(pl.multiple_of(lax.rem(block, half) * rows, rows), rows)
        lower_ref[lax.rem(block, 2)] = lower_of(
            own_ref[here, :], other_ref[here, :], weights_ref[lax.div(block, half)]
        )

    @pl.when(step == 0)
    def _():
        prepare(step)

    update_rows(
        m_ref, lower_ref[lax.rem(step, 2)], upper_ref, out_ref, lax.axis_index("col") < 2
    )
    prepare(jnp.minimum(step + 1, 2 * half - 1))


def trailing(matrix, own, other, weights, upper):
    rows, cols = matrix.shape
    size = min(512, rows // 2)
    vmem = pl.BlockSpec(memory_space=pltpu.VMEM)
    return pl.pallas_call(
        trailing_kernel,
        out_shape=jax.ShapeDtypeStruct((rows, cols), jnp.float32),
        grid=(rows // size,),
        in_specs=[pl.BlockSpec((size, cols), lambda i: (i, 0))] + [vmem] * 4,
        out_specs=pl.BlockSpec((size, cols), lambda i: (i, 0)),
        scratch_shapes=[pltpu.VMEM((2, size, 3 * NP), jnp.bfloat16)],
        compiler_params=pltpu.CompilerParams(vmem_limit_bytes=40 * MIB),
        cost_estimate=pl.CostEstimate(
            flops=6 * rows * cols * NP, bytes_accessed=8 * rows * cols, transcendentals=0
        ),
        name="trailing",
    )(matrix, own, other, weights, upper)


def place_kernel(grid_rows, over_ref, piv_ref, owned_ref, *refs):
    moved_refs = refs[:grid_rows]
    all_ref, top_ref, _, out_ref, sem = refs[grid_rows:]
    my_row = lax.axis_index("row")
    first, total = owned_ref[NP], owned_ref[NP + 1]

    @pl.when(my_row < 2)
    def _():
        pltpu.make_async_copy(top_ref, out_ref.at[pl.ds(0, NB), :], sem).start()

    def put(source_ref, source_row, t):
        to = local_of(piv_ref[t], grid_rows)
        pltpu.make_async_copy(
            source_ref.at[pl.ds(source_row, 1), :], out_ref.at[pl.ds(to, 1), :], sem
        ).start()

    def put_from(n, carry, source_ref, row_of):
        t = owned_ref[n]
        put(source_ref, row_of(n, t), t)
        return carry

    def put_all(low, high, source_ref, row_of):
        lax.fori_loop(
            low, high, functools.partial(put_from, source_ref=source_ref, row_of=row_of), 0
        )

    packed = over_ref[0] == 0
    for panel, low, high in ((0, jnp.int32(0), first), (1, first, total)):
        back = lax.rem(my_row - panel + grid_rows, grid_rows)

        @pl.when(packed & (back == 0))
        def _(panel=panel, low=low, high=high):
            put_all(low, high, moved_refs[0], lambda n, t: t - panel * NB)

        for s in range(1, grid_rows):

            @pl.when(packed & (back == s))
            def _(s=s, low=low, high=high):
                put_all(low, high, moved_refs[s], lambda n, t: n - low)

    @pl.when(~packed)
    def _():
        put_all(0, total, all_ref, lambda n, t: t)

    def wait(_, carry):
        pltpu.make_async_copy(
            moved_refs[0].at[pl.ds(0, 1), :], out_ref.at[pl.ds(0, 1), :], sem
        ).wait()
        return carry

    lax.fori_loop(0, total, wait, 0)

    @pl.when(my_row < 2)
    def _():
        pltpu.make_async_copy(top_ref, out_ref.at[pl.ds(0, NB), :], sem).wait()


def place_moved(moved, everything, top, result, pivots, owned, over, grid_rows):
    smem = pl.BlockSpec(memory_space=pltpu.SMEM)
    anywhere = pl.BlockSpec(memory_space=pl.ANY)
    return pl.pallas_call(
        functools.partial(place_kernel, grid_rows),
        out_shape=jax.ShapeDtypeStruct(result.shape, result.dtype),
        in_specs=[smem, smem, smem] + [anywhere] * (grid_rows + 3),
        out_specs=anywhere,
        input_output_aliases={grid_rows + 5: 0},
        scratch_shapes=[pltpu.SemaphoreType.DMA(())],
        compiler_params=pltpu.CompilerParams(vmem_limit_bytes=16 * MIB),
        name="place_moved",
    )(over, pivots, owned, *moved, everything, top, result)


def spread_chips(value, order, my_chip, chips):
    reached = [0]
    for bit in order:
        pairs = [(2 * c + k, 2 * (c | bit) + k) for c in reached for k in range(2)]
        arrived = lax.ppermute(value, "col", pairs)
        value = jnp.where((my_chip & bit) != 0, arrived, value)
        reached = reached + [c | bit for c in reached]
    return value


def shards(matrix, pivots):
    grid_rows = lax.axis_size("row")
    grid_cols = lax.axis_size("col")
    chips = grid_cols // 2
    assert grid_rows > 1 and chips * 2 == grid_cols and not chips & (chips - 1)
    my_row = lax.axis_index("row")
    my_chip = lax.axis_index("col") // 2
    cap, cap_top = capacities(grid_rows)
    flat = pivots.reshape(-1)
    swap = [(c, c ^ 1) for c in range(grid_cols)]
    bits = [1 << b for b in range(chips.bit_length() - 1)]

    rows, corner, owned, unwritten = gather_rows(matrix, flat, cap, grid_rows)
    all_corner = lax.psum(corner, ("row", "col"))
    all_rows = lax.all_gather(rows, "row", tiled=True)

    packed = pack_panel(matrix, corner, 2)
    quarter = packed.shape[0] // 2
    own = jnp.concatenate(
        [
            spread_chips(packed[:quarter], bits, my_chip, chips),
            spread_chips(packed[quarter:], bits[::-1], my_chip, chips),
        ],
        axis=0,
    )
    other = lax.ppermute(own, "col", swap)

    owner = owner_of(flat, grid_rows)
    number = jnp.arange(NP, dtype=jnp.int32)
    same = owner[:, None] == owner[None, :]
    rank = jnp.sum(same & (number[None, :] < number[:, None]), axis=1, dtype=jnp.int32)
    alike = same & (number[None, :] // NB == number[:, None] // NB)
    panel_count = jnp.sum(alike, axis=1, dtype=jnp.int32)
    over = (jnp.max(jnp.maximum(rank + 1 - cap, panel_count - cap_top)) > 0).astype(jnp.int32)
    position = jnp.where(over > 0, number, owner * cap + rank)
    order = position[:, None] == jnp.arange(grid_rows * cap, dtype=jnp.int32)[None, :]
    order = order.astype(jnp.bfloat16)

    def sum_rows(state):
        mine = owner == my_row
        local = jnp.where(mine, local_of(flat, grid_rows), 0)
        picked = jnp.where(mine[:, None], matrix[local], 0.0)
        return jnp.int32(0), lax.psum(picked, "row")

    everything = lax.while_loop(lambda state: state[0] > 0, sum_rows, (over, unwritten))[1]

    over_list = over.reshape(1)
    lu, linv, weights = factor_corner(all_corner, order)
    upper, top = upper_rows_of(all_rows, everything, linv, lu, over_list)
    kept, *leaving = moved_rows(matrix, own, other, weights, upper, flat, cap_top, grid_rows)
    moved = [kept]
    for s in range(1, grid_rows):
        pairs = [(c, (c + s) % grid_rows) for c in range(2)]
        moved.append(lax.ppermute(leaving[s - 1], "row", pairs))

    def sum_moved(state):
        halves = [jnp.where(my_row == c, kept, 0.0) for c in range(2)]
        return jnp.int32(0), lax.psum(jnp.concatenate(halves, axis=0), "row")

    everything = lax.while_loop(lambda state: state[0] > 0, sum_moved, (over, everything))[1]
    result = trailing(matrix, own, other, weights, upper)
    return place_moved(moved, everything, top, result, flat, owned, over_list, grid_rows)


def solution(mesh):
    placed = (P("row", "col"), P())
    return jax.shard_map(
        shards, mesh=mesh, in_specs=placed, out_specs=P("row", "col"), check_vma=False
    )
```

time: 140 us -> 239 us (1.71)
  waiting for transfers between devices: 12 us -> 134 us
  starting transfers between devices: 39.7 us -> 22 us
  Pallas kernels: 68.1 us -> 59.6 us
    psum x0 -> x1, waiting for transfers between devices: none -> 115 us  [shards(): all_corner = lax.psum(corner, ('row', 'col'))]
    ppermute x4, waiting for transfers between devices: 0.01 us -> 17.8 us  [spread_chips(): arrived = lax.ppermute(value, 'col', pairs)]
    ppermute x12 -> x1, starting transfers between devices: 17 us -> 0.07 us  [shards(): other = lax.ppermute(own, 'col', swap)]
    pallas_call x3, Pallas kernels: 52.5 us -> 40.2 us  [the longest x1 27.4 us: trailing(): pl.pallas_call(trailing_kernel, out_shape=jax.ShapeDtypeStruct((rows, col...]
    ppermute x12 -> x1, waiting for transfers between devices: 12 us -> 0.01 us  [shards(): other = lax.ppermute(own, 'col', swap)]
  transfers between devices with their start and end apart: 19 -> 10, of which waited for: 3 -> 5; matrix products, arithmetic and copies ran while one was open for 2% -> 1% of each run, Pallas kernels for 43% -> 17%
where the time goes in v2:
time: 239 us; the launch traced here: 237 us
  waiting for transfers between devices  134 us (56%)
  Pallas kernels  59.6 us (25%)
  starting transfers between devices  22 us (9%)
  between operations  15.7 us (7%)
  local copies, waits for them, and re-layouts  3.88 us (2%)
    psum x1, waiting for transfers between devices, shards(): all_corner = lax.psum(corner, ('row', 'col'))  115 us
    pallas_call x1, Pallas kernels, trailing(): pl.pallas_call(trailing_kernel, out_shape=jax.ShapeDtypeStruct((rows, col...  27.4 us
    ppermute x4, waiting for transfers between devices, spread_chips(): arrived = lax.ppermute(value, 'col', pairs)  17.8 us
    ppermute x4, starting transfers between devices, spread_chips(): arrived = lax.ppermute(value, 'col', pairs)  13.9 us
    pallas_call x1, Pallas kernels, factor_corner(): pl.pallas_call(corner_kernel, out_shape=(jax.ShapeDtypeStruct((NP, NP), j...  12 us
    pallas_call x1, Pallas kernels, place_moved(): pl.pallas_call(functools.partial(place_kernel, grid_rows), out_shape=jax....  8.15 us
    ppermute x3, starting transfers between devices, shards(): moved.append(lax.ppermute(leaving[s - 1], 'row', pairs))  7.96 us
    pallas_call x1, Pallas kernels, moved_rows(): pl.pallas_call(functools.partial(moved_kernel, grid_rows, cap_top), out_s...  5.08 us
  transfers between devices with their start and end apart: 10, of which 5 were waited for; matrix products, arithmetic and copies ran while one was open for 1% of the time, Pallas kernels for 17%

profile of v2, /device:TPU:0, one launch (start us, length us, event | category | flops | bytes accessed | tf_op | source)
XLA Modules:
  0.0 236.6 jit_solution(3835963340597680755)
XLA Ops:
  7.4 0.8 reshape.203.piv_ref
  8.1 4.5 %gather_rows.1 = (f32[48,2048]{1,0:T(8,128)}, f32[128,128]{1,0:T(8,128)}, s32[130]{0:T(256)S(1)}, f32[128,2048]{1,0:T(8,128)}) custom-call(s32[128]{0:T(128)S(1)} %reshape.203.piv_ref, f32[4096,2048]{1,0:T(8,128)} %m_ref.5), custom_call_target="tpu_custom_call" | custom-call | tf_op jit(solution)/shard_map/gather_rows/pallas_call | solution.py:100
  12.6 1.8 pack_panel.1
  14.4 0.9 fusion.5
  15.3 4.9 %collective-permute-start = (f32[1024,128]{1,0:T(8,128)}, f32[1024,128]{1,0:T(8,128)S(1)}, u32[]{:S(2)}, u32[]{:S(2)}) collective-permute-start(f32[1024,128]{1,0:T(8,128)} %get-tuple-element.111), channel_id=1, source_target_pairs={{0,2},{1,3},{8,10},{9,11},{16,18},{17,19},{24,26},{25,27}} | collective-permute-start | bytes 1572872 | tf_op jit(solution)/shard_map/ppermute | solution.py:482
  20.1 2.1 collective-permute-start.2
  22.2 0.2 convert_reduce_fusion.1
  22.4 0.6 maximum_reduce_fusion
  23.7 0.0 all-reduce.8.cloned.1.call-start
  23.8 0.5 all-reduce.8.cloned.1.call-update
  24.3 0.0 all-gather.2.cloned.1.call-start
  24.4 0.7 all-gather.2.cloned.1.call-update
  25.1 6.5 %collective-permute-done = f32[1024,128]{1,0:T(8,128)S(1)} collective-permute-done((f32[1024,128]{1,0:T(8,128)}, f32[1024,128]{1,0:T(8,128)S(1)}, u32[]{:S(2)}, u32[]{:S(2)}) %collective-permute-start) | collective-permute-done | bytes 524320 | tf_op jit(solution)/shard_map/ppermute | solution.py:482
  31.6 1.0 collective-permute-done.2
  32.6 0.2 broadcast_select_fusion.4
  32.8 5.6 %collective-permute-start.1 = (f32[1024,128]{1,0:T(8,128)S(1)}, f32[1024,128]{1,0:T(8,128)S(1)}, u32[]{:S(2)}, u32[]{:S(2)}) collective-permute-start(f32[1024,128]{1,0:T(8,128)S(1)} %get-tuple-element.109), channel_id=1, source_target_pairs={{0,4},{1,5},{2,6},{3,7},{8,12},{9,13},{10,14},{11,15},{16,20},{17,... | collective-permute-start | bytes 1572872 | tf_op jit(solution)/shard_map/ppermute | solution.py:482
  38.4 1.3 collective-permute-start.3
  39.7 9.0 %collective-permute-done.1 = f32[1024,128]{1,0:T(8,128)S(1)} collective-permute-done((f32[1024,128]{1,0:T(8,128)S(1)}, f32[1024,128]{1,0:T(8,128)S(1)}, u32[]{:S(2)}, u32[]{:S(2)}) %collective-permute-start.1) | collective-permute-done | bytes 524320 | tf_op jit(solution)/shard_map/ppermute | solution.py:482
  48.7 0.1 broadcast_select_fusion.6
  48.8 1.3 collective-permute-done.3
  50.0 0.1 broadcast_select_fusion.3
  50.1 0.1 pad_maximum_fusion.1.own_ref
  50.2 0.1 collective-permute-start.4
  50.3 0.1 fusion.2.order_ref
  50.4 115.1 %all-reduce.8.cloned.1.call-done.corner_ref = f32[128,128]{1,0:T(8,128)} async-done(((f32[128,128]{1,0:T(8,128)}), f32[128,128]{1,0:T(8,128)}) %all-reduce.8.cloned.1.call-update) | async-done | bytes 65552 | tf_op jit(solution)/shard_map/psum | solution.py:501
  165.4 0.0 copy-start.1
  165.4 0.8 copy-done.1
  166.3 12.0 %factor_corner.1 = (f32[128,128]{1,0:T(8,128)S(1)}, bf16[128,384]{1,0:T(8,128)(2,1)S(1)}, f32[2,256,128]{2,1,0:T(8,128)S(1)}) custom-call(f32[128,128]{1,0:T(8,128)S(1)} %copy-done.1, bf16[128,192]{1,0:T(8,128)(2,1)S(1)} %fusion.2.order_ref), custom_call_target="tpu_custom_call" | custom-call | tf_op jit(solution)/shard_map/factor_corner/pallas_call | solution.py:220
  178.2 0.0 all-gather.2.cloned.1.call-done.rows_ref
  178.3 0.0 copy-start
  178.3 1.4 copy-done
  179.7 0.8 upper_rows.1
  180.5 0.0 collective-permute-done.4.other_ref
  180.5 5.1 %moved_rows.1 = (f32[64,2048]{1,0:T(8,128)}, f32[32,2048]{1,0:T(8,128)}, f32[32,2048]{1,0:T(8,128)}, f32[32,2048]{1,0:T(8,128)}) custom-call(s32[128]{0:T(128)S(1)} %get-tuple-element.177, f32[4096,2048]{1,0:T(8,128)} %get-tuple-element.163, f32[2048,128]{1,0:T(8,128)S(1)} %pad_maximum_fusion.1.own_ref, f32[2048,128]{1,0:T(8,128)S(1)} %collective-permute-done.4.other_ref, ...), custom_call_target="tpu_custom_call" | custom-call | tf_op jit(solution)/shard_map/moved_rows/pallas_call | solution.py:352
  185.6 4.7 %collective-permute-start.5 = (f32[32,2048]{1,0:T(8,128)}, f32[32,2048]{1,0:T(8,128)S(1)}, u32[]{:S(2)}, u32[]{:S(2)}) collective-permute-start(f32[32,2048]{1,0:T(8,128)} %get-tuple-element.78), channel_id=1, source_target_pairs={{0,8},{8,16},{1,9},{9,17},{2,10},{10,18},{3,11},{11,19},{4,12},{12... | collective-permute-start | bytes 786440 | tf_op jit(solution)/shard_map/ppermute | solution.py:541
  190.4 1.3 collective-permute-start.6
  191.7 1.9 collective-permute-start.7
  193.6 27.4 %trailing.1.refs_6_ = f32[4096,2048]{1,0:T(8,128)} custom-call(f32[4096,2048]{1,0:T(8,128)} %get-tuple-element.163, f32[2048,128]{1,0:T(8,128)S(1)} %pad_maximum_fusion.1.own_ref, f32[2048,128]{1,0:T(8,128)S(1)} %collective-permute-done.4.other_ref, f32[2,256,128]{2,1,0:T(8,128)S(1)} %get-tuple-element.70.weights_ref, ...), custom_call_target="tpu_custom_call" | custom-call | flops 6442450944 | bytes 67108864 | tf_op jit(solution)/shard_map/trailing/pallas_call | solution.py:391
  221.0 0.0 collective-permute-done.5.refs_1_
  221.0 0.0 collective-permute-done.6.refs_2_
  221.0 0.0 collective-permute-done.7.refs_3_
  221.0 8.2 %place_moved.1 = f32[4096,2048]{1,0:T(8,128)} custom-call(s32[1]{0:T(128)} %bitcast.3.over_ref, s32[128]{0:T(128)S(1)} %get-tuple-element.177, s32[130]{0:T(256)S(1)} %get-tuple-element.68.owned_ref, f32[64,2048]{1,0:T(8,128)} %get-tuple-element.168, f32[32,2048]{1,0:T(8,128)S(1)} %collective-permute-done.5.refs_1_, ...), custom_call_target="tpu_custom_call", output_to_operand_aliasing={{}: (9, {})} | custom-call | tf_op jit(solution)/shard_map/place_moved/pallas_call | solution.py:466
  (5 shorter events, 0.0 us)
Async XLA Ops:
  15.3 16.3 %collective-permute-start = (f32[1024,128]{1,0:T(8,128)}, f32[1024,128]{1,0:T(8,128)S(1)}, u32[]{:S(2)}, u32[]{:S(2)}) collective-permute-start(f32[1024,128]{1,0:T(8,128)} %get-tuple-element.111), channel_id=1, source_target_pairs={{0,2},{1,3},{8,10},{9,11},{16,18},{17,19},{24,26},{25,27}} | collective-permute-start | bytes 1572872 | tf_op jit(solution)/shard_map/ppermute | solution.py:482
  20.1 12.5 %collective-permute-start.2 = (f32[1024,128]{1,0:T(8,128)S(1)}, f32[1024,128]{1,0:T(8,128)}, u32[]{:S(2)}, u32[]{:S(2)}) collective-permute-start(f32[1024,128]{1,0:T(8,128)S(1)} %get-tuple-element.112), channel_id=1, source_target_pairs={{0,4},{1,5},{8,12},{9,13},{16,20},{17,21},{24,28},{25,29}} | collective-permute-start | bytes 1572872 | tf_op jit(solution)/shard_map/ppermute | solution.py:482
  23.7 141.7 %all-reduce.8.cloned.1.call-start = ((), (), s32[]{:S(2)}) async-start(), calls=%async_computation.2 | async-start | bytes 131072 | tf_op jit(solution)/shard_map/psum | solution.py:501
  24.3 153.9 %all-gather.2.cloned.1.call-start = ((), (), s32[]{:S(2)}) async-start(), calls=%async_computation.3 | async-start | bytes 1966080 | tf_op jit(solution)/shard_map/all_gather | solution.py:502
  32.8 15.9 %collective-permute-start.1 = (f32[1024,128]{1,0:T(8,128)S(1)}, f32[1024,128]{1,0:T(8,128)S(1)}, u32[]{:S(2)}, u32[]{:S(2)}) collective-permute-start(f32[1024,128]{1,0:T(8,128)S(1)} %get-tuple-element.109), channel_id=1, source_target_pairs={{0,4},{1,5},{2,6},{3,7},{8,12},{9,13},{10,14},{11,15},{16,20},{17,... | collective-permute-start | bytes 1572872 | tf_op jit(solution)/shard_map/ppermute | solution.py:482
  38.4 11.7 %collective-permute-start.3 = (f32[1024,128]{1,0:T(8,128)S(1)}, f32[1024,128]{1,0:T(8,128)S(1)}, u32[]{:S(2)}, u32[]{:S(2)}) collective-permute-start(f32[1024,128]{1,0:T(8,128)S(1)} %get-tuple-element.110), channel_id=1, source_target_pairs={{0,2},{1,3},{4,6},{5,7},{8,10},{9,11},{12,14},{13,15},{16,18},{17,... | collective-permute-start | bytes 1572872 | tf_op jit(solution)/shard_map/ppermute | solution.py:482
  50.2 130.4 %collective-permute-start.4 = (f32[2048,128]{1,0:T(8,128)S(1)}, f32[2048,128]{1,0:T(8,128)S(1)}, u32[]{:S(2)}, u32[]{:S(2)}) collective-permute-start(f32[2048,128]{1,0:T(8,128)S(1)} %pad_maximum_fusion.1.own_ref), channel_id=1, source_target_pairs={{0,1},{1,0},{2,3},{3,2},{4,5},{5,4},{6,7},{7,6},{8,9},{9,8},{10,11... | collective-permute-start | bytes 3145736 | tf_op jit(solution)/shard_map/ppermute | solution.py:513
  165.4 0.8 copy-start.1
  178.3 1.4 copy-start
  185.6 35.4 %collective-permute-start.5 = (f32[32,2048]{1,0:T(8,128)}, f32[32,2048]{1,0:T(8,128)S(1)}, u32[]{:S(2)}, u32[]{:S(2)}) collective-permute-start(f32[32,2048]{1,0:T(8,128)} %get-tuple-element.78), channel_id=1, source_target_pairs={{0,8},{8,16},{1,9},{9,17},{2,10},{10,18},{3,11},{11,19},{4,12},{12... | collective-permute-start | bytes 786440 | tf_op jit(solution)/shard_map/ppermute | solution.py:541
  190.4 30.6 %collective-permute-start.6 = (f32[32,2048]{1,0:T(8,128)}, f32[32,2048]{1,0:T(8,128)S(1)}, u32[]{:S(2)}, u32[]{:S(2)}) collective-permute-start(f32[32,2048]{1,0:T(8,128)} %get-tuple-element.79), channel_id=1, source_target_pairs={{0,16},{8,24},{1,17},{9,25},{2,18},{10,26},{3,19},{11,27},{4,20},{... | collective-permute-start | bytes 786440 | tf_op jit(solution)/shard_map/ppermute | solution.py:541
  191.7 29.3 %collective-permute-start.7 = (f32[32,2048]{1,0:T(8,128)}, f32[32,2048]{1,0:T(8,128)}, u32[]{:S(2)}, u32[]{:S(2)}) collective-permute-start(f32[32,2048]{1,0:T(8,128)} %get-tuple-element.80), channel_id=1, source_target_pairs={{0,24},{8,0},{1,25},{9,1},{2,26},{10,2},{3,27},{11,3},{4,28},{12,4... | collective-permute-start | bytes 786440 | tf_op jit(solution)/shard_map/ppermute | solution.py:541
Sparse Core Ops, SparseCore 0:
  26.7 36.9 all-gather.1
Sparse Core Ops, SparseCore 1:
  29.8 135.6 all-reduce.7

commit v3 on v2

v3 whole, which is shorter than its diff:
```python
import functools

import jax
import jax.numpy as jnp
from jax import lax
from jax.experimental import pallas as pl
from jax.experimental.pallas import tpu as pltpu
from jax.sharding import PartitionSpec as P

NB = 64
NP = 2 * NB
LANES = 128
SUB = 8
HIGHEST_PRECISION = lax.Precision.HIGHEST
MIB = 1024 * 1024


def capacities(grid_rows):
    cap = min(NP, -(-3 * NP // (2 * grid_rows * SUB)) * SUB)
    cap_top = min(NB, -(-2 * NB // (grid_rows * SUB)) * SUB)
    return cap, cap_top


def owner_of(row, grid_rows):
    return lax.rem(lax.div(row, NB), grid_rows)


def local_of(row, grid_rows):
    return lax.div(row, NB * grid_rows) * NB + lax.rem(row, NB)


def split(x):
    high = x.astype(jnp.bfloat16)
    return high, (x - high.astype(jnp.float32)).astype(jnp.bfloat16)


def mm(a, b):
    return jnp.dot(a, b, preferred_element_type=jnp.float32)


def gather_kernel(
    grid_rows, piv_ref, m_ref, _, rows_ref, corner_ref, owned_ref, *refs
):
    line_ref, head_ref, sem = refs[1:]
    my_row = lax.axis_index("row")
    my_col = lax.axis_index("col")
    cap = rows_ref.shape[0]
    head = pltpu.make_async_copy(m_ref.at[pl.ds(0, NB), pl.ds(0, LANES)], head_ref, sem.at[2])
    head.start()
    line_ref[...] = jnp.zeros_like(line_ref)
    rows_ref[...] = jnp.zeros_like(rows_ref)

    def line_copy(row, t):
        return pltpu.make_async_copy(
            m_ref.at[pl.ds(row, 1), pl.ds(0, LANES)], line_ref.at[pl.ds(t, 1), :], sem.at[0]
        )

    def row_copy(row, slot):
        return pltpu.make_async_copy(
            m_ref.at[pl.ds(row, 1), :], rows_ref.at[pl.ds(slot, 1), :], sem.at[1]
        )

    def start(t, count):
        row = piv_ref[t]
        mine = owner_of(row, grid_rows) == my_row

        @pl.when(mine)
        def _():
            owned_ref[count] = t
            line_copy(local_of(row, grid_rows), t).start()

        @pl.when(mine & (count < cap))
        def _():
            row_copy(local_of(row, grid_rows), count).start()

        return count + mine.astype(jnp.int32)

    first = lax.fori_loop(0, NB, start, jnp.int32(0))
    count = lax.fori_loop(NB, NP, start, first)
    owned_ref[NP] = first
    owned_ref[NP + 1] = count

    def wait_line(_, carry):
        line_copy(0, 0).wait()
        return carry

    def wait_row(_, carry):
        row_copy(0, 0).wait()
        return carry

    lax.fori_loop(0, count, wait_line, 0)
    head.wait()
    left = lax.broadcasted_iota(jnp.int32, (NB, LANES), 1) < NB
    corner_ref[:NB] = jnp.where(left, line_ref[:NB], pltpu.roll(line_ref[NB:], NB, 1))
    first_half = jnp.where(my_row == 0, head_ref[...], 0.0)
    second_half = jnp.where(my_row == 1, pltpu.roll(head_ref[...], NB, 1), 0.0)
    corner_ref[NB:] = jnp.where(left, first_half, second_half)
    lax.fori_loop(0, jnp.minimum(count, cap), wait_row, 0)


def gather_rows(matrix, pivots, after, cap, grid_rows):
    cols = matrix.shape[1]
    smem = pl.BlockSpec(memory_space=pltpu.SMEM)
    vmem = pl.BlockSpec(memory_space=pltpu.VMEM)
    anywhere = pl.BlockSpec(memory_space=pl.ANY)
    return pl.pallas_call(
        functools.partial(gather_kernel, grid_rows),
        out_shape=(
            jax.ShapeDtypeStruct((cap, cols), jnp.float32),
            jax.ShapeDtypeStruct((NP, LANES), jnp.float32),
            jax.ShapeDtypeStruct((NP + 2,), jnp.int32),
            jax.ShapeDtypeStruct((NP, cols), jnp.float32),
        ),
        in_specs=[smem, anywhere, anywhere],
        out_specs=(vmem, vmem, smem, anywhere),
        scratch_shapes=[
            pltpu.VMEM((NP, LANES), jnp.float32),
            pltpu.VMEM((NB, LANES), jnp.float32),
            pltpu.SemaphoreType.DMA((3,)),
        ],
        compiler_params=pltpu.CompilerParams(vmem_limit_bytes=16 * MIB),
        name="gather_rows",
    )(pivots, matrix, after)


def pack_kernel(a_ref, b_ref, c_ref, d_ref, first_ref, second_ref):
    left = lax.broadcasted_iota(jnp.int32, first_ref.shape, 1) < NB
    first_ref[...] = jnp.where(left, a_ref[...], pltpu.roll(c_ref[...], NB, 1))
    second_ref[...] = jnp.where(left, b_ref[...], pltpu.roll(d_ref[...], NB, 1))


def pack_panel(matrix):
    size = matrix.shape[0] // 4
    piece = jax.ShapeDtypeStruct((size, LANES), jnp.float32)
    return pl.pallas_call(
        pack_kernel,
        out_shape=(piece, piece),
        grid=(1,),
        in_specs=[pl.BlockSpec((size, LANES), lambda i, k=k: (k, 0)) for k in range(4)],
        out_specs=(pl.BlockSpec((size, LANES), lambda i: (0, 0)),) * 2,
        compiler_params=pltpu.CompilerParams(vmem_limit_bytes=16 * MIB),
        name="pack_panel",
    )(matrix, matrix, matrix, matrix)


def top_kernel(grid_rows, piv_ref, m_ref, _, *refs):
    out_refs = refs[:grid_rows]
    count_ref, sem = refs[grid_rows:]
    my_row = lax.axis_index("row")
    cap_top = out_refs[0].shape[0]
    for r in range(grid_rows):
        count_ref[r] = 0

    def row_copy(k, out_ref, slot):
        return pltpu.make_async_copy(m_ref.at[pl.ds(k, 1), :], out_ref.at[pl.ds(slot, 1), :], sem)

    def start(k, total):
        owner = owner_of(piv_ref[my_row * NB + k], grid_rows)
        slot = count_ref[owner]
        count_ref[owner] = slot + 1
        ahead = lax.rem(owner - my_row + grid_rows, grid_rows)
        for s in range(grid_rows):

            @pl.when((ahead == s) & (slot < cap_top))
            def _(s=s):
                row_copy(k, out_refs[s], slot).start()

        return total + (slot < cap_top).astype(jnp.int32)

    def wait(_, carry):
        row_copy(0, out_refs[0], 0).wait()
        return carry

    @pl.when(my_row < 2)
    def _():
        total = lax.fori_loop(0, NB, start, jnp.int32(0))
        lax.fori_loop(0, total, wait, 0)


def top_rows(matrix, pivots, after, cap_top, grid_rows):
    cols = matrix.shape[1]
    smem = pl.BlockSpec(memory_space=pltpu.SMEM)
    vmem = pl.BlockSpec(memory_space=pltpu.VMEM)
    anywhere = pl.BlockSpec(memory_space=pl.ANY)
    return pl.pallas_call(
        functools.partial(top_kernel, grid_rows),
        out_shape=(jax.ShapeDtypeStruct((cap_top, cols), jnp.float32),) * grid_rows,
        in_specs=[smem, anywhere, anywhere],
        out_specs=(vmem,) * grid_rows,
        scratch_shapes=[pltpu.SMEM((grid_rows,), jnp.int32), pltpu.SemaphoreType.DMA(())],
        compiler_params=pltpu.CompilerParams(vmem_limit_bytes=16 * MIB),
        name="top_rows",
    )(pivots, matrix, after)


GROUP = 4


def eliminate_in_place(work, lane, sub):
    count = len(work)
    work = list(work)
    shape = work[0].shape
    for first in range(0, NP, GROUP):
        block, inner = divmod(first, SUB)
        below = list(range(block, count))
        cols = [
            {i: jnp.broadcast_to(work[i][:, first + j : first + j + 1], shape) for i in below}
            for j in range(GROUP)
        ]
        rows = [
            jnp.broadcast_to(work[block][inner + j : inner + j + 1, :], shape)
            for j in range(GROUP)
        ]
        spots = [
            [jnp.broadcast_to(cols[j][block][inner + i : inner + i + 1, :], shape) for j in range(GROUP)]
            for i in range(GROUP)
        ]
        scaled = []
        for j in range(GROUP):
            weight = 1.0 / spots[j][j]
            at_j = lane == first + j
            line = jnp.where(at_j, 1.0, rows[j]) * weight
            factor = {l: spots[j][l] * weight for l in range(j + 1, GROUP)}
            for i in range(j + 1, GROUP):
                rows[i] = jnp.where(at_j, 0.0, rows[i]) - spots[i][j] * line
                for l in range(j + 1, GROUP):
                    spots[i][l] = spots[i][l] - spots[i][j] * factor[l]
            for l in range(j + 1, GROUP):
                for i in below:
                    cols[l][i] = cols[l][i] - cols[j][i] * factor[l]
            later = (lane > first + j) & (lane < first + GROUP)
            scaled.append(jnp.where(later, 0.0, line))
        in_group = (lane >= first) & (lane < first + GROUP)
        for i in below:
            updated = jnp.where(in_group, 0.0, work[i])
            for j in range(GROUP):
                updated = updated - cols[j][i] * scaled[j]
            if i == block:
                updated = jnp.where(sub < inner, work[i], updated)
                for j in range(GROUP):
                    updated = jnp.where(sub == inner + j, rows[j], updated)
            work[i] = updated
    return work


def square_of(even_part, odd_part):
    left = lax.broadcasted_iota(jnp.int32, (NB, LANES), 1) < NB
    upper = jnp.where(left, even_part, pltpu.roll(odd_part, NB, 1))
    lower = jnp.where(left, pltpu.roll(even_part, NB, 1), odd_part)
    return jnp.concatenate([upper, lower], axis=0)


def corner_kernel(mine_ref, other_ref, order_ref, _, lu_ref, linv_ref, weights_ref, moved_ref):
    my_col = lax.axis_index("col")
    odd = lax.rem(my_col, 2) == 1
    even_part = jnp.where(odd, other_ref[...], mine_ref[...])
    odd_part = jnp.where(odd, mine_ref[...], other_ref[...])
    a = square_of(even_part[:NB], odd_part[:NB])
    a_t = a.T
    lane = lax.broadcasted_iota(jnp.int32, (SUB, LANES), 1)
    sub = lax.broadcasted_iota(jnp.int32, (SUB, LANES), 0)
    blocks = range(0, NP, SUB)
    first = eliminate_in_place([a[i : i + SUB] for i in blocks], lane, sub)
    second = eliminate_in_place([a_t[i : i + SUB] for i in blocks], lane, sub)
    w1 = jnp.concatenate(first, axis=0)
    w2 = jnp.concatenate(second, axis=0)
    row = lax.broadcasted_iota(jnp.int32, (NP, NP), 0)
    col = lax.broadcasted_iota(jnp.int32, (NP, NP), 1)
    inverse_d = 1.0 / jnp.sum(jnp.where(row == col, w1, 0.0), axis=0, keepdims=True)
    order = order_ref[...]
    linv = split(jnp.where(row > col, w1, jnp.where(row == col, 1.0, 0.0)))
    linv_ref[...] = jnp.concatenate([mm(x, order).astype(jnp.bfloat16) for x in linv], axis=1)
    w2_t = w2.T
    lu = jnp.where(row <= col, w1, w2_t * inverse_d)
    lu_ref[...] = jnp.where(my_col == 1, pltpu.roll(lu, NB, 1), lu)
    uinv = jnp.where(row < col, w2_t, jnp.where(row == col, 1.0, 0.0)) * inverse_d
    moved_ref[...] = multipliers(square_of(even_part[NB:], odd_part[NB:]), uinv)
    mine = jnp.where(odd, uinv[NB:], uinv[:NB])
    other = jnp.where(odd, uinv[:NB], uinv[NB:])
    zero = jnp.zeros_like(mine)
    weights_ref[0] = jnp.concatenate([mine, zero, other, zero], axis=0)
    weights_ref[1] = jnp.concatenate([zero, mine, zero, other], axis=0)


def factor_corner(mine, other, order, after):
    vmem = pl.BlockSpec(memory_space=pltpu.VMEM)
    return pl.pallas_call(
        corner_kernel,
        out_shape=(
            jax.ShapeDtypeStruct((NP, NP), jnp.float32),
            jax.ShapeDtypeStruct((NP, 2 * order.shape[1]), jnp.bfloat16),
            jax.ShapeDtypeStruct((2, 2 * NP, NP), jnp.float32),
            jax.ShapeDtypeStruct((NP, 3 * NP), jnp.bfloat16),
        ),
        in_specs=[vmem, vmem, vmem, pl.BlockSpec(memory_space=pl.ANY)],
        out_specs=(vmem,) * 4,
        compiler_params=pltpu.CompilerParams(vmem_limit_bytes=24 * MIB),
        name="factor_corner",
    )(mine, other, order, after)


def upper_kernel(rows_ref, linv_ref, lu_ref, upper_ref, top_ref, a_ref):
    my_row = lax.axis_index("row")
    my_col = lax.axis_index("col")
    count, cols = rows_ref.shape
    width = min(cols, 512)
    linv_high = linv_ref[:, :count]
    linv_both = linv_ref[...]
    for start in range(0, cols, width):
        span = slice(start, start + width)
        high, low = split(rows_ref[:, span])
        a_ref[:, span] = mm(linv_both, jnp.concatenate([high, high], axis=0)) + mm(linv_high, low)

    @pl.when(my_row == 0)
    def _():
        top_ref[...] = a_ref[:NB]

    @pl.when(my_row != 0)
    def _():
        top_ref[...] = a_ref[NB:]

    @pl.when(my_col < 2)
    def _():
        lane = lax.broadcasted_iota(jnp.int32, (NP, LANES), 1)
        row = lax.broadcasted_iota(jnp.int32, (NP, LANES), 0)
        lu_part = jnp.where(my_row == 0, lu_ref[:NB], lu_ref[NB:])
        top_ref[:, :LANES] = jnp.where(lane[:NB] < NB, lu_part, top_ref[:, :LANES])
        unit = jnp.where(row == lane + my_col * NB, -1.0, 0.0)
        a_ref[:, :LANES] = jnp.where(lane < NB, unit, a_ref[:, :LANES])

    high, low = split(a_ref[...])
    upper_ref[:NP] = high
    upper_ref[NP : 2 * NP] = high
    upper_ref[2 * NP :] = low


def upper_rows_of(rows, linv, lu):
    cols = rows.shape[1]
    vmem = pl.BlockSpec(memory_space=pltpu.VMEM)
    return pl.pallas_call(
        upper_kernel,
        out_shape=(
            jax.ShapeDtypeStruct((3 * NP, cols), jnp.bfloat16),
            jax.ShapeDtypeStruct((NB, cols), jnp.float32),
        ),
        in_specs=[vmem] * 3,
        out_specs=(vmem, vmem),
        scratch_shapes=[pltpu.VMEM((NP, cols), jnp.float32)],
        compiler_params=pltpu.CompilerParams(vmem_limit_bytes=32 * MIB),
        name="upper_rows",
    )(rows, linv, lu)


def multipliers(panel, weights):
    p_high, p_low = split(panel)
    w_high, w_low = split(weights)
    lower = mm(p_high, w_high) + (mm(p_high, w_low) + mm(p_low, w_high))
    high, low = split(lower)
    return jnp.concatenate([high, low, high], axis=1)


def update_rows(a_ref, lower, upper_ref, out_ref, is_panel):
    rows, cols = out_ref.shape
    width = min(cols, 1024)
    lane = lax.broadcasted_iota(jnp.int32, (rows, LANES), 1)

    for start in range(0, cols, width):
        span = slice(start, start + width)
        a = a_ref[:, span]
        if start == 0:
            first = jnp.where((lane < NB) & is_panel, 0.0, a[:, :LANES])
            a = jnp.concatenate([first, a[:, LANES:]], axis=1)
        out_ref[:, span] = a - mm(lower, upper_ref[:, span])


def trailing_kernel(m_ref, own_ref, other_ref, weights_ref, upper_ref, out_ref, lower_ref):
    step = pl.program_id(0)
    rows = m_ref.shape[0]
    half = own_ref.shape[0] // rows

    def prepare(block):
        here = pl.ds(pl.multiple_of(lax.rem(block, half) * rows, rows), rows)
        panel = jnp.concatenate([own_ref[here, :], other_ref[here, :]], axis=1)
        lower_ref[lax.rem(block, 2)] = multipliers(panel, weights_ref[lax.div(block, half)])

    @pl.when(step == 0)
    def _():
        prepare(step)

    update_rows(
        m_ref, lower_ref[lax.rem(step, 2)], upper_ref, out_ref, lax.axis_index("col") < 2
    )
    prepare(jnp.minimum(step + 1, 2 * half - 1))


def trailing(matrix, own, other, weights, upper):
    rows, cols = matrix.shape
    size = min(512, rows // 2)
    vmem = pl.BlockSpec(memory_space=pltpu.VMEM)
    return pl.pallas_call(
        trailing_kernel,
        out_shape=jax.ShapeDtypeStruct((rows, cols), jnp.float32),
        grid=(rows // size,),
        in_specs=[pl.BlockSpec((size, cols), lambda i: (i, 0))] + [vmem] * 4,
        out_specs=pl.BlockSpec((size, cols), lambda i: (i, 0)),
        scratch_shapes=[pltpu.VMEM((2, size, 3 * NP), jnp.bfloat16)],
        compiler_params=pltpu.CompilerParams(vmem_limit_bytes=40 * MIB),
        cost_estimate=pl.CostEstimate(
            flops=6 * rows * cols * NP, bytes_accessed=8 * rows * cols, transcendentals=0
        ),
        name="trailing",
    )(matrix, own, other, weights, upper)


def place_kernel(grid_rows, over_ref, piv_ref, owned_ref, *refs):
    piece_refs = refs[:grid_rows]
    order_ref, moved_ref, upper_ref, all_ref, top_ref, _, out_ref, f_ref, sem = refs[grid_rows:]
    my_row = lax.axis_index("row")
    first, total = owned_ref[NP], owned_ref[NP + 1]
    over = over_ref[0] != 0
    cap_top = piece_refs[0].shape[0]

    @pl.when(my_row < 2)
    def _():
        pltpu.make_async_copy(top_ref, out_ref.at[pl.ds(0, NB), :], sem.at[0]).start()

    @pl.when(over)
    def _():
        copy = pltpu.make_async_copy(all_ref, f_ref.at[pl.ds(0, NP), :], sem.at[1])
        copy.start()
        copy.wait()

    @pl.when(~over)
    def _():
        for s in range(grid_rows):
            f_ref[pl.ds(s * cap_top, cap_top), :] = piece_refs[s][...]

    lower = mm(order_ref[...], moved_ref[...]).astype(jnp.bfloat16)
    update_rows(f_ref, lower, upper_ref, f_ref, lax.axis_index("col") < 2)

    def put(n, carry, base):
        t = owned_ref[n]
        slot = jnp.where(over, t, n + base)
        pltpu.make_async_copy(
            f_ref.at[pl.ds(slot, 1), :],
            out_ref.at[pl.ds(local_of(piv_ref[t], grid_rows), 1), :],
            sem.at[1],
        ).start()
        return carry

    for panel, low, high in ((0, jnp.int32(0), first), (1, first, total)):
        back = lax.rem(my_row - panel + grid_rows, grid_rows)
        lax.fori_loop(low, high, functools.partial(put, base=back * cap_top - low), 0)

    def wait(_, carry):
        pltpu.make_async_copy(
            f_ref.at[pl.ds(0, 1), :], out_ref.at[pl.ds(0, 1), :], sem.at[1]
        ).wait()
        return carry

    lax.fori_loop(0, total, wait, 0)

    @pl.when(my_row < 2)
    def _():
        pltpu.make_async_copy(top_ref, out_ref.at[pl.ds(0, NB), :], sem.at[0]).wait()


def place_moved(pieces, order, moved, upper, everything, top, result, pivots, owned, over):
    grid_rows = len(pieces)
    cols = result.shape[1]
    smem = pl.BlockSpec(memory_space=pltpu.SMEM)
    vmem = pl.BlockSpec(memory_space=pltpu.VMEM)
    anywhere = pl.BlockSpec(memory_space=pl.ANY)
    return pl.pallas_call(
        functools.partial(place_kernel, grid_rows),
        out_shape=jax.ShapeDtypeStruct(result.shape, result.dtype),
        in_specs=[smem] * 3 + [vmem] * (grid_rows + 3) + [anywhere] * 3,
        out_specs=anywhere,
        input_output_aliases={grid_rows + 8: 0},
        scratch_shapes=[
            pltpu.VMEM((order.shape[0], cols), jnp.float32),
            pltpu.SemaphoreType.DMA((2,)),
        ],
        compiler_params=pltpu.CompilerParams(vmem_limit_bytes=24 * MIB),
        name="place_moved",
    )(over, pivots, owned, *pieces, order, moved, upper, everything, top, result)


def merge_kernel(bits, arrived1, arrived2, held1, held2, _, out_ref):
    chip = lax.div(lax.axis_index("col"), 2)
    size = held1.shape[0]
    for k, (bit, arrived, held) in enumerate(zip(bits, (arrived1, arrived2), (held1, held2))):
        here = pl.ds(k * size, size)
        came = (chip & bit) != 0

        @pl.when(came)
        def _(arrived=arrived, here=here):
            out_ref[here, :] = arrived[...]

        @pl.when(~came)
        def _(held=held, here=here):
            out_ref[here, :] = held[...]


def merge(bits, arrived, held, after):
    size = held[0].shape[0]
    vmem = pl.BlockSpec(memory_space=pltpu.VMEM)
    return pl.pallas_call(
        functools.partial(merge_kernel, bits),
        out_shape=jax.ShapeDtypeStruct((2 * size, LANES), jnp.float32),
        in_specs=[vmem] * 4 + [pl.BlockSpec(memory_space=pl.ANY)],
        out_specs=vmem,
        compiler_params=pltpu.CompilerParams(vmem_limit_bytes=16 * MIB),
        name="merge",
    )(*arrived, *held, after)


def spread_round(value, bit, reached):
    pairs = [(2 * c + k, 2 * (c | bit) + k) for c in reached for k in range(2)]
    return lax.ppermute(value, "col", pairs)


def shards(matrix, pivots):
    grid_rows = lax.axis_size("row")
    grid_cols = lax.axis_size("col")
    chips = grid_cols // 2
    assert grid_rows > 1 and chips * 2 == grid_cols and not chips & (chips - 1)
    my_row = lax.axis_index("row")
    my_chip = lax.axis_index("col") // 2
    cap, cap_top = capacities(grid_rows)
    flat = pivots.reshape(-1)
    swap = [(c, c ^ 1) for c in range(grid_cols)]
    bits = [1 << b for b in range(chips.bit_length() - 1)]

    halves = pack_panel(matrix)
    rows, corner, owned, unwritten = gather_rows(matrix, flat, halves[0], cap, grid_rows)
    all_rows = lax.all_gather(rows, "row", tiled=True)

    shifts = [[(r, (r + s) % grid_rows) for r in range(grid_rows)] for s in range(1, grid_rows)]
    corner = corner + sum(lax.ppermute(corner, "row", shift) for shift in shifts)
    corner = jnp.where(my_chip == 0, corner, 0.0) + sum(
        lax.ppermute(corner, "col", [(0, 2 * chip), (1, 2 * chip + 1)]) for chip in range(1, chips)
    )
    corner_other = lax.ppermute(corner, "col", swap)

    owner = owner_of(flat, grid_rows)
    number = jnp.arange(NP, dtype=jnp.int32)
    panel = number // NB
    same = owner[:, None] == owner[None, :]
    alike = same & (panel[None, :] == panel[:, None])
    before = number[None, :] < number[:, None]
    rank = jnp.sum(same & before, axis=1, dtype=jnp.int32)
    panel_rank = jnp.sum(alike & before, axis=1, dtype=jnp.int32)
    over = jnp.max(jnp.maximum(rank - cap, panel_rank - cap_top)) >= 0
    position = jnp.where(over, number, owner * cap + rank)
    order = position[:, None] == jnp.arange(grid_rows * cap, dtype=jnp.int32)[None, :]
    order = order.astype(jnp.bfloat16)
    back = (my_row - panel + grid_rows) % grid_rows
    slot = jnp.where(over, number, back * cap_top + panel_rank)
    slots = jnp.arange(grid_rows * cap_top, dtype=jnp.int32)
    order_top = (slot[None, :] == slots[:, None]) & (owner == my_row)[None, :]
    order_top = order_top.astype(jnp.bfloat16)
    over = over.astype(jnp.int32)
    over_list = over.reshape(1)

    quarter = halves[0].shape[0]
    held = halves
    reached = ([0], [0])
    for step, both in enumerate(zip(bits, bits[::-1])):
        arrived = [spread_round(v, bit, r) for v, bit, r in zip(held, both, reached)]
        reached = [r + [c | bit for c in r] for bit, r in zip(both, reached)]
        if step + 1 == len(bits):
            lu, linv, weights, moved = factor_corner(corner, corner_other, order, held[0])
        own = merge(both, arrived, held, corner if step + 1 < len(bits) else lu)
        held = (own[:quarter], own[quarter:])
    other = lax.ppermute(own, "col", swap)

    tops = top_rows(matrix, flat, lu, cap_top, grid_rows)
    pieces = [tops[0]]
    for s in range(1, grid_rows):
        pairs = [(c, (c + s) % grid_rows) for c in range(2)]
        pieces.append(lax.ppermute(tops[s], "row", pairs))
    def sum_rows(state):
        mine = owner == my_row
        local = jnp.where(mine, local_of(flat, grid_rows), 0)
        picked = jnp.where(mine[:, None], matrix[local], 0.0)
        tops = jnp.where((panel == my_row)[:, None], matrix[number % NB], 0.0)
        picked, tops = lax.psum((picked, tops), "row")
        return jnp.int32(0), jnp.zeros_like(state[1]).at[:NP].set(picked), tops

    _, all_rows, summed_tops = lax.while_loop(
        lambda state: state[0] > 0, sum_rows, (over, all_rows, unwritten)
    )

    upper, top = upper_rows_of(all_rows, linv, lu)
    result = trailing(matrix, own, other, weights, upper)
    return place_moved(
        pieces, order_top, moved, upper, summed_tops, top, result, flat, owned, over_list
    )


def solution(mesh):
    placed = (P("row", "col"), P())
    return jax.shard_map(
        shards, mesh=mesh, in_specs=placed, out_specs=P("row", "col"), check_vma=False
    )
```

time: 239 us -> 124 us (0.52)
  waiting for transfers between devices: 134 us -> 7.67 us
  local copies, waits for them, and re-layouts: 3.88 us -> 13.8 us
  starting transfers between devices: 22 us -> 29.7 us
  Pallas kernels: 59.6 us -> 55.9 us
    psum x1 -> x0, waiting for transfers between devices: 115 us -> none  [shards(): all_corner = lax.psum(corner, ('row', 'col'))]
    unnamed x4 -> x20, local copies, waits for them, and re-layouts: 2.24 us -> 13 us
    ppermute x7 -> x14, waiting for transfers between devices: 17.8 us -> 7.63 us  [the longest x3 3.34 us: shards(): lax.ppermute(corner, 'col', [(0, 2 * chip), (1, 2 * chip + 1)])]
    ppermute x7 -> x14, starting transfers between devices: 21.8 us -> 29.6 us  [the longest x4 12 us: spread_round(): return lax.ppermute(value, 'col', pairs)]
    pallas_call x1, Pallas kernels: 8.15 us -> 2.68 us  [place_moved(): pl.pallas_call(functools.partial(place_kernel, grid_rows), out_shape=jax....]
    pallas_call x2 -> x4, Pallas kernels: 6.86 us -> 6.05 us  [the longest x1 3.87 us: top_rows(): pl.pallas_call(functools.partial(top_kernel, grid_rows), out_shape=(jax.S...]
  transfers between devices with their start and end apart: 10 -> 16, of which waited for: 5 -> 4; matrix products, arithmetic and copies ran while one was open for 1% -> 1% of each run, Pallas kernels for 17% -> 37%
where the time goes in v3:
time: 124 us; the launch traced here: 123 us
  Pallas kernels  55.9 us (45%)
  starting transfers between devices  29.7 us (24%)
  between operations  14.4 us (12%)
  local copies, waits for them, and re-layouts  13.8 us (11%)
  waiting for transfers between devices  7.67 us (6%)
    pallas_call x1, Pallas kernels, trailing(): pl.pallas_call(trailing_kernel, out_shape=jax.ShapeDtypeStruct((rows, col...  27.5 us
    unnamed x20, local copies, waits for them, and re-layouts  13 us
    pallas_call x1, Pallas kernels, factor_corner(): pl.pallas_call(corner_kernel, out_shape=(jax.ShapeDtypeStruct((NP, NP), j...  12.1 us
    ppermute x4, starting transfers between devices, spread_round(): return lax.ppermute(value, 'col', pairs)  12 us
    ppermute x3, starting transfers between devices, shards(): pieces.append(lax.ppermute(tops[s], 'row', pairs))  9.06 us
    pallas_call x1, Pallas kernels, gather_rows(): pl.pallas_call(functools.partial(gather_kernel, grid_rows), out_shape=(ja...  5.38 us
    ppermute x3, starting transfers between devices, shards(): lax.ppermute(corner, 'row', shift)  4.66 us
    ppermute x3, starting transfers between devices, shards(): lax.ppermute(corner, 'col', [(0, 2 * chip), (1, 2 * chip + 1)])  3.88 us
  transfers between devices with their start and end apart: 16, of which 4 were waited for; matrix products, arithmetic and copies ran while one was open for 1% of the time, Pallas kernels for 37%

profile of v3, /device:TPU:0, one launch (start us, length us, event | category | flops | bytes accessed | tf_op | source)
XLA Modules:
  0.0 122.7 jit_solution(13290070782699011976)
XLA Ops:
  6.5 0.8 reshape.262.piv_ref
  7.3 2.0 %pack_panel.1 = (f32[1024,128]{1,0:T(8,128)S(1)}, f32[1024,128]{1,0:T(8,128)S(1)}) custom-call(f32[4096,2048]{1,0:T(8,128)} %m_ref.5, f32[4096,2048]{1,0:T(8,128)} %m_ref.5, f32[4096,2048]{1,0:T(8,128)} %m_ref.5, f32[4096,2048]{1,0:T(8,128)} %m_ref.5), custom_call_target="tpu_custom_call" | custom-call | tf_op jit(solution)/shard_map/pack_panel/pallas_call | solution.py:135
  9.3 9.2 %copy-done.8 = f32[4096,2048]{1,0:T(8,128)S(1)} copy-done((f32[4096,2048]{1,0:T(8,128)S(1)}, f32[4096,2048]{1,0:T(8,128)}, u32[]{:S(2)}) %copy-start.8) | copy-done | bytes 33554456
  18.5 5.4 %gather_rows.1 = (f32[48,2048]{1,0:T(8,128)}, f32[128,128]{1,0:T(8,128)S(1)}, s32[130]{0:T(256)S(1)}, f32[128,2048]{1,0:T(8,128)}) custom-call(s32[128]{0:T(128)S(1)} %reshape.262.piv_ref, f32[4096,2048]{1,0:T(8,128)S(1)} %copy-done.8, f32[1024,128]{1,0:T(8,128)S(1)} %get-tuple-element.78._.held1), custom_call_target="tpu_custom_call" | custom-call | tf_op jit(solution)/shard_map/gather_rows/pallas_call | solution.py:106
  23.9 0.0 all-gather.2.cloned.1.call-update
  23.9 4.9 %collective-permute-start.7 = (f32[1024,128]{1,0:T(8,128)S(1)}, f32[1024,128]{1,0:T(8,128)S(1)}, u32[]{:S(2)}, u32[]{:S(2)}) collective-permute-start(f32[1024,128]{1,0:T(8,128)S(1)} %get-tuple-element.78._.held1), channel_id=1, source_target_pairs={{0,2},{1,3},{8,10},{9,11},{16,18},{17,19},{24,26},{25,27}} | collective-permute-start | bytes 1572872 | tf_op jit(solution)/shard_map/ppermute | solution.py:520
  28.8 3.9 %collective-permute-start.2 = (f32[128,128]{1,0:T(8,128)S(1)}, f32[128,128]{1,0:T(8,128)S(1)}, u32[]{:S(2)}, u32[]{:S(2)}) collective-permute-start(f32[128,128]{1,0:T(8,128)S(1)} %get-tuple-element.80), channel_id=1, source_target_pairs={{0,24},{8,0},{16,8},{24,16},{1,25},{9,1},{17,9},{25,17},{2,26},{10... | collective-permute-start | bytes 196616 | tf_op jit(solution)/shard_map/ppermute | solution.py:540
  32.7 0.0 collective-permute-start.1
  32.7 0.7 collective-permute-start
  33.5 1.3 %collective-permute-start.8 = (f32[1024,128]{1,0:T(8,128)S(1)}, f32[1024,128]{1,0:T(8,128)S(1)}, u32[]{:S(2)}, u32[]{:S(2)}) collective-permute-start(f32[1024,128]{1,0:T(8,128)S(1)} %get-tuple-element.81.held2), channel_id=1, source_target_pairs={{0,4},{1,5},{8,12},{9,13},{16,20},{17,21},{24,28},{25,29}} | collective-permute-start | bytes 1572872 | tf_op jit(solution)/shard_map/ppermute | solution.py:520
  34.8 0.2 convert_reduce_fusion.1
  35.0 0.6 maximum_reduce_fusion
  36.3 1.8 %collective-permute-done.1 = f32[128,128]{1,0:T(8,128)S(1)} collective-permute-done((f32[128,128]{1,0:T(8,128)S(1)}, f32[128,128]{1,0:T(8,128)S(1)}, u32[]{:S(2)}, u32[]{:S(2)}) %collective-permute-start.1) | collective-permute-done | bytes 65568 | tf_op jit(solution)/shard_map/ppermute | solution.py:540
  38.1 1.2 %collective-permute-done = f32[128,128]{1,0:T(8,128)S(1)} collective-permute-done((f32[128,128]{1,0:T(8,128)S(1)}, f32[128,128]{1,0:T(8,128)S(1)}, u32[]{:S(2)}, u32[]{:S(2)}) %collective-permute-start) | collective-permute-done | bytes 65568 | tf_op jit(solution)/shard_map/ppermute | solution.py:540
  39.4 1.3 %collective-permute-start.5 = (f32[128,128]{1,0:T(8,128)S(1)}, f32[128,128]{1,0:T(8,128)S(1)}, u32[]{:S(2)}, u32[]{:S(2)}) collective-permute-start(f32[128,128]{1,0:T(8,128)S(1)} %add_add_fusion.1), channel_id=1, source_target_pairs={{0,6},{1,7},{8,14},{9,15},{16,22},{17,23},{24,30},{25,31}} | collective-permute-start | bytes 196616 | tf_op jit(solution)/shard_map/ppermute | solution.py:542
  40.7 1.3 %collective-permute-start.4 = (f32[128,128]{1,0:T(8,128)S(1)}, f32[128,128]{1,0:T(8,128)S(1)}, u32[]{:S(2)}, u32[]{:S(2)}) collective-permute-start(f32[128,128]{1,0:T(8,128)S(1)} %add_add_fusion.1), channel_id=1, source_target_pairs={{0,4},{1,5},{8,12},{9,13},{16,20},{17,21},{24,28},{25,29}} | collective-permute-start | bytes 196616 | tf_op jit(solution)/shard_map/ppermute | solution.py:542
  42.0 1.3 %collective-permute-start.3 = (f32[128,128]{1,0:T(8,128)S(1)}, f32[128,128]{1,0:T(8,128)S(1)}, u32[]{:S(2)}, u32[]{:S(2)}) collective-permute-start(f32[128,128]{1,0:T(8,128)S(1)} %add_add_fusion.1), channel_id=1, source_target_pairs={{0,2},{1,3},{8,10},{9,11},{16,18},{17,19},{24,26},{25,27}} | collective-permute-start | bytes 196616 | tf_op jit(solution)/shard_map/ppermute | solution.py:542
  43.3 0.0 collective-permute-done.5
  43.3 3.3 %collective-permute-done.4 = f32[128,128]{1,0:T(8,128)S(1)} collective-permute-done((f32[128,128]{1,0:T(8,128)S(1)}, f32[128,128]{1,0:T(8,128)S(1)}, u32[]{:S(2)}, u32[]{:S(2)}) %collective-permute-start.4) | collective-permute-done | bytes 65568 | tf_op jit(solution)/shard_map/ppermute | solution.py:542
  46.7 0.0 collective-permute-done.7.arrived1
  46.7 0.1 merge.2
  46.8 0.1 fusion.17
  46.9 2.8 %collective-permute-start.13 = (f32[1024,128]{1,0:T(8,128)S(1)}, f32[1024,128]{1,0:T(8,128)S(1)}, u32[]{:S(2)}, u32[]{:S(2)}) collective-permute-start(f32[1024,128]{1,0:T(8,128)S(1)} %get-tuple-element.133.held2), channel_id=1, source_target_pairs={{0,2},{1,3},{4,6},{5,7},{8,10},{9,11},{12,14},{13,15},{16,18},{17,... | collective-permute-start | bytes 1572872 | tf_op jit(solution)/shard_map/ppermute | solution.py:520
  49.7 2.9 %collective-permute-start.12 = (f32[1024,128]{1,0:T(8,128)S(1)}, f32[1024,128]{1,0:T(8,128)S(1)}, u32[]{:S(2)}, u32[]{:S(2)}) collective-permute-start(f32[1024,128]{1,0:T(8,128)S(1)} %get-tuple-element.134._.held1), channel_id=1, source_target_pairs={{0,4},{1,5},{2,6},{3,7},{8,12},{9,13},{10,14},{11,15},{16,20},{17,... | collective-permute-start | bytes 1572872 | tf_op jit(solution)/shard_map/ppermute | solution.py:520
  52.7 0.1 fusion.8.order_ref
  52.8 0.1 collective-permute-start.6
  52.9 1.2 collective-permute-done.6.other_ref
  54.1 12.1 %factor_corner.1 = (f32[128,128]{1,0:T(8,128)S(1)}, bf16[128,384]{1,0:T(8,128)(2,1)S(1)}, f32[2,256,128]{2,1,0:T(8,128)S(1)}, bf16[128,384]{1,0:T(8,128)(2,1)S(1)}) custom-call(f32[128,128]{1,0:T(8,128)S(1)} %add_add_fusion._.mine_ref, f32[128,128]{1,0:T(8,128)S(1)} %collective-permute-done.6.other_ref, bf16[128,192]{1,0:T(8,128)(2,1)S(1)} %fusion.8.order_ref, ...), custom_call_target="tpu_custom_call" | custom-call | tf_op jit(solution)/shard_map/factor_corner/pallas_call | solution.py:287
  66.2 0.6 copy-done.4
  66.9 0.6 copy-done.6
  67.5 3.9 %top_rows.1 = (f32[32,2048]{1,0:T(8,128)S(1)}, f32[32,2048]{1,0:T(8,128)}, f32[32,2048]{1,0:T(8,128)}, f32[32,2048]{1,0:T(8,128)}) custom-call(s32[128]{0:T(128)S(1)} %reshape.262.piv_ref, f32[4096,2048]{1,0:T(8,128)} %m_ref.5, f32[128,128]{1,0:T(8,128)S(1)} %get-tuple-element.82._.lu_ref), custom_call_target="tpu_custom_call" | custom-call | tf_op jit(solution)/shard_map/top_rows/pallas_call | solution.py:185
  71.4 5.2 %collective-permute-start.9 = (f32[32,2048]{1,0:T(8,128)}, f32[32,2048]{1,0:T(8,128)}, u32[]{:S(2)}, u32[]{:S(2)}) collective-permute-start(f32[32,2048]{1,0:T(8,128)} %get-tuple-element.84), channel_id=1, source_target_pairs={{0,8},{8,16},{1,9},{9,17},{2,10},{10,18},{3,11},{11,19},{4,12},{12... | collective-permute-start | bytes 786440 | tf_op jit(solution)/shard_map/ppermute | solution.py:582
  76.6 2.0 %collective-permute-start.10 = (f32[32,2048]{1,0:T(8,128)}, f32[32,2048]{1,0:T(8,128)}, u32[]{:S(2)}, u32[]{:S(2)}) collective-permute-start(f32[32,2048]{1,0:T(8,128)} %get-tuple-element.85), channel_id=1, source_target_pairs={{0,16},{8,24},{1,17},{9,25},{2,18},{10,26},{3,19},{11,27},{4,20},{... | collective-permute-start | bytes 786440 | tf_op jit(solution)/shard_map/ppermute | solution.py:582
  78.6 1.9 %collective-permute-start.11 = (f32[32,2048]{1,0:T(8,128)}, f32[32,2048]{1,0:T(8,128)}, u32[]{:S(2)}, u32[]{:S(2)}) collective-permute-start(f32[32,2048]{1,0:T(8,128)} %get-tuple-element.86), channel_id=1, source_target_pairs={{0,24},{8,0},{1,25},{9,1},{2,26},{10,2},{3,27},{11,3},{4,28},{12,4... | collective-permute-start | bytes 786440 | tf_op jit(solution)/shard_map/ppermute | solution.py:582
  80.5 0.0 collective-permute-done.13.arrived2
  80.5 0.0 collective-permute-done.12.arrived1
  80.5 0.0 copy-start
  80.5 0.8 copy-done
  81.3 1.0 copy-done.1
  82.4 0.1 merge.3.own_ref
  82.4 0.1 collective-permute-start.14
  82.5 0.0 all-gather.2.cloned.1.call-done
  82.6 0.2 while.13
  82.8 0.7 copy-done.7
  83.4 2.2 %upper_rows.1 = (bf16[384,2048]{1,0:T(8,128)(2,1)S(1)}, f32[64,2048]{1,0:T(8,128)S(1)}) custom-call(f32[192,2048]{1,0:T(8,128)} %get-tuple-element.90.rows_ref, bf16[128,384]{1,0:T(8,128)(2,1)S(1)} %copy-done.7, f32[128,128]{1,0:T(8,128)S(1)} %get-tuple-element.82._.lu_ref), custom_call_target="tpu_custom_call" | custom-call | tf_op jit(solution)/shard_map/upper_rows/pallas_call | solution.py:340
  85.7 0.0 collective-permute-done.14.other_ref
  85.7 27.5 %trailing.1.refs_9_ = f32[4096,2048]{1,0:T(8,128)} custom-call(f32[4096,2048]{1,0:T(8,128)} %get-tuple-element.183, f32[2048,128]{1,0:T(8,128)S(1)} %merge.3.own_ref, f32[2048,128]{1,0:T(8,128)S(1)} %collective-permute-done.14.other_ref, f32[2,256,128]{2,1,0:T(8,128)S(1)} %copy-done.3, bf16[384,2048]{1,0:T(8,128)(2,1)S(1)} %get-tuple-element.92.upper_ref.refs_6_), custom_call_target="tpu_custom_call" | custom-call | flops 6442450944 | bytes 67108864 | tf_op jit(solution)/shard_map/trailing/pallas_call | solution.py:400
  113.2 2.7 %place_moved.1 = f32[4096,2048]{1,0:T(8,128)} custom-call(s32[1]{0:T(128)} %bitcast.over_ref, s32[128]{0:T(128)S(1)} %get-tuple-element.200, s32[130]{0:T(256)S(1)} %get-tuple-element.79.owned_ref, f32[32,2048]{1,0:T(8,128)S(1)} %get-tuple-element.83.refs_0_, f32[32,2048]{1,0:T(8,128)} %collective-permute-done.9.refs_1_, ...), custom_call_target="tpu_custom_call", output_to_operand_aliasing={{}: (12, {})} | custom-call | tf_op jit(solution)/shard_map/place_moved/pallas_call | solution.py:474
  (27 shorter events, 0.1 us)
Async XLA Ops:
  6.5 76.0 %all-gather.2.cloned.1.call-start = ((), (), s32[]{:S(2)}) async-start(), calls=%async_computation | async-start | bytes 1966080 | tf_op jit(solution)/shard_map/all_gather | solution.py:537
  7.3 11.2 %copy-start.8 = (f32[4096,2048]{1,0:T(8,128)S(1)}, f32[4096,2048]{1,0:T(8,128)}, u32[]{:S(2)}) copy-start(f32[4096,2048]{1,0:T(8,128)} %m_ref.5) | copy-start | bytes 100663296
  23.9 22.8 %collective-permute-start.7 = (f32[1024,128]{1,0:T(8,128)S(1)}, f32[1024,128]{1,0:T(8,128)S(1)}, u32[]{:S(2)}, u32[]{:S(2)}) collective-permute-start(f32[1024,128]{1,0:T(8,128)S(1)} %get-tuple-element.78._.held1), channel_id=1, source_target_pairs={{0,2},{1,3},{8,10},{9,11},{16,18},{17,19},{24,26},{25,27}} | collective-permute-start | bytes 1572872 | tf_op jit(solution)/shard_map/ppermute | solution.py:520
  28.8 7.5 %collective-permute-start.2 = (f32[128,128]{1,0:T(8,128)S(1)}, f32[128,128]{1,0:T(8,128)S(1)}, u32[]{:S(2)}, u32[]{:S(2)}) collective-permute-start(f32[128,128]{1,0:T(8,128)S(1)} %get-tuple-element.80), channel_id=1, source_target_pairs={{0,24},{8,0},{16,8},{24,16},{1,25},{9,1},{17,9},{25,17},{2,26},{10... | collective-permute-start | bytes 196616 | tf_op jit(solution)/shard_map/ppermute | solution.py:540
  32.7 5.4 %collective-permute-start.1 = (f32[128,128]{1,0:T(8,128)S(1)}, f32[128,128]{1,0:T(8,128)S(1)}, u32[]{:S(2)}, u32[]{:S(2)}) collective-permute-start(f32[128,128]{1,0:T(8,128)S(1)} %get-tuple-element.80), channel_id=1, source_target_pairs={{0,16},{8,24},{16,0},{24,8},{1,17},{9,25},{17,1},{25,9},{2,18},{10... | collective-permute-start | bytes 196616 | tf_op jit(solution)/shard_map/ppermute | solution.py:540
  32.7 6.6 %collective-permute-start = (f32[128,128]{1,0:T(8,128)S(1)}, f32[128,128]{1,0:T(8,128)S(1)}, u32[]{:S(2)}, u32[]{:S(2)}) collective-permute-start(f32[128,128]{1,0:T(8,128)S(1)} %get-tuple-element.80), channel_id=1, source_target_pairs={{0,8},{8,16},{16,24},{24,0},{1,9},{9,17},{17,25},{25,1},{2,10},{10... | collective-permute-start | bytes 196616 | tf_op jit(solution)/shard_map/ppermute | solution.py:540
  33.5 13.2 %collective-permute-start.8 = (f32[1024,128]{1,0:T(8,128)S(1)}, f32[1024,128]{1,0:T(8,128)S(1)}, u32[]{:S(2)}, u32[]{:S(2)}) collective-permute-start(f32[1024,128]{1,0:T(8,128)S(1)} %get-tuple-element.81.held2), channel_id=1, source_target_pairs={{0,4},{1,5},{8,12},{9,13},{16,20},{17,21},{24,28},{25,29}} | collective-permute-start | bytes 1572872 | tf_op jit(solution)/shard_map/ppermute | solution.py:520
  39.4 3.9 %collective-permute-start.5 = (f32[128,128]{1,0:T(8,128)S(1)}, f32[128,128]{1,0:T(8,128)S(1)}, u32[]{:S(2)}, u32[]{:S(2)}) collective-permute-start(f32[128,128]{1,0:T(8,128)S(1)} %add_add_fusion.1), channel_id=1, source_target_pairs={{0,6},{1,7},{8,14},{9,15},{16,22},{17,23},{24,30},{25,31}} | collective-permute-start | bytes 196616 | tf_op jit(solution)/shard_map/ppermute | solution.py:542
  40.7 6.0 %collective-permute-start.4 = (f32[128,128]{1,0:T(8,128)S(1)}, f32[128,128]{1,0:T(8,128)S(1)}, u32[]{:S(2)}, u32[]{:S(2)}) collective-permute-start(f32[128,128]{1,0:T(8,128)S(1)} %add_add_fusion.1), channel_id=1, source_target_pairs={{0,4},{1,5},{8,12},{9,13},{16,20},{17,21},{24,28},{25,29}} | collective-permute-start | bytes 196616 | tf_op jit(solution)/shard_map/ppermute | solution.py:542
  42.0 4.7 %collective-permute-start.3 = (f32[128,128]{1,0:T(8,128)S(1)}, f32[128,128]{1,0:T(8,128)S(1)}, u32[]{:S(2)}, u32[]{:S(2)}) collective-permute-start(f32[128,128]{1,0:T(8,128)S(1)} %add_add_fusion.1), channel_id=1, source_target_pairs={{0,2},{1,3},{8,10},{9,11},{16,18},{17,19},{24,26},{25,27}} | collective-permute-start | bytes 196616 | tf_op jit(solution)/shard_map/ppermute | solution.py:542
  46.9 33.6 %collective-permute-start.13 = (f32[1024,128]{1,0:T(8,128)S(1)}, f32[1024,128]{1,0:T(8,128)S(1)}, u32[]{:S(2)}, u32[]{:S(2)}) collective-permute-start(f32[1024,128]{1,0:T(8,128)S(1)} %get-tuple-element.133.held2), channel_id=1, source_target_pairs={{0,2},{1,3},{4,6},{5,7},{8,10},{9,11},{12,14},{13,15},{16,18},{17,... | collective-permute-start | bytes 1572872 | tf_op jit(solution)/shard_map/ppermute | solution.py:520
  49.7 30.8 %collective-permute-start.12 = (f32[1024,128]{1,0:T(8,128)S(1)}, f32[1024,128]{1,0:T(8,128)S(1)}, u32[]{:S(2)}, u32[]{:S(2)}) collective-permute-start(f32[1024,128]{1,0:T(8,128)S(1)} %get-tuple-element.134._.held1), channel_id=1, source_target_pairs={{0,4},{1,5},{2,6},{3,7},{8,12},{9,13},{10,14},{11,15},{16,20},{17,... | collective-permute-start | bytes 1572872 | tf_op jit(solution)/shard_map/ppermute | solution.py:520
  52.8 1.3 %collective-permute-start.6 = (f32[128,128]{1,0:T(8,128)S(1)}, f32[128,128]{1,0:T(8,128)S(1)}, u32[]{:S(2)}, u32[]{:S(2)}) collective-permute-start(f32[128,128]{1,0:T(8,128)S(1)} %add_add_fusion._.mine_ref), channel_id=1, source_target_pairs={{0,1},{1,0},{2,3},{3,2},{4,5},{5,4},{6,7},{7,6},{8,9},{9,8},{10,11... | collective-permute-start | bytes 196616 | tf_op jit(solution)/shard_map/ppermute | solution.py:544
  66.2 0.7 copy-start.4
  66.9 0.7 copy-start.6
  67.5 3.9 %copy-start.2 = (f32[2,256,128]{2,1,0:T(8,128)}, f32[2,256,128]{2,1,0:T(8,128)S(1)}, u32[]{:S(2)}) copy-start(f32[2,256,128]{2,1,0:T(8,128)S(1)} %get-tuple-element.95.weights_ref) | copy-start | bytes 786436
  71.4 41.7 %collective-permute-start.9 = (f32[32,2048]{1,0:T(8,128)}, f32[32,2048]{1,0:T(8,128)}, u32[]{:S(2)}, u32[]{:S(2)}) collective-permute-start(f32[32,2048]{1,0:T(8,128)} %get-tuple-element.84), channel_id=1, source_target_pairs={{0,8},{8,16},{1,9},{9,17},{2,10},{10,18},{3,11},{11,19},{4,12},{12... | collective-permute-start | bytes 786440 | tf_op jit(solution)/shard_map/ppermute | solution.py:582
  76.6 36.6 %collective-permute-start.10 = (f32[32,2048]{1,0:T(8,128)}, f32[32,2048]{1,0:T(8,128)}, u32[]{:S(2)}, u32[]{:S(2)}) collective-permute-start(f32[32,2048]{1,0:T(8,128)} %get-tuple-element.85), channel_id=1, source_target_pairs={{0,16},{8,24},{1,17},{9,25},{2,18},{10,26},{3,19},{11,27},{4,20},{... | collective-permute-start | bytes 786440 | tf_op jit(solution)/shard_map/ppermute | solution.py:582
  78.6 34.6 %collective-permute-start.11 = (f32[32,2048]{1,0:T(8,128)}, f32[32,2048]{1,0:T(8,128)}, u32[]{:S(2)}, u32[]{:S(2)}) collective-permute-start(f32[32,2048]{1,0:T(8,128)} %get-tuple-element.86), channel_id=1, source_target_pairs={{0,24},{8,0},{1,25},{9,1},{2,26},{10,2},{3,27},{11,3},{4,28},{12,4... | collective-permute-start | bytes 786440 | tf_op jit(solution)/shard_map/ppermute | solution.py:582
  80.5 0.8 copy-start
  81.3 1.0 copy-start.1
  82.4 3.2 %collective-permute-start.14 = (f32[2048,128]{1,0:T(8,128)S(1)}, f32[2048,128]{1,0:T(8,128)S(1)}, u32[]{:S(2)}, u32[]{:S(2)}) collective-permute-start(f32[2048,128]{1,0:T(8,128)S(1)} %merge.3.own_ref), channel_id=1, source_target_pairs={{0,1},{1,0},{2,3},{3,2},{4,5},{5,4},{6,7},{7,6},{8,9},{9,8},{10,11... | collective-permute-start | bytes 3145736 | tf_op jit(solution)/shard_map/ppermute | solution.py:576
  82.5 0.9 copy-start.7
  82.8 2.9 %copy-start.3 = (f32[2,256,128]{2,1,0:T(8,128)S(1)}, f32[2,256,128]{2,1,0:T(8,128)}, u32[]{:S(2)}) copy-start(f32[2,256,128]{2,1,0:T(8,128)} %copy-done.2) | copy-start | bytes 786436
  85.7 27.5 %copy-start.5 = (bf16[128,384]{1,0:T(8,128)(2,1)S(1)}, bf16[128,384]{1,0:T(8,128)(2,1)}, u32[]{:S(2)}) copy-start(bf16[128,384]{1,0:T(8,128)(2,1)} %copy-done.4) | copy-start | bytes 294916
  85.7 27.5 %copy-start.10 = (f32[128,2048]{1,0:T(8,128)S(1)}, f32[128,2048]{1,0:T(8,128)}, u32[]{:S(2)}) copy-start(f32[128,2048]{1,0:T(8,128)} %get-tuple-element.93.refs_7_) | copy-start | bytes 3145732
Sparse Core Ops, SparseCore 0:
  24.0 40.3 all-gather.1

commit v4 on v3

--- a/solution.py
+++ b/solution.py
@@ -111,7 +111,7 @@
             jax.ShapeDtypeStruct((NP + 2,), jnp.int32),
             jax.ShapeDtypeStruct((NP, cols), jnp.float32),
         ),
-        in_specs=[smem, anywhere, anywhere],
+        in_specs=[smem, pl.BlockSpec(memory_space=pltpu.HBM), anywhere],
         out_specs=(vmem, vmem, smem, anywhere),
         scratch_shapes=[
             pltpu.VMEM((NP, LANES), jnp.float32),
@@ -185,7 +185,7 @@
     return pl.pallas_call(
         functools.partial(top_kernel, grid_rows),
         out_shape=(jax.ShapeDtypeStruct((cap_top, cols), jnp.float32),) * grid_rows,
-        in_specs=[smem, anywhere, anywhere],
+        in_specs=[smem, pl.BlockSpec(memory_space=pltpu.HBM), anywhere],
         out_specs=(vmem,) * grid_rows,
         scratch_shapes=[pltpu.SMEM((grid_rows,), jnp.int32), pltpu.SemaphoreType.DMA(())],
         compiler_params=pltpu.CompilerParams(vmem_limit_bytes=16 * MIB),
@@ -373,43 +373,35 @@
         out_ref[:, span] = a - mm(lower, upper_ref[:, span])
 
 
-def trailing_kernel(m_ref, own_ref, other_ref, weights_ref, upper_ref, out_ref, lower_ref):
-    step = pl.program_id(0)
-    rows = m_ref.shape[0]
-    half = own_ref.shape[0] // rows
-
-    def prepare(block):
-        here = pl.ds(pl.multiple_of(lax.rem(block, half) * rows, rows), rows)
-        panel = jnp.concatenate([own_ref[here, :], other_ref[here, :]], axis=1)
-        lower_ref[lax.rem(block, 2)] = multipliers(panel, weights_ref[lax.div(block, half)])
-
-    @pl.when(step == 0)
-    def _():
-        prepare(step)
-
-    update_rows(
-        m_ref, lower_ref[lax.rem(step, 2)], upper_ref, out_ref, lax.axis_index("col") < 2
-    )
-    prepare(jnp.minimum(step + 1, 2 * half - 1))
-
-
-def trailing(matrix, own, other, weights, upper):
-    rows, cols = matrix.shape
-    size = min(512, rows // 2)
-    vmem = pl.BlockSpec(memory_space=pltpu.VMEM)
-    return pl.pallas_call(
-        trailing_kernel,
-        out_shape=jax.ShapeDtypeStruct((rows, cols), jnp.float32),
-        grid=(rows // size,),
-        in_specs=[pl.BlockSpec((size, cols), lambda i: (i, 0))] + [vmem] * 4,
-        out_specs=pl.BlockSpec((size, cols), lambda i: (i, 0)),
-        scratch_shapes=[pltpu.VMEM((2, size, 3 * NP), jnp.bfloat16)],
-        compiler_params=pltpu.CompilerParams(vmem_limit_bytes=40 * MIB),
-        cost_estimate=pl.CostEstimate(
-            flops=6 * rows * cols * NP, bytes_accessed=8 * rows * cols, transcendentals=0
-        ),
-        name="trailing",
-    )(matrix, own, other, weights, upper)
+def lower_kernel(own_ref, other_ref, weights_ref, out_ref):
+    panel = jnp.concatenate([own_ref[...], other_ref[...]], axis=1)
+    out_ref[...] = multipliers(panel, weights_ref[0])
+
+
+def lower_rows(own, other, weights):
+    half = own.shape[0]
+    size = min(1024, half)
+    steps = half // size
+    packed = pl.BlockSpec((size, LANES), lambda i: (lax.rem(i, steps), 0))
+    return pl.pallas_call(
+        lower_kernel,
+        out_shape=jax.ShapeDtypeStruct((2 * half, 3 * NP), jnp.bfloat16),
+        grid=(2 * steps,),
+        in_specs=[
+            packed,
+            packed,
+            pl.BlockSpec((1, 2 * NP, NP), lambda i: (lax.div(i, steps), 0, 0)),
+        ],
+        out_specs=pl.BlockSpec((size, 3 * NP), lambda i: (i, 0)),
+        compiler_params=pltpu.CompilerParams(vmem_limit_bytes=24 * MIB),
+        name="lower_rows",
+    )(own, other, weights)
+
+
+def trailing(matrix, lower, upper, is_panel):
+    column = jnp.arange(matrix.shape[1], dtype=jnp.int32)
+    kept = jnp.where((is_panel & (column < NB))[None, :], 0.0, matrix)
+    return kept - mm(lower, upper)
 
 
 def place_kernel(grid_rows, over_ref, piv_ref, owned_ref, *refs):
@@ -593,7 +585,8 @@
     )
 
     upper, top = upper_rows_of(all_rows, linv, lu)
-    result = trailing(matrix, own, other, weights, upper)
+    lower = lower_rows(own, other, weights)
+    result = trailing(matrix, lower, upper, lax.axis_index("col") < 2)
     return place_moved(
         pieces, order_top, moved, upper, summed_tops, top, result, flat, owned, over_list
     )

time: 124 us -> 117 us (0.944)
  matrix products: 0 us -> 26.6 us
  Pallas kernels: 55.9 us -> 30 us
  local copies, waits for them, and re-layouts: 13.8 us -> 5.11 us
    dot_general x0 -> x1, matrix products: none -> 26.6 us  [mm(): return jnp.dot(a, b, preferred_element_type=jnp.float32)]
    pallas_call x1, Pallas kernels: 27.5 us -> 2.4 us  [lower_rows(): pl.pallas_call(lower_kernel, out_shape=jax.ShapeDtypeStruct((2 * half, 3...]
    unnamed x20 -> x22, local copies, waits for them, and re-layouts: 13 us -> 4.96 us
  transfers between devices with their start and end apart: 16 -> 16, of which waited for: 4 -> 4; matrix products, arithmetic and copies ran while one was open for 1% -> 24% of each run, Pallas kernels for 37% -> 22%
where the time goes in v4:
time: 117 us; the launch traced here: 116 us
  starting transfers between devices  30.5 us (26%)
  Pallas kernels  30 us (26%)
  matrix products  26.6 us (23%)
  between operations  14.4 us (12%)
  waiting for transfers between devices  8.12 us (7%)
  local copies, waits for them, and re-layouts  5.11 us (4%)
    dot_general x1, matrix products, mm(): return jnp.dot(a, b, preferred_element_type=jnp.float32)  26.6 us
    pallas_call x1, Pallas kernels, factor_corner(): pl.pallas_call(corner_kernel, out_shape=(jax.ShapeDtypeStruct((NP, NP), j...  12.1 us
    ppermute x4, starting transfers between devices, spread_round(): return lax.ppermute(value, 'col', pairs)  11.9 us
    ppermute x3, starting transfers between devices, shards(): pieces.append(lax.ppermute(tops[s], 'row', pairs))  9.01 us
    unnamed x22, local copies, waits for them, and re-layouts  4.96 us
    ppermute x3, starting transfers between devices, shards(): lax.ppermute(corner, 'row', shift)  4.83 us
    pallas_call x1, Pallas kernels, gather_rows(): pl.pallas_call(functools.partial(gather_kernel, grid_rows), out_shape=(ja...  4.63 us
    ppermute x3, starting transfers between devices, shards(): lax.ppermute(corner, 'col', [(0, 2 * chip), (1, 2 * chip + 1)])  4.48 us
  transfers between devices with their start and end apart: 16, of which 4 were waited for; matrix products, arithmetic and copies ran while one was open for 24% of the time, Pallas kernels for 22%

profile of v4, /device:TPU:0, one launch (start us, length us, event | category | flops | bytes accessed | tf_op | source)
XLA Modules:
  0.0 115.9 jit_solution(13263636972271286599)
XLA Ops:
  6.5 1.9 %pack_panel.1 = (f32[1024,128]{1,0:T(8,128)S(1)}, f32[1024,128]{1,0:T(8,128)S(1)}) custom-call(f32[4096,2048]{1,0:T(8,128)} %m_ref.3, f32[4096,2048]{1,0:T(8,128)} %m_ref.3, f32[4096,2048]{1,0:T(8,128)} %m_ref.3, f32[4096,2048]{1,0:T(8,128)} %m_ref.3), custom_call_target="tpu_custom_call" | custom-call | tf_op jit(solution)/shard_map/pack_panel/pallas_call | solution.py:135
  8.4 4.9 %collective-permute-start.7 = (f32[1024,128]{1,0:T(8,128)S(1)}, f32[1024,128]{1,0:T(8,128)S(1)}, u32[]{:S(2)}, u32[]{:S(2)}) collective-permute-start(f32[1024,128]{1,0:T(8,128)S(1)} %get-tuple-element.78._.held1), channel_id=1, source_target_pairs={{0,2},{1,3},{8,10},{9,11},{16,18},{17,19},{24,26},{25,27}} | collective-permute-start | bytes 1572872 | tf_op jit(solution)/shard_map/ppermute | solution.py:512
  13.3 0.1 reshape.267.piv_ref
  13.4 4.6 %gather_rows.1 = (f32[48,2048]{1,0:T(8,128)}, f32[128,128]{1,0:T(8,128)S(1)}, s32[130]{0:T(256)S(1)}, f32[128,2048]{1,0:T(8,128)}) custom-call(s32[128]{0:T(128)S(1)} %reshape.267.piv_ref, f32[4096,2048]{1,0:T(8,128)} %m_ref.3, f32[1024,128]{1,0:T(8,128)S(1)} %get-tuple-element.78._.held1), custom_call_target="tpu_custom_call" | custom-call | tf_op jit(solution)/shard_map/gather_rows/pallas_call | solution.py:106
  18.0 3.8 %collective-permute-start.2 = (f32[128,128]{1,0:T(8,128)S(1)}, f32[128,128]{1,0:T(8,128)S(1)}, u32[]{:S(2)}, u32[]{:S(2)}) collective-permute-start(f32[128,128]{1,0:T(8,128)S(1)} %get-tuple-element.80), channel_id=1, source_target_pairs={{0,24},{8,0},{16,8},{24,16},{1,25},{9,1},{17,9},{25,17},{2,26},{10... | collective-permute-start | bytes 196616 | tf_op jit(solution)/shard_map/ppermute | solution.py:532
  21.8 0.0 collective-permute-start.1
  21.8 1.0 collective-permute-start
  22.9 1.3 %collective-permute-start.8 = (f32[1024,128]{1,0:T(8,128)S(1)}, f32[1024,128]{1,0:T(8,128)S(1)}, u32[]{:S(2)}, u32[]{:S(2)}) collective-permute-start(f32[1024,128]{1,0:T(8,128)S(1)} %get-tuple-element.81.held2), channel_id=1, source_target_pairs={{0,4},{1,5},{8,12},{9,13},{16,20},{17,21},{24,28},{25,29}} | collective-permute-start | bytes 1572872 | tf_op jit(solution)/shard_map/ppermute | solution.py:512
  24.2 0.0 all-gather.2.cloned.1.call-update
  24.3 0.1 collective-permute-done.2
  24.3 3.7 %collective-permute-done.1 = f32[128,128]{1,0:T(8,128)S(1)} collective-permute-done((f32[128,128]{1,0:T(8,128)S(1)}, f32[128,128]{1,0:T(8,128)S(1)}, u32[]{:S(2)}, u32[]{:S(2)}) %collective-permute-start.1) | collective-permute-done | bytes 65568 | tf_op jit(solution)/shard_map/ppermute | solution.py:532
  28.1 0.0 collective-permute-done
  28.1 1.9 %collective-permute-start.5 = (f32[128,128]{1,0:T(8,128)S(1)}, f32[128,128]{1,0:T(8,128)S(1)}, u32[]{:S(2)}, u32[]{:S(2)}) collective-permute-start(f32[128,128]{1,0:T(8,128)S(1)} %add_add_fusion.1), channel_id=1, source_target_pairs={{0,6},{1,7},{8,14},{9,15},{16,22},{17,23},{24,30},{25,31}} | collective-permute-start | bytes 196616 | tf_op jit(solution)/shard_map/ppermute | solution.py:534
  30.0 1.3 %collective-permute-start.4 = (f32[128,128]{1,0:T(8,128)S(1)}, f32[128,128]{1,0:T(8,128)S(1)}, u32[]{:S(2)}, u32[]{:S(2)}) collective-permute-start(f32[128,128]{1,0:T(8,128)S(1)} %add_add_fusion.1), channel_id=1, source_target_pairs={{0,4},{1,5},{8,12},{9,13},{16,20},{17,21},{24,28},{25,29}} | collective-permute-start | bytes 196616 | tf_op jit(solution)/shard_map/ppermute | solution.py:534
  31.3 1.3 %collective-permute-start.3 = (f32[128,128]{1,0:T(8,128)S(1)}, f32[128,128]{1,0:T(8,128)S(1)}, u32[]{:S(2)}, u32[]{:S(2)}) collective-permute-start(f32[128,128]{1,0:T(8,128)S(1)} %add_add_fusion.1), channel_id=1, source_target_pairs={{0,2},{1,3},{8,10},{9,11},{16,18},{17,19},{24,26},{25,27}} | collective-permute-start | bytes 196616 | tf_op jit(solution)/shard_map/ppermute | solution.py:534
  32.6 0.2 convert_reduce_fusion.1
  32.8 3.1 %collective-permute-done.4 = f32[128,128]{1,0:T(8,128)S(1)} collective-permute-done((f32[128,128]{1,0:T(8,128)S(1)}, f32[128,128]{1,0:T(8,128)S(1)}, u32[]{:S(2)}, u32[]{:S(2)}) %collective-permute-start.4) | collective-permute-done | bytes 65568 | tf_op jit(solution)/shard_map/ppermute | solution.py:534
  35.9 0.0 collective-permute-done.3
  35.9 0.0 collective-permute-done.8.arrived2
  35.9 0.1 merge.2
  36.0 0.1 fusion.18
  36.1 2.9 %collective-permute-start.13 = (f32[1024,128]{1,0:T(8,128)S(1)}, f32[1024,128]{1,0:T(8,128)S(1)}, u32[]{:S(2)}, u32[]{:S(2)}) collective-permute-start(f32[1024,128]{1,0:T(8,128)S(1)} %get-tuple-element.133.held2), channel_id=1, source_target_pairs={{0,2},{1,3},{4,6},{5,7},{8,10},{9,11},{12,14},{13,15},{16,18},{17,... | collective-permute-start | bytes 1572872 | tf_op jit(solution)/shard_map/ppermute | solution.py:512
  39.0 2.9 %collective-permute-start.12 = (f32[1024,128]{1,0:T(8,128)S(1)}, f32[1024,128]{1,0:T(8,128)S(1)}, u32[]{:S(2)}, u32[]{:S(2)}) collective-permute-start(f32[1024,128]{1,0:T(8,128)S(1)} %get-tuple-element.134._.held1), channel_id=1, source_target_pairs={{0,4},{1,5},{2,6},{3,7},{8,12},{9,13},{10,14},{11,15},{16,20},{17,... | collective-permute-start | bytes 1572872 | tf_op jit(solution)/shard_map/ppermute | solution.py:512
  41.9 0.6 maximum_reduce_fusion
  43.2 0.1 collective-permute-start.6
  43.2 0.1 fusion.8.order_ref
  43.3 1.1 collective-permute-done.6.other_ref
  44.5 12.1 %factor_corner.1 = (f32[128,128]{1,0:T(8,128)S(1)}, bf16[128,384]{1,0:T(8,128)(2,1)S(1)}, f32[2,256,128]{2,1,0:T(8,128)S(1)}, bf16[128,384]{1,0:T(8,128)(2,1)S(1)}) custom-call(f32[128,128]{1,0:T(8,128)S(1)} %add_add_fusion._.mine_ref, f32[128,128]{1,0:T(8,128)S(1)} %collective-permute-done.6.other_ref, bf16[128,192]{1,0:T(8,128)(2,1)S(1)} %fusion.8.order_ref, ...), custom_call_target="tpu_custom_call" | custom-call | tf_op jit(solution)/shard_map/factor_corner/pallas_call | solution.py:287
  56.7 0.0 collective-permute-done.12.arrived1
  56.7 0.1 merge.3.own_ref
  56.8 0.5 copy-done.4
  57.3 0.0 copy-done.6
  57.4 0.0 copy-done.8
  57.4 0.2 collective-permute-start.14
  57.6 3.9 %top_rows.1 = (f32[32,2048]{1,0:T(8,128)S(1)}, f32[32,2048]{1,0:T(8,128)}, f32[32,2048]{1,0:T(8,128)}, f32[32,2048]{1,0:T(8,128)}) custom-call(s32[128]{0:T(128)S(1)} %reshape.267.piv_ref, f32[4096,2048]{1,0:T(8,128)} %m_ref.3, f32[128,128]{1,0:T(8,128)S(1)} %get-tuple-element.82._.lu_ref), custom_call_target="tpu_custom_call" | custom-call | tf_op jit(solution)/shard_map/top_rows/pallas_call | solution.py:185
  61.5 5.1 %collective-permute-start.9 = (f32[32,2048]{1,0:T(8,128)}, f32[32,2048]{1,0:T(8,128)}, u32[]{:S(2)}, u32[]{:S(2)}) collective-permute-start(f32[32,2048]{1,0:T(8,128)} %get-tuple-element.84), channel_id=1, source_target_pairs={{0,8},{8,16},{1,9},{9,17},{2,10},{10,18},{3,11},{11,19},{4,12},{12... | collective-permute-start | bytes 786440 | tf_op jit(solution)/shard_map/ppermute | solution.py:574
  66.6 2.0 %collective-permute-start.10 = (f32[32,2048]{1,0:T(8,128)}, f32[32,2048]{1,0:T(8,128)}, u32[]{:S(2)}, u32[]{:S(2)}) collective-permute-start(f32[32,2048]{1,0:T(8,128)} %get-tuple-element.85), channel_id=1, source_target_pairs={{0,16},{8,24},{1,17},{9,25},{2,18},{10,26},{3,19},{11,27},{4,20},{... | collective-permute-start | bytes 786440 | tf_op jit(solution)/shard_map/ppermute | solution.py:574
  68.6 1.9 %collective-permute-start.11 = (f32[32,2048]{1,0:T(8,128)}, f32[32,2048]{1,0:T(8,128)}, u32[]{:S(2)}, u32[]{:S(2)}) collective-permute-start(f32[32,2048]{1,0:T(8,128)} %get-tuple-element.86), channel_id=1, source_target_pairs={{0,24},{8,0},{1,25},{9,1},{2,26},{10,2},{3,27},{11,3},{4,28},{12,4... | collective-permute-start | bytes 786440 | tf_op jit(solution)/shard_map/ppermute | solution.py:574
  70.5 1.0 copy-done.2
  71.5 1.2 %copy-done.1 = f32[2048,128]{1,0:T(8,128)S(1)} copy-done((f32[2048,128]{1,0:T(8,128)S(1)}, f32[2048,128]{1,0:T(8,128)}, u32[]{:S(2)}) %copy-start.1) | copy-done | bytes 1048600
  72.7 1.2 %copy-done.3 = f32[2048,128]{1,0:T(8,128)S(1)} copy-done((f32[2048,128]{1,0:T(8,128)S(1)}, f32[2048,128]{1,0:T(8,128)}, u32[]{:S(2)}) %copy-start.3) | copy-done | bytes 1048600
  74.0 2.4 %lower_rows.1 = bf16[4096,384]{1,0:T(8,128)(2,1)S(1)} custom-call(f32[2048,128]{1,0:T(8,128)S(1)} %copy-done.1, f32[2048,128]{1,0:T(8,128)S(1)} %copy-done.3, f32[2,256,128]{2,1,0:T(8,128)S(1)} %copy-done.5), custom_call_target="tpu_custom_call" | custom-call | tf_op jit(solution)/shard_map/lower_rows/pallas_call | solution.py:386
  76.4 0.0 all-gather.2.cloned.1.call-done
  76.4 0.2 while.13
  76.6 0.9 copy-done.9
  77.5 2.2 %upper_rows.1 = (bf16[384,2048]{1,0:T(8,128)(2,1)S(1)}, f32[64,2048]{1,0:T(8,128)S(1)}) custom-call(f32[192,2048]{1,0:T(8,128)} %get-tuple-element.90.rows_ref, bf16[128,384]{1,0:T(8,128)(2,1)S(1)} %copy-done.9, f32[128,128]{1,0:T(8,128)S(1)} %get-tuple-element.82._.lu_ref), custom_call_target="tpu_custom_call" | custom-call | tf_op jit(solution)/shard_map/upper_rows/pallas_call | solution.py:340
  79.7 26.6 %select_subtract_fusion.refs_9_ = f32[4096,2048]{1,0:T(8,128)} fusion(f32[4096,2048]{1,0:T(8,128)} %get-tuple-element.183, pred[2048]{0:T(1024)(128)(4,1)S(1)} %fusion.12, bf16[4096,384]{1,0:T(8,128)(2,1)S(1)} %lower_rows.1, bf16[384,2048]{1,0:T(8,128)(2,1)S(1)} %get-tuple-element.92.refs_6_), kind=kOutput, calls=%fused_computation.25 | convolution fusion | flops 6459228160 | bytes 71829504 | tf_op jit(solution)/shard_map/dot_general | solution.py:38
  106.4 2.7 %place_moved.1 = f32[4096,2048]{1,0:T(8,128)} custom-call(s32[1]{0:T(128)} %bitcast.over_ref, s32[128]{0:T(128)S(1)} %get-tuple-element.200, s32[130]{0:T(256)S(1)} %get-tuple-element.79.owned_ref, f32[32,2048]{1,0:T(8,128)S(1)} %get-tuple-element.83.refs_0_, f32[32,2048]{1,0:T(8,128)} %collective-permute-done.9.refs_1_, ...), custom_call_target="tpu_custom_call", output_to_operand_aliasing={{}: (12, {})} | custom-call | tf_op jit(solution)/shard_map/place_moved/pallas_call | solution.py:466
  (31 shorter events, 0.1 us)
Async XLA Ops:
  6.5 6.8 %copy-start.10 = (s32[2,64]{1,0:T(2,128)S(1)}, s32[2,64]{1,0:T(2,128)}, u32[]{:S(2)}) copy-start(s32[2,64]{1,0:T(2,128)} %param.7) | copy-start | bytes 1540
  6.5 69.9 %all-gather.2.cloned.1.call-start = ((), (), s32[]{:S(2)}) async-start(), calls=%async_computation | async-start | bytes 1966080 | tf_op jit(solution)/shard_map/all_gather | solution.py:529
  8.4 27.5 %collective-permute-start.7 = (f32[1024,128]{1,0:T(8,128)S(1)}, f32[1024,128]{1,0:T(8,128)S(1)}, u32[]{:S(2)}, u32[]{:S(2)}) collective-permute-start(f32[1024,128]{1,0:T(8,128)S(1)} %get-tuple-element.78._.held1), channel_id=1, source_target_pairs={{0,2},{1,3},{8,10},{9,11},{16,18},{17,19},{24,26},{25,27}} | collective-permute-start | bytes 1572872 | tf_op jit(solution)/shard_map/ppermute | solution.py:512
  18.0 6.3 %collective-permute-start.2 = (f32[128,128]{1,0:T(8,128)S(1)}, f32[128,128]{1,0:T(8,128)S(1)}, u32[]{:S(2)}, u32[]{:S(2)}) collective-permute-start(f32[128,128]{1,0:T(8,128)S(1)} %get-tuple-element.80), channel_id=1, source_target_pairs={{0,24},{8,0},{16,8},{24,16},{1,25},{9,1},{17,9},{25,17},{2,26},{10... | collective-permute-start | bytes 196616 | tf_op jit(solution)/shard_map/ppermute | solution.py:532
  21.8 6.2 %collective-permute-start.1 = (f32[128,128]{1,0:T(8,128)S(1)}, f32[128,128]{1,0:T(8,128)S(1)}, u32[]{:S(2)}, u32[]{:S(2)}) collective-permute-start(f32[128,128]{1,0:T(8,128)S(1)} %get-tuple-element.80), channel_id=1, source_target_pairs={{0,16},{8,24},{16,0},{24,8},{1,17},{9,25},{17,1},{25,9},{2,18},{10... | collective-permute-start | bytes 196616 | tf_op jit(solution)/shard_map/ppermute | solution.py:532
  21.8 6.2 %collective-permute-start = (f32[128,128]{1,0:T(8,128)S(1)}, f32[128,128]{1,0:T(8,128)S(1)}, u32[]{:S(2)}, u32[]{:S(2)}) collective-permute-start(f32[128,128]{1,0:T(8,128)S(1)} %get-tuple-element.80), channel_id=1, source_target_pairs={{0,8},{8,16},{16,24},{24,0},{1,9},{9,17},{17,25},{25,1},{2,10},{10... | collective-permute-start | bytes 196616 | tf_op jit(solution)/shard_map/ppermute | solution.py:532
  22.9 13.0 %collective-permute-start.8 = (f32[1024,128]{1,0:T(8,128)S(1)}, f32[1024,128]{1,0:T(8,128)S(1)}, u32[]{:S(2)}, u32[]{:S(2)}) collective-permute-start(f32[1024,128]{1,0:T(8,128)S(1)} %get-tuple-element.81.held2), channel_id=1, source_target_pairs={{0,4},{1,5},{8,12},{9,13},{16,20},{17,21},{24,28},{25,29}} | collective-permute-start | bytes 1572872 | tf_op jit(solution)/shard_map/ppermute | solution.py:512
  28.1 4.7 %collective-permute-start.5 = (f32[128,128]{1,0:T(8,128)S(1)}, f32[128,128]{1,0:T(8,128)S(1)}, u32[]{:S(2)}, u32[]{:S(2)}) collective-permute-start(f32[128,128]{1,0:T(8,128)S(1)} %add_add_fusion.1), channel_id=1, source_target_pairs={{0,6},{1,7},{8,14},{9,15},{16,22},{17,23},{24,30},{25,31}} | collective-permute-start | bytes 196616 | tf_op jit(solution)/shard_map/ppermute | solution.py:534
  30.0 5.9 %collective-permute-start.4 = (f32[128,128]{1,0:T(8,128)S(1)}, f32[128,128]{1,0:T(8,128)S(1)}, u32[]{:S(2)}, u32[]{:S(2)}) collective-permute-start(f32[128,128]{1,0:T(8,128)S(1)} %add_add_fusion.1), channel_id=1, source_target_pairs={{0,4},{1,5},{8,12},{9,13},{16,20},{17,21},{24,28},{25,29}} | collective-permute-start | bytes 196616 | tf_op jit(solution)/shard_map/ppermute | solution.py:534
  31.3 4.6 %collective-permute-start.3 = (f32[128,128]{1,0:T(8,128)S(1)}, f32[128,128]{1,0:T(8,128)S(1)}, u32[]{:S(2)}, u32[]{:S(2)}) collective-permute-start(f32[128,128]{1,0:T(8,128)S(1)} %add_add_fusion.1), channel_id=1, source_target_pairs={{0,2},{1,3},{8,10},{9,11},{16,18},{17,19},{24,26},{25,27}} | collective-permute-start | bytes 196616 | tf_op jit(solution)/shard_map/ppermute | solution.py:534
  36.1 20.6 %collective-permute-start.13 = (f32[1024,128]{1,0:T(8,128)S(1)}, f32[1024,128]{1,0:T(8,128)S(1)}, u32[]{:S(2)}, u32[]{:S(2)}) collective-permute-start(f32[1024,128]{1,0:T(8,128)S(1)} %get-tuple-element.133.held2), channel_id=1, source_target_pairs={{0,2},{1,3},{4,6},{5,7},{8,10},{9,11},{12,14},{13,15},{16,18},{17,... | collective-permute-start | bytes 1572872 | tf_op jit(solution)/shard_map/ppermute | solution.py:512
  39.0 17.7 %collective-permute-start.12 = (f32[1024,128]{1,0:T(8,128)S(1)}, f32[1024,128]{1,0:T(8,128)S(1)}, u32[]{:S(2)}, u32[]{:S(2)}) collective-permute-start(f32[1024,128]{1,0:T(8,128)S(1)} %get-tuple-element.134._.held1), channel_id=1, source_target_pairs={{0,4},{1,5},{2,6},{3,7},{8,12},{9,13},{10,14},{11,15},{16,20},{17,... | collective-permute-start | bytes 1572872 | tf_op jit(solution)/shard_map/ppermute | solution.py:512
  43.2 1.3 %collective-permute-start.6 = (f32[128,128]{1,0:T(8,128)S(1)}, f32[128,128]{1,0:T(8,128)S(1)}, u32[]{:S(2)}, u32[]{:S(2)}) collective-permute-start(f32[128,128]{1,0:T(8,128)S(1)} %add_add_fusion._.mine_ref), channel_id=1, source_target_pairs={{0,1},{1,0},{2,3},{3,2},{4,5},{5,4},{6,7},{7,6},{8,9},{9,8},{10,11... | collective-permute-start | bytes 196616 | tf_op jit(solution)/shard_map/ppermute | solution.py:536
  56.6 0.7 copy-start.4
  56.6 0.7 copy-start.6
  56.6 0.8 copy-start.8
  57.4 4.1 %copy-start = (f32[2048,128]{1,0:T(8,128)}, f32[2048,128]{1,0:T(8,128)S(1)}, u32[]{:S(2)}) copy-start(f32[2048,128]{1,0:T(8,128)S(1)} %merge.3.own_ref) | copy-start | bytes 3145732
  57.4 13.1 %collective-permute-start.14 = (f32[2048,128]{1,0:T(8,128)S(1)}, f32[2048,128]{1,0:T(8,128)S(1)}, u32[]{:S(2)}, u32[]{:S(2)}) collective-permute-start(f32[2048,128]{1,0:T(8,128)S(1)} %merge.3.own_ref), channel_id=1, source_target_pairs={{0,1},{1,0},{2,3},{3,2},{4,5},{5,4},{6,7},{7,6},{8,9},{9,8},{10,11... | collective-permute-start | bytes 3145736 | tf_op jit(solution)/shard_map/ppermute | solution.py:568
  57.6 13.9 %copy-start.5 = (f32[2,256,128]{2,1,0:T(8,128)S(1)}, f32[2,256,128]{2,1,0:T(8,128)}, u32[]{:S(2)}) copy-start(f32[2,256,128]{2,1,0:T(8,128)} %copy-done.4) | copy-start | bytes 786436
  61.5 44.8 %collective-permute-start.9 = (f32[32,2048]{1,0:T(8,128)}, f32[32,2048]{1,0:T(8,128)}, u32[]{:S(2)}, u32[]{:S(2)}) collective-permute-start(f32[32,2048]{1,0:T(8,128)} %get-tuple-element.84), channel_id=1, source_target_pairs={{0,8},{8,16},{1,9},{9,17},{2,10},{10,18},{3,11},{11,19},{4,12},{12... | collective-permute-start | bytes 786440 | tf_op jit(solution)/shard_map/ppermute | solution.py:574
  66.6 39.8 %collective-permute-start.10 = (f32[32,2048]{1,0:T(8,128)}, f32[32,2048]{1,0:T(8,128)}, u32[]{:S(2)}, u32[]{:S(2)}) collective-permute-start(f32[32,2048]{1,0:T(8,128)} %get-tuple-element.85), channel_id=1, source_target_pairs={{0,16},{8,24},{1,17},{9,25},{2,18},{10,26},{3,19},{11,27},{4,20},{... | collective-permute-start | bytes 786440 | tf_op jit(solution)/shard_map/ppermute | solution.py:574
  68.6 37.8 %collective-permute-start.11 = (f32[32,2048]{1,0:T(8,128)}, f32[32,2048]{1,0:T(8,128)}, u32[]{:S(2)}, u32[]{:S(2)}) collective-permute-start(f32[32,2048]{1,0:T(8,128)} %get-tuple-element.86), channel_id=1, source_target_pairs={{0,24},{8,0},{1,25},{9,1},{2,26},{10,2},{3,27},{11,3},{4,28},{12,4... | collective-permute-start | bytes 786440 | tf_op jit(solution)/shard_map/ppermute | solution.py:574
  70.5 1.0 copy-start.2
  71.5 1.2 %copy-start.1 = (f32[2048,128]{1,0:T(8,128)S(1)}, f32[2048,128]{1,0:T(8,128)}, u32[]{:S(2)}) copy-start(f32[2048,128]{1,0:T(8,128)} %copy-done) | copy-start | bytes 3145732
  72.7 1.2 %copy-start.3 = (f32[2048,128]{1,0:T(8,128)S(1)}, f32[2048,128]{1,0:T(8,128)}, u32[]{:S(2)}) copy-start(f32[2048,128]{1,0:T(8,128)} %copy-done.2) | copy-start | bytes 3145732
  76.6 0.9 copy-start.9
  79.7 26.6 %copy-start.7 = (bf16[128,384]{1,0:T(8,128)(2,1)S(1)}, bf16[128,384]{1,0:T(8,128)(2,1)}, u32[]{:S(2)}) copy-start(bf16[128,384]{1,0:T(8,128)(2,1)} %copy-done.6) | copy-start | bytes 294916
Sparse Core Ops, SparseCore 0:
  24.3 35.6 all-gather.1

commit v5 on v4

--- a/solution.py
+++ b/solution.py
@@ -361,7 +361,7 @@
 
 def update_rows(a_ref, lower, upper_ref, out_ref, is_panel):
     rows, cols = out_ref.shape
-    width = min(cols, 1024)
+    width = min(cols, 512)
     lane = lax.broadcasted_iota(jnp.int32, (rows, LANES), 1)
 
     for start in range(0, cols, width):
@@ -398,10 +398,30 @@
     )(own, other, weights)
 
 
-def trailing(matrix, lower, upper, is_panel):
-    column = jnp.arange(matrix.shape[1], dtype=jnp.int32)
-    kept = jnp.where((is_panel & (column < NB))[None, :], 0.0, matrix)
-    return kept - mm(lower, upper)
+def trailing_kernel(m_ref, lower_ref, upper_ref, out_ref):
+    update_rows(m_ref, lower_ref[...], upper_ref, out_ref, lax.axis_index("col") < 2)
+
+
+def trailing(matrix, lower, upper):
+    rows, cols = matrix.shape
+    size = min(512, rows)
+    block = pl.BlockSpec((size, cols), lambda i: (i, 0))
+    return pl.pallas_call(
+        trailing_kernel,
+        out_shape=jax.ShapeDtypeStruct((rows, cols), jnp.float32),
+        grid=(rows // size,),
+        in_specs=[
+            block,
+            pl.BlockSpec((size, 3 * NP), lambda i: (i, 0)),
+            pl.BlockSpec(memory_space=pltpu.VMEM),
+        ],
+        out_specs=block,
+        compiler_params=pltpu.CompilerParams(vmem_limit_bytes=28 * MIB),
+        cost_estimate=pl.CostEstimate(
+            flops=6 * rows * cols * NP, bytes_accessed=8 * rows * cols, transcendentals=0
+        ),
+        name="trailing",
+    )(matrix, lower, upper)
 
 
 def place_kernel(grid_rows, over_ref, piv_ref, owned_ref, *refs):
@@ -586,7 +606,7 @@
 
     upper, top = upper_rows_of(all_rows, linv, lu)
     lower = lower_rows(own, other, weights)
-    result = trailing(matrix, lower, upper, lax.axis_index("col") < 2)
+    result = trailing(matrix, lower, upper)
     return place_moved(
         pieces, order_top, moved, upper, summed_tops, top, result, flat, owned, over_list
     )

time: 117 us -> 116 us (level)
  matrix products: 26.6 us -> 0 us
  Pallas kernels: 30 us -> 56.4 us
    dot_general x1 -> x0, matrix products: 26.6 us -> none  [mm(): return jnp.dot(a, b, preferred_element_type=jnp.float32)]
    pallas_call x0 -> x1, Pallas kernels: none -> 26.1 us  [trailing(): pl.pallas_call(trailing_kernel, out_shape=jax.ShapeDtypeStruct((rows, col...]
    unnamed x22 -> x24, local copies, waits for them, and re-layouts: 4.96 us -> 4.97 us
  transfers between devices with their start and end apart: 16 -> 16, of which waited for: 4 -> 5; matrix products, arithmetic and copies ran while one was open for 24% -> 1% of each run, Pallas kernels for 22% -> 45%
where the time goes in v5:
time: 116 us
  Pallas kernels  56.4 us (49%)
  starting transfers between devices  30.3 us (26%)
  between operations  14.4 us (12%)
  waiting for transfers between devices  8.12 us (7%)
  local copies, waits for them, and re-layouts  5.12 us (4%)
    pallas_call x1, Pallas kernels, trailing(): pl.pallas_call(trailing_kernel, out_shape=jax.ShapeDtypeStruct((rows, col...  26.1 us
    pallas_call x1, Pallas kernels, factor_corner(): pl.pallas_call(corner_kernel, out_shape=(jax.ShapeDtypeStruct((NP, NP), j...  12.1 us
    ppermute x4, starting transfers between devices, spread_round(): return lax.ppermute(value, 'col', pairs)  11.9 us
    ppermute x3, starting transfers between devices, shards(): pieces.append(lax.ppermute(tops[s], 'row', pairs))  9.08 us
    unnamed x24, local copies, waits for them, and re-layouts  4.97 us
    pallas_call x1, Pallas kernels, gather_rows(): pl.pallas_call(functools.partial(gather_kernel, grid_rows), out_shape=(ja...  4.76 us
    ppermute x3, starting transfers between devices, shards(): lax.ppermute(corner, 'row', shift)  4.6 us
    ppermute x3, starting transfers between devices, shards(): lax.ppermute(corner, 'col', [(0, 2 * chip), (1, 2 * chip + 1)])  4.48 us
  transfers between devices with their start and end apart: 16, of which 5 were waited for; matrix products, arithmetic and copies ran while one was open for 1% of the time, Pallas kernels for 45%

profile of v5, /device:TPU:0, one launch (start us, length us, event | category | flops | bytes accessed | tf_op | source)
XLA Modules:
  0.0 115.6 jit_solution(146475069462410994)
XLA Ops:
  6.5 1.9 %pack_panel.1 = (f32[1024,128]{1,0:T(8,128)S(1)}, f32[1024,128]{1,0:T(8,128)S(1)}) custom-call(f32[4096,2048]{1,0:T(8,128)} %m_ref.5, f32[4096,2048]{1,0:T(8,128)} %m_ref.5, f32[4096,2048]{1,0:T(8,128)} %m_ref.5, f32[4096,2048]{1,0:T(8,128)} %m_ref.5), custom_call_target="tpu_custom_call" | custom-call | tf_op jit(solution)/shard_map/pack_panel/pallas_call | solution.py:135
  8.4 4.9 %collective-permute-start.7 = (f32[1024,128]{1,0:T(8,128)S(1)}, f32[1024,128]{1,0:T(8,128)S(1)}, u32[]{:S(2)}, u32[]{:S(2)}) collective-permute-start(f32[1024,128]{1,0:T(8,128)S(1)} %get-tuple-element.78._.held1), channel_id=1, source_target_pairs={{0,2},{1,3},{8,10},{9,11},{16,18},{17,19},{24,26},{25,27}} | collective-permute-start | bytes 1572872 | tf_op jit(solution)/shard_map/ppermute | solution.py:532
  13.3 0.1 reshape.262.piv_ref
  13.4 4.8 %gather_rows.1 = (f32[48,2048]{1,0:T(8,128)}, f32[128,128]{1,0:T(8,128)S(1)}, s32[130]{0:T(256)S(1)}, f32[128,2048]{1,0:T(8,128)}) custom-call(s32[128]{0:T(128)S(1)} %reshape.262.piv_ref, f32[4096,2048]{1,0:T(8,128)} %m_ref.5, f32[1024,128]{1,0:T(8,128)S(1)} %get-tuple-element.78._.held1), custom_call_target="tpu_custom_call" | custom-call | tf_op jit(solution)/shard_map/gather_rows/pallas_call | solution.py:106
  18.2 3.7 %collective-permute-start.2 = (f32[128,128]{1,0:T(8,128)S(1)}, f32[128,128]{1,0:T(8,128)S(1)}, u32[]{:S(2)}, u32[]{:S(2)}) collective-permute-start(f32[128,128]{1,0:T(8,128)S(1)} %get-tuple-element.80), channel_id=1, source_target_pairs={{0,24},{8,0},{16,8},{24,16},{1,25},{9,1},{17,9},{25,17},{2,26},{10... | collective-permute-start | bytes 196616 | tf_op jit(solution)/shard_map/ppermute | solution.py:552
  21.8 0.9 collective-permute-start
  22.8 1.3 %collective-permute-start.8 = (f32[1024,128]{1,0:T(8,128)S(1)}, f32[1024,128]{1,0:T(8,128)S(1)}, u32[]{:S(2)}, u32[]{:S(2)}) collective-permute-start(f32[1024,128]{1,0:T(8,128)S(1)} %get-tuple-element.81.held2), channel_id=1, source_target_pairs={{0,4},{1,5},{8,12},{9,13},{16,20},{17,21},{24,28},{25,29}} | collective-permute-start | bytes 1572872 | tf_op jit(solution)/shard_map/ppermute | solution.py:532
  24.1 0.0 all-gather.2.cloned.1.call-update
  24.2 0.2 collective-permute-done.2
  24.3 2.9 %collective-permute-done.1 = f32[128,128]{1,0:T(8,128)S(1)} collective-permute-done((f32[128,128]{1,0:T(8,128)S(1)}, f32[128,128]{1,0:T(8,128)S(1)}, u32[]{:S(2)}, u32[]{:S(2)}) %collective-permute-start.1) | collective-permute-done | bytes 65568 | tf_op jit(solution)/shard_map/ppermute | solution.py:552
  27.3 0.7 collective-permute-done
  28.0 1.9 %collective-permute-start.5 = (f32[128,128]{1,0:T(8,128)S(1)}, f32[128,128]{1,0:T(8,128)S(1)}, u32[]{:S(2)}, u32[]{:S(2)}) collective-permute-start(f32[128,128]{1,0:T(8,128)S(1)} %add_add_fusion.1), channel_id=1, source_target_pairs={{0,6},{1,7},{8,14},{9,15},{16,22},{17,23},{24,30},{25,31}} | collective-permute-start | bytes 196616 | tf_op jit(solution)/shard_map/ppermute | solution.py:554
  29.9 1.3 %collective-permute-start.4 = (f32[128,128]{1,0:T(8,128)S(1)}, f32[128,128]{1,0:T(8,128)S(1)}, u32[]{:S(2)}, u32[]{:S(2)}) collective-permute-start(f32[128,128]{1,0:T(8,128)S(1)} %add_add_fusion.1), channel_id=1, source_target_pairs={{0,4},{1,5},{8,12},{9,13},{16,20},{17,21},{24,28},{25,29}} | collective-permute-start | bytes 196616 | tf_op jit(solution)/shard_map/ppermute | solution.py:554
  31.2 1.3 %collective-permute-start.3 = (f32[128,128]{1,0:T(8,128)S(1)}, f32[128,128]{1,0:T(8,128)S(1)}, u32[]{:S(2)}, u32[]{:S(2)}) collective-permute-start(f32[128,128]{1,0:T(8,128)S(1)} %add_add_fusion.1), channel_id=1, source_target_pairs={{0,2},{1,3},{8,10},{9,11},{16,18},{17,19},{24,26},{25,27}} | collective-permute-start | bytes 196616 | tf_op jit(solution)/shard_map/ppermute | solution.py:554
  32.5 0.2 convert_reduce_fusion.1
  32.7 0.0 collective-permute-done.5
  32.7 3.1 %collective-permute-done.4 = f32[128,128]{1,0:T(8,128)S(1)} collective-permute-done((f32[128,128]{1,0:T(8,128)S(1)}, f32[128,128]{1,0:T(8,128)S(1)}, u32[]{:S(2)}, u32[]{:S(2)}) %collective-permute-start.4) | collective-permute-done | bytes 65568 | tf_op jit(solution)/shard_map/ppermute | solution.py:554
  35.8 0.0 collective-permute-done.3
  35.8 0.0 collective-permute-done.8.arrived2
  35.8 0.1 merge.2
  35.9 0.1 fusion.17
  36.0 2.9 %collective-permute-start.13 = (f32[1024,128]{1,0:T(8,128)S(1)}, f32[1024,128]{1,0:T(8,128)S(1)}, u32[]{:S(2)}, u32[]{:S(2)}) collective-permute-start(f32[1024,128]{1,0:T(8,128)S(1)} %get-tuple-element.133.held2), channel_id=1, source_target_pairs={{0,2},{1,3},{4,6},{5,7},{8,10},{9,11},{12,14},{13,15},{16,18},{17,... | collective-permute-start | bytes 1572872 | tf_op jit(solution)/shard_map/ppermute | solution.py:532
  38.9 2.9 %collective-permute-start.12 = (f32[1024,128]{1,0:T(8,128)S(1)}, f32[1024,128]{1,0:T(8,128)S(1)}, u32[]{:S(2)}, u32[]{:S(2)}) collective-permute-start(f32[1024,128]{1,0:T(8,128)S(1)} %get-tuple-element.134._.held1), channel_id=1, source_target_pairs={{0,4},{1,5},{2,6},{3,7},{8,12},{9,13},{10,14},{11,15},{16,20},{17,... | collective-permute-start | bytes 1572872 | tf_op jit(solution)/shard_map/ppermute | solution.py:532
  41.8 0.6 maximum_reduce_fusion
  43.1 0.1 collective-permute-start.6
  43.1 0.1 fusion.8.order_ref
  43.2 1.1 collective-permute-done.6.other_ref
  44.4 12.1 %factor_corner.1 = (f32[128,128]{1,0:T(8,128)S(1)}, bf16[128,384]{1,0:T(8,128)(2,1)S(1)}, f32[2,256,128]{2,1,0:T(8,128)S(1)}, bf16[128,384]{1,0:T(8,128)(2,1)S(1)}) custom-call(f32[128,128]{1,0:T(8,128)S(1)} %add_add_fusion._.mine_ref, f32[128,128]{1,0:T(8,128)S(1)} %collective-permute-done.6.other_ref, bf16[128,192]{1,0:T(8,128)(2,1)S(1)} %fusion.8.order_ref, ...), custom_call_target="tpu_custom_call" | custom-call | tf_op jit(solution)/shard_map/factor_corner/pallas_call | solution.py:287
  56.6 0.0 collective-permute-done.12.arrived1
  56.6 0.1 merge.3.own_ref
  56.7 0.5 copy-done.4
  57.2 0.0 copy-done.6
  57.3 0.1 copy-done.8
  57.3 0.2 collective-permute-start.14
  57.5 3.9 %top_rows.1 = (f32[32,2048]{1,0:T(8,128)S(1)}, f32[32,2048]{1,0:T(8,128)}, f32[32,2048]{1,0:T(8,128)}, f32[32,2048]{1,0:T(8,128)}) custom-call(s32[128]{0:T(128)S(1)} %reshape.262.piv_ref, f32[4096,2048]{1,0:T(8,128)} %m_ref.5, f32[128,128]{1,0:T(8,128)S(1)} %get-tuple-element.82._.lu_ref), custom_call_target="tpu_custom_call" | custom-call | tf_op jit(solution)/shard_map/top_rows/pallas_call | solution.py:185
  61.4 5.2 %collective-permute-start.9 = (f32[32,2048]{1,0:T(8,128)}, f32[32,2048]{1,0:T(8,128)}, u32[]{:S(2)}, u32[]{:S(2)}) collective-permute-start(f32[32,2048]{1,0:T(8,128)} %get-tuple-element.84), channel_id=1, source_target_pairs={{0,8},{8,16},{1,9},{9,17},{2,10},{10,18},{3,11},{11,19},{4,12},{12... | collective-permute-start | bytes 786440 | tf_op jit(solution)/shard_map/ppermute | solution.py:594
  66.6 2.0 %collective-permute-start.10 = (f32[32,2048]{1,0:T(8,128)}, f32[32,2048]{1,0:T(8,128)}, u32[]{:S(2)}, u32[]{:S(2)}) collective-permute-start(f32[32,2048]{1,0:T(8,128)} %get-tuple-element.85), channel_id=1, source_target_pairs={{0,16},{8,24},{1,17},{9,25},{2,18},{10,26},{3,19},{11,27},{4,20},{... | collective-permute-start | bytes 786440 | tf_op jit(solution)/shard_map/ppermute | solution.py:594
  68.6 1.9 %collective-permute-start.11 = (f32[32,2048]{1,0:T(8,128)}, f32[32,2048]{1,0:T(8,128)}, u32[]{:S(2)}, u32[]{:S(2)}) collective-permute-start(f32[32,2048]{1,0:T(8,128)} %get-tuple-element.86), channel_id=1, source_target_pairs={{0,24},{8,0},{1,25},{9,1},{2,26},{10,2},{3,27},{11,3},{4,28},{12,4... | collective-permute-start | bytes 786440 | tf_op jit(solution)/shard_map/ppermute | solution.py:594
  70.5 1.0 copy-done.2
  71.5 1.2 %copy-done.1 = f32[2048,128]{1,0:T(8,128)S(1)} copy-done((f32[2048,128]{1,0:T(8,128)S(1)}, f32[2048,128]{1,0:T(8,128)}, u32[]{:S(2)}) %copy-start.1) | copy-done | bytes 1048600
  72.7 1.2 %copy-done.3 = f32[2048,128]{1,0:T(8,128)S(1)} copy-done((f32[2048,128]{1,0:T(8,128)S(1)}, f32[2048,128]{1,0:T(8,128)}, u32[]{:S(2)}) %copy-start.3) | copy-done | bytes 1048600
  73.9 2.4 %lower_rows.1.lower_ref = bf16[4096,384]{1,0:T(8,128)(2,1)S(1)} custom-call(f32[2048,128]{1,0:T(8,128)S(1)} %copy-done.1, f32[2048,128]{1,0:T(8,128)S(1)} %copy-done.3, f32[2,256,128]{2,1,0:T(8,128)S(1)} %copy-done.5), custom_call_target="tpu_custom_call" | custom-call | tf_op jit(solution)/shard_map/lower_rows/pallas_call | solution.py:386
  76.4 0.0 all-gather.2.cloned.1.call-done
  76.4 0.2 while.13
  76.6 0.9 copy-done.9
  77.5 2.2 %upper_rows.1 = (bf16[384,2048]{1,0:T(8,128)(2,1)S(1)}, f32[64,2048]{1,0:T(8,128)S(1)}) custom-call(f32[192,2048]{1,0:T(8,128)} %get-tuple-element.90.rows_ref, bf16[128,384]{1,0:T(8,128)(2,1)S(1)} %copy-done.9, f32[128,128]{1,0:T(8,128)S(1)} %get-tuple-element.82._.lu_ref), custom_call_target="tpu_custom_call" | custom-call | tf_op jit(solution)/shard_map/upper_rows/pallas_call | solution.py:340
  79.7 26.1 %trailing.1.refs_9_ = f32[4096,2048]{1,0:T(8,128)} custom-call(f32[4096,2048]{1,0:T(8,128)} %get-tuple-element.183, bf16[4096,384]{1,0:T(8,128)(2,1)S(1)} %lower_rows.1.lower_ref, bf16[384,2048]{1,0:T(8,128)(2,1)S(1)} %get-tuple-element.92.upper_ref.refs_6_), custom_call_target="tpu_custom_call" | custom-call | flops 6442450944 | bytes 67108864 | tf_op jit(solution)/shard_map/trailing/pallas_call | solution.py:409
  105.9 2.8 %place_moved.1 = f32[4096,2048]{1,0:T(8,128)} custom-call(s32[1]{0:T(128)} %bitcast.over_ref, s32[128]{0:T(128)S(1)} %get-tuple-element.200, s32[130]{0:T(256)S(1)} %get-tuple-element.79.owned_ref, f32[32,2048]{1,0:T(8,128)S(1)} %get-tuple-element.83.refs_0_, f32[32,2048]{1,0:T(8,128)} %collective-permute-done.9.refs_1_, ...), custom_call_target="tpu_custom_call", output_to_operand_aliasing={{}: (12, {})} | custom-call | tf_op jit(solution)/shard_map/place_moved/pallas_call | solution.py:486
  (32 shorter events, 0.1 us)
Async XLA Ops:
  6.5 6.8 %copy-start.11 = (s32[2,64]{1,0:T(2,128)S(1)}, s32[2,64]{1,0:T(2,128)}, u32[]{:S(2)}) copy-start(s32[2,64]{1,0:T(2,128)} %param.7) | copy-start | bytes 1540
  6.5 69.8 %all-gather.2.cloned.1.call-start = ((), (), s32[]{:S(2)}) async-start(), calls=%async_computation | async-start | bytes 1966080 | tf_op jit(solution)/shard_map/all_gather | solution.py:549
  8.4 27.4 %collective-permute-start.7 = (f32[1024,128]{1,0:T(8,128)S(1)}, f32[1024,128]{1,0:T(8,128)S(1)}, u32[]{:S(2)}, u32[]{:S(2)}) collective-permute-start(f32[1024,128]{1,0:T(8,128)S(1)} %get-tuple-element.78._.held1), channel_id=1, source_target_pairs={{0,2},{1,3},{8,10},{9,11},{16,18},{17,19},{24,26},{25,27}} | collective-permute-start | bytes 1572872 | tf_op jit(solution)/shard_map/ppermute | solution.py:532
  18.2 6.2 %collective-permute-start.2 = (f32[128,128]{1,0:T(8,128)S(1)}, f32[128,128]{1,0:T(8,128)S(1)}, u32[]{:S(2)}, u32[]{:S(2)}) collective-permute-start(f32[128,128]{1,0:T(8,128)S(1)} %get-tuple-element.80), channel_id=1, source_target_pairs={{0,24},{8,0},{16,8},{24,16},{1,25},{9,1},{17,9},{25,17},{2,26},{10... | collective-permute-start | bytes 196616 | tf_op jit(solution)/shard_map/ppermute | solution.py:552
  21.8 5.4 %collective-permute-start.1 = (f32[128,128]{1,0:T(8,128)S(1)}, f32[128,128]{1,0:T(8,128)S(1)}, u32[]{:S(2)}, u32[]{:S(2)}) collective-permute-start(f32[128,128]{1,0:T(8,128)S(1)} %get-tuple-element.80), channel_id=1, source_target_pairs={{0,16},{8,24},{16,0},{24,8},{1,17},{9,25},{17,1},{25,9},{2,18},{10... | collective-permute-start | bytes 196616 | tf_op jit(solution)/shard_map/ppermute | solution.py:552
  21.8 6.1 %collective-permute-start = (f32[128,128]{1,0:T(8,128)S(1)}, f32[128,128]{1,0:T(8,128)S(1)}, u32[]{:S(2)}, u32[]{:S(2)}) collective-permute-start(f32[128,128]{1,0:T(8,128)S(1)} %get-tuple-element.80), channel_id=1, source_target_pairs={{0,8},{8,16},{16,24},{24,0},{1,9},{9,17},{17,25},{25,1},{2,10},{10... | collective-permute-start | bytes 196616 | tf_op jit(solution)/shard_map/ppermute | solution.py:552
  22.8 13.0 %collective-permute-start.8 = (f32[1024,128]{1,0:T(8,128)S(1)}, f32[1024,128]{1,0:T(8,128)S(1)}, u32[]{:S(2)}, u32[]{:S(2)}) collective-permute-start(f32[1024,128]{1,0:T(8,128)S(1)} %get-tuple-element.81.held2), channel_id=1, source_target_pairs={{0,4},{1,5},{8,12},{9,13},{16,20},{17,21},{24,28},{25,29}} | collective-permute-start | bytes 1572872 | tf_op jit(solution)/shard_map/ppermute | solution.py:532
  28.0 4.7 %collective-permute-start.5 = (f32[128,128]{1,0:T(8,128)S(1)}, f32[128,128]{1,0:T(8,128)S(1)}, u32[]{:S(2)}, u32[]{:S(2)}) collective-permute-start(f32[128,128]{1,0:T(8,128)S(1)} %add_add_fusion.1), channel_id=1, source_target_pairs={{0,6},{1,7},{8,14},{9,15},{16,22},{17,23},{24,30},{25,31}} | collective-permute-start | bytes 196616 | tf_op jit(solution)/shard_map/ppermute | solution.py:554
  29.9 5.9 %collective-permute-start.4 = (f32[128,128]{1,0:T(8,128)S(1)}, f32[128,128]{1,0:T(8,128)S(1)}, u32[]{:S(2)}, u32[]{:S(2)}) collective-permute-start(f32[128,128]{1,0:T(8,128)S(1)} %add_add_fusion.1), channel_id=1, source_target_pairs={{0,4},{1,5},{8,12},{9,13},{16,20},{17,21},{24,28},{25,29}} | collective-permute-start | bytes 196616 | tf_op jit(solution)/shard_map/ppermute | solution.py:554
  31.2 4.6 %collective-permute-start.3 = (f32[128,128]{1,0:T(8,128)S(1)}, f32[128,128]{1,0:T(8,128)S(1)}, u32[]{:S(2)}, u32[]{:S(2)}) collective-permute-start(f32[128,128]{1,0:T(8,128)S(1)} %add_add_fusion.1), channel_id=1, source_target_pairs={{0,2},{1,3},{8,10},{9,11},{16,18},{17,19},{24,26},{25,27}} | collective-permute-start | bytes 196616 | tf_op jit(solution)/shard_map/ppermute | solution.py:554
  36.0 20.6 %collective-permute-start.13 = (f32[1024,128]{1,0:T(8,128)S(1)}, f32[1024,128]{1,0:T(8,128)S(1)}, u32[]{:S(2)}, u32[]{:S(2)}) collective-permute-start(f32[1024,128]{1,0:T(8,128)S(1)} %get-tuple-element.133.held2), channel_id=1, source_target_pairs={{0,2},{1,3},{4,6},{5,7},{8,10},{9,11},{12,14},{13,15},{16,18},{17,... | collective-permute-start | bytes 1572872 | tf_op jit(solution)/shard_map/ppermute | solution.py:532
  38.9 17.7 %collective-permute-start.12 = (f32[1024,128]{1,0:T(8,128)S(1)}, f32[1024,128]{1,0:T(8,128)S(1)}, u32[]{:S(2)}, u32[]{:S(2)}) collective-permute-start(f32[1024,128]{1,0:T(8,128)S(1)} %get-tuple-element.134._.held1), channel_id=1, source_target_pairs={{0,4},{1,5},{2,6},{3,7},{8,12},{9,13},{10,14},{11,15},{16,20},{17,... | collective-permute-start | bytes 1572872 | tf_op jit(solution)/shard_map/ppermute | solution.py:532
  43.1 1.3 %collective-permute-start.6 = (f32[128,128]{1,0:T(8,128)S(1)}, f32[128,128]{1,0:T(8,128)S(1)}, u32[]{:S(2)}, u32[]{:S(2)}) collective-permute-start(f32[128,128]{1,0:T(8,128)S(1)} %add_add_fusion._.mine_ref), channel_id=1, source_target_pairs={{0,1},{1,0},{2,3},{3,2},{4,5},{5,4},{6,7},{7,6},{8,9},{9,8},{10,11... | collective-permute-start | bytes 196616 | tf_op jit(solution)/shard_map/ppermute | solution.py:556
  56.5 0.7 copy-start.4
  56.5 0.7 copy-start.6
  56.6 0.8 copy-start.8
  57.3 4.1 %copy-start = (f32[2048,128]{1,0:T(8,128)}, f32[2048,128]{1,0:T(8,128)S(1)}, u32[]{:S(2)}) copy-start(f32[2048,128]{1,0:T(8,128)S(1)} %merge.3.own_ref) | copy-start | bytes 3145732
  57.3 13.2 %collective-permute-start.14 = (f32[2048,128]{1,0:T(8,128)S(1)}, f32[2048,128]{1,0:T(8,128)S(1)}, u32[]{:S(2)}, u32[]{:S(2)}) collective-permute-start(f32[2048,128]{1,0:T(8,128)S(1)} %merge.3.own_ref), channel_id=1, source_target_pairs={{0,1},{1,0},{2,3},{3,2},{4,5},{5,4},{6,7},{7,6},{8,9},{9,8},{10,11... | collective-permute-start | bytes 3145736 | tf_op jit(solution)/shard_map/ppermute | solution.py:588
  57.5 14.0 %copy-start.5 = (f32[2,256,128]{2,1,0:T(8,128)S(1)}, f32[2,256,128]{2,1,0:T(8,128)}, u32[]{:S(2)}) copy-start(f32[2,256,128]{2,1,0:T(8,128)} %copy-done.4) | copy-start | bytes 786436
  61.4 44.5 %collective-permute-start.9 = (f32[32,2048]{1,0:T(8,128)}, f32[32,2048]{1,0:T(8,128)}, u32[]{:S(2)}, u32[]{:S(2)}) collective-permute-start(f32[32,2048]{1,0:T(8,128)} %get-tuple-element.84), channel_id=1, source_target_pairs={{0,8},{8,16},{1,9},{9,17},{2,10},{10,18},{3,11},{11,19},{4,12},{12... | collective-permute-start | bytes 786440 | tf_op jit(solution)/shard_map/ppermute | solution.py:594
  66.6 39.3 %collective-permute-start.10 = (f32[32,2048]{1,0:T(8,128)}, f32[32,2048]{1,0:T(8,128)}, u32[]{:S(2)}, u32[]{:S(2)}) collective-permute-start(f32[32,2048]{1,0:T(8,128)} %get-tuple-element.85), channel_id=1, source_target_pairs={{0,16},{8,24},{1,17},{9,25},{2,18},{10,26},{3,19},{11,27},{4,20},{... | collective-permute-start | bytes 786440 | tf_op jit(solution)/shard_map/ppermute | solution.py:594
  68.6 37.3 %collective-permute-start.11 = (f32[32,2048]{1,0:T(8,128)}, f32[32,2048]{1,0:T(8,128)}, u32[]{:S(2)}, u32[]{:S(2)}) collective-permute-start(f32[32,2048]{1,0:T(8,128)} %get-tuple-element.86), channel_id=1, source_target_pairs={{0,24},{8,0},{1,25},{9,1},{2,26},{10,2},{3,27},{11,3},{4,28},{12,4... | collective-permute-start | bytes 786440 | tf_op jit(solution)/shard_map/ppermute | solution.py:594
  70.5 1.0 copy-start.2
  71.5 1.2 %copy-start.1 = (f32[2048,128]{1,0:T(8,128)S(1)}, f32[2048,128]{1,0:T(8,128)}, u32[]{:S(2)}) copy-start(f32[2048,128]{1,0:T(8,128)} %copy-done) | copy-start | bytes 3145732
  72.7 1.2 %copy-start.3 = (f32[2048,128]{1,0:T(8,128)S(1)}, f32[2048,128]{1,0:T(8,128)}, u32[]{:S(2)}) copy-start(f32[2048,128]{1,0:T(8,128)} %copy-done.2) | copy-start | bytes 3145732
  76.6 0.9 copy-start.9
  79.7 26.2 %copy-start.7 = (bf16[128,384]{1,0:T(8,128)(2,1)S(1)}, bf16[128,384]{1,0:T(8,128)(2,1)}, u32[]{:S(2)}) copy-start(bf16[128,384]{1,0:T(8,128)(2,1)} %copy-done.6) | copy-start | bytes 294916
  79.7 26.2 %copy-start.10 = (f32[128,2048]{1,0:T(8,128)S(1)}, f32[128,2048]{1,0:T(8,128)}, u32[]{:S(2)}) copy-start(f32[128,2048]{1,0:T(8,128)} %get-tuple-element.93.refs_7_) | copy-start | bytes 3145732
Sparse Core Ops, SparseCore 0:
  24.2 35.7 all-gather.1
